TPU v7x, 512 devices: a whole 4x8x8 slice. The times are simulated.
512 devices in a mesh: gx: 32 (over y, x), gy: 16 (over z, core).
Axes of the slice: x: 4, y: 8, z: 8, core: 2. Of those that a mesh axis runs over, the one named last changes fastest.
Arguments:
- pressure: float32 [5, 1024, 2048], P(None, 'gx', 'gy'), may hold values from -4 to -0.05
- newton_rhs: float32 [5, 1024, 2048], P(None, 'gx', 'gy'), may hold values from -6 to 6
- geology: int32 [5, 1024, 2048], P(None, 'gx', 'gy'), may hold values from 0 to 15
- saturated_conductivity: float32 [16], replicated, may hold values from 0.1 to 10
- genuchten_alpha: float32 [16], replicated, may hold values from 0.5 to 4
- genuchten_exponent: float32 [16], replicated, may hold values from 1.5 to 3
- land_mask: int32 [1024, 2048], P('gx', 'gy'), may hold values from 0 to 1, as said below
- ponding: float32 [1024, 2048], P('gx', 'gy'), may hold values from 0.01 to 0.3
- slope_class: int32 [1024, 2048], P('gx', 'gy'), may hold values from 0 to 7
- slope_table: float32 [8], replicated, may hold values from 0.001 to 0.05
- flow_direction: int32 [1024, 2048], P('gx', 'gy'), may hold values from 0 to 1
- soil_class: int32 [1024, 2048], P('gx', 'gy'), may hold values from 0 to 11
- soil_inverse: float32 [12, 20, 20], replicated, may hold values from -2 to 2
- soil_state: float32 [20, 1024, 2048], P(None, 'gx', 'gy'), may hold values from -6 to 6
Outputs:
- correction: float32 [5, 1024, 2048], P(None, 'gx', 'gy')
- ponding_next: float32 [1024, 2048], P('gx', 'gy')
- soil_next: float32 [20, 1024, 2048], P(None, 'gx', 'gy')
Inputs may be any that keep to these rules, and one draw needn't show every extreme that they name: `land_mask`: land shares differ strongly between aligned 8 x 8 blocks of columns, from all sea to all land.
All inputs are finite; a program needn't handle non-finite values.
Results may differ from a plain program's by a relative error of at most 0.0001.
Values sent between devices are 32-bit elements; how exact they have to be, the bound alone decides.
No kernel may reach another device: no remote copies, remote signals or barrier semaphores. Data moves between devices by JAX's collectives and lax.ppermute only.
A program may use at most 64 MiB of HBM per device.

v0:
```python
import jax
import jax.numpy as jnp
from jax import lax
from jax.sharding import PartitionSpec as P

ITERS = 3


def extended(cells, sides, width):
    for axis, dim in sides:
        count = lax.axis_size(axis)
        ends = count - 1
        head = lax.slice_in_dim(cells, 0, width, axis=dim)
        tail = lax.slice_in_dim(cells, cells.shape[dim] - width, cells.shape[dim], axis=dim)
        cells = jnp.concatenate(
            [
                lax.ppermute(tail, axis, [(i, (i + 1) % count) for i in range(ends)]),
                cells,
                lax.ppermute(head, axis, [((i + 1) % count, i) for i in range(ends)]),
            ],
            axis=dim,
        )
    return cells


def passed_along(shard, axis, by):
    length = lax.axis_size(axis)
    pairs = [(i, i + by) for i in range(length) if 0 <= i + by < length]
    return lax.ppermute(shard, axis, pairs)


def lookup(table, index):
    total = jnp.zeros(index.shape, jnp.float32)
    for entry in range(table.shape[0]):
        total = jnp.where(index == entry, table[entry], total)
    return total


def harmonic(first, second):
    return 2.0 * first * second / (first + second)


def vertical_pad(field):
    return jnp.pad(field, ((1, 1), (0, 0), (0, 0)))


def hydraulics(pressure, geology, saturated_conductivity, genuchten_alpha, genuchten_exponent):
    alpha_cell = lookup(genuchten_alpha, geology)
    exponent = lookup(genuchten_exponent, geology)
    base_cond = lookup(saturated_conductivity, geology)
    shape_m = 1.0 - 1.0 / exponent
    scaled = alpha_cell * jnp.abs(pressure)
    powered = jnp.power(scaled, exponent)
    conductivity = base_cond * jnp.power(1.0 + powered, -shape_m)
    capacity = 0.05 + 0.4 * shape_m * exponent * alpha_cell * jnp.power(
        scaled, exponent - 1.0
    ) * jnp.power(1.0 + powered, -shape_m - 1.0)
    return (conductivity, capacity)


def face_terms(padded_cond):
    center = padded_cond[1:-1, 1:-1, 1:-1]
    return (
        harmonic(center, padded_cond[1:-1, :-2, 1:-1]),
        harmonic(center, padded_cond[1:-1, 2:, 1:-1]),
        harmonic(center, padded_cond[1:-1, 1:-1, :-2]),
        harmonic(center, padded_cond[1:-1, 1:-1, 2:]),
        harmonic(center, padded_cond[:-2, 1:-1, 1:-1]),
        harmonic(center, padded_cond[2:, 1:-1, 1:-1]),
    )


def apply_operator(field, faces, diagonal):
    padded = vertical_pad(extended(field, (("gx", 1), ("gy", 2)), 1))
    beside = faces[0] * padded[1:-1, :-2, 1:-1] + faces[1] * padded[1:-1, 2:, 1:-1]
    beside = beside + faces[2] * padded[1:-1, 1:-1, :-2] + faces[3] * padded[1:-1, 1:-1, 2:]
    beside = beside + faces[4] * padded[:-2, 1:-1, 1:-1] + faces[5] * padded[2:, 1:-1, 1:-1]
    return diagonal * field - beside


def squared_total(residual):
    return lax.psum(jnp.sum(residual * residual), ("gx", "gy"))


def overland(ponding, slope_class, slope_table, flow_direction, land):
    outflow = jnp.sqrt(lookup(slope_table, slope_class)) / 0.03 * jnp.power(ponding, 5.0 / 3.0)
    eastward = jnp.where(flow_direction == 0, outflow, 0.0)
    southward = outflow - eastward
    from_west = passed_along(eastward[-1:, :], "gx", 1)
    from_north = passed_along(southward[:, -1:], "gy", 1)
    inflow = jnp.concatenate([from_west, eastward[:-1, :]], axis=0) + jnp.concatenate(
        [from_north, southward[:, :-1]], axis=1
    )
    return land * (ponding + 0.2 * (inflow - outflow))


def soil_solve(soil_state, ponding_next, top_correction, soil_class, soil_inverse, land_mask):
    forcing = soil_state.at[0].add(0.5 * ponding_next)
    forcing = forcing.at[1].add(0.5 * top_correction)
    solved = jnp.zeros_like(soil_state)
    for entry in range(soil_inverse.shape[0]):
        product = jnp.einsum(
            "ij,jxy->ixy", soil_inverse[entry], forcing, precision=lax.Precision.HIGHEST
        )
        solved = jnp.where((soil_class == entry)[None], product, solved)
    return jnp.where((land_mask == 1)[None], solved, soil_state)


def on_device(
    pressure,
    newton_rhs,
    geology,
    saturated_conductivity,
    genuchten_alpha,
    genuchten_exponent,
    land_mask,
    ponding,
    slope_class,
    slope_table,
    flow_direction,
    soil_class,
    soil_inverse,
    soil_state,
):
    land = land_mask.astype(jnp.float32)
    conductivity, capacity = hydraulics(
        pressure, geology, saturated_conductivity, genuchten_alpha, genuchten_exponent
    )
    padded_cond = vertical_pad(extended(conductivity, (("gx", 1), ("gy", 2)), 1))
    faces = face_terms(padded_cond)
    diagonal = (
        capacity
        + 4.0 * (1.0 - land)[None]
        + faces[0]
        + faces[1]
        + faces[2]
        + faces[3]
        + faces[4]
        + faces[5]
    )
    correction = jnp.zeros_like(newton_rhs)
    residual = newton_rhs
    direction = newton_rhs
    norm_now = squared_total(residual)
    for step in range(ITERS):
        image = apply_operator(direction, faces, diagonal)
        alpha = norm_now / lax.psum(jnp.sum(direction * image), ("gx", "gy"))
        correction = correction + alpha * direction
        residual = residual - alpha * image
        norm_next = squared_total(residual)
        direction = residual + norm_next / norm_now * direction
        norm_now = norm_next
    ponding_next = overland(ponding, slope_class, slope_table, flow_direction, land)
    soil_next = soil_solve(
        soil_state, ponding_next, correction[0], soil_class, soil_inverse, land_mask
    )
    return (correction, ponding_next, soil_next)


def solution(mesh):
    in_specs = (
        P(None, "gx", "gy"),
        P(None, "gx", "gy"),
        P(None, "gx", "gy"),
        P(),
        P(),
        P(),
        P("gx", "gy"),
        P("gx", "gy"),
        P("gx", "gy"),
        P(),
        P("gx", "gy"),
        P("gx", "gy"),
        P(),
        P(None, "gx", "gy"),
    )
    out_specs = (P(None, "gx", "gy"), P("gx", "gy"), P(None, "gx", "gy"))
    return jax.shard_map(
        on_device, mesh=mesh, in_specs=in_specs, out_specs=out_specs, check_vma=False
    )
```

profile of v0, /device:TPU:1, one launch (start us, length us, event | category | flops | bytes accessed | tf_op | source)
XLA Modules:
  0.0 658.8 jit_solution(2684235651974638283)
XLA Ops:
  0.6 0.8 fusion.117
  1.4 4.1 collective-permute-start.4
  5.5 1.3 collective-permute-start.5
  6.8 0.7 fusion.121
  7.5 0.7 fusion.119
  8.3 0.7 fusion.120
  9.0 0.9 copy-done.10
  9.9 30.7 %power_multiply_fusion = (f32[5,32,128]{2,1,0:T(8,128)S(1)}, pred[5,32,128]{2,1,0:T(8,128)(4,1)S(1)}, pred[5,32,128]{2,1,0:T(8,128)(4,1)S(1)}, pred[5,32,128]{2,...) fusion(f32[]{:T(128)} %bitcast.47, f32[]{:T(128)} %bitcast.46, ...), kind=kLoop, calls=%fused_computation.150 | loop fusion | flops 1454080 | bytes 573632 | tf_op jit(solution)/shard_map/mul | solution.py:54
  40.6 4.0 collective-permute-start
  44.6 1.3 collective-permute-start.1
  46.0 0.1 fusion.113
  46.1 5.4 collective-permute-start.6
  51.5 2.6 collective-permute-start.7
  54.1 0.1 fusion.112
  54.2 3.0 collective-permute-start.2
  57.2 1.9 collective-permute-start.3
  59.1 0.2 select_maximum_fusion.8
  59.3 3.8 collective-permute-done.3
  63.2 0.2 select_maximum_fusion.12
  63.3 21.4 %multiply_reduce_fusion.3 = (f32[]{:T(128)}, f32[]{:T(128)}, f32[5,32,128]{2,1,0:T(8,128)S(1)}, f32[5,32,128]{2,1,0:T(8,128)S(1)}, f32[5,32,128]{2,1,0:T(8,128)S(1)}, /*index=5*/f32[5,32,128]{2,1,0:T(8,128)S(1)}) fusion(f32[5,32,128]{2,1,0:T(8,128)S(1)} %copy-done.2, f32[7,34,130]{2,1,0:T(8,128)S(1)} %select_maximum_fusion.8, ...), kind=kLoop, calls=%fused_computation.144 | loop fusion | flops 2150398 | bytes 1258280 | tf_op jit(solution)/shard_map/reduce_sum | solution.py:147
  84.7 109.3 %all-reduce.4 = (f32[]{:T(128)}, f32[]{:T(128)}) all-reduce(f32[]{:T(128)} %get-tuple-element.31, f32[]{:T(128)} %get-tuple-element.30), channel_id=1, replica_groups=mesh['gx'=32,'gy'=16] {'gx','gy'}, use_global_device_ids=true, to_apply=%region_1.2 | all-reduce | flops 2 | bytes 16 | tf_op jit(solution)/shard_map/psum | solution.py:82
  195.3 0.6 multiply_reduce_fusion.2
  196.0 95.9 %psum.44 = f32[]{:T(128)} all-reduce(f32[]{:T(128)} %get-tuple-element.38), channel_id=1, replica_groups=mesh['gx'=32,'gy'=16] {'gx','gy'}, use_global_device_ids=true, to_apply=%region_5.6 | all-reduce | flops 1 | bytes 8 | tf_op jit(solution)/shard_map/psum | solution.py:82
  293.3 2.8 collective-permute-start.8
  296.1 1.3 collective-permute-start.9
  297.4 0.7 fusion.118
  298.1 2.3 collective-permute-done.9
  300.4 0.1 fusion.111
  300.6 6.2 collective-permute-start.10
  306.8 1.9 collective-permute-start.11
  308.7 5.1 compare_select_fusion
  313.9 1.6 collective-permute-start.16
  315.6 0.2 select_maximum_fusion.4
  315.8 0.9 multiply_reduce_fusion.1
  316.7 100.0 %psum.45 = f32[]{:T(128)} all-reduce(f32[]{:T(128)} %get-tuple-element.36), channel_id=1, replica_groups=mesh['gx'=32,'gy'=16] {'gx','gy'}, use_global_device_ids=true, to_apply=%region_7.8 | all-reduce | flops 1 | bytes 8 | tf_op jit(solution)/shard_map/psum | solution.py:147
  418.0 0.6 multiply_reduce_fusion
  418.6 4.3 collective-permute-start.17
  423.0 94.7 %psum.46 = f32[]{:T(128)} all-reduce(f32[]{:T(128)} %multiply_reduce_fusion), channel_id=1, replica_groups=mesh['gx'=32,'gy'=16] {'gx','gy'}, use_global_device_ids=true, to_apply=%region_9.10 | all-reduce | flops 1 | bytes 8 | tf_op jit(solution)/shard_map/psum | solution.py:82
  519.1 3.1 collective-permute-start.12
  522.2 1.3 collective-permute-start.13
  523.5 3.0 collective-permute-done.13
  526.5 0.1 fusion.110
  526.6 5.4 collective-permute-start.14
  532.0 1.9 collective-permute-start.15
  534.0 4.0 collective-permute-done.15
  538.0 0.2 select_maximum_fusion
  538.2 0.9 fusion.40
  539.1 5.8 fusion.81
  544.9 101.8 %psum.47 = f32[]{:T(128)} all-reduce(f32[]{:T(128)} %fusion.40), channel_id=1, replica_groups=mesh['gx'=32,'gy'=16] {'gx','gy'}, use_global_device_ids=true, to_apply=%region_11.12 | all-reduce | flops 1 | bytes 8 | tf_op jit(solution)/shard_map/psum | solution.py:147
  648.2 0.8 copy-done.5
  649.0 0.7 fusion.32
  649.7 0.7 fusion.30
  650.4 0.7 fusion.28
  651.0 0.7 fusion.26
  651.7 0.7 fusion.24
  652.4 0.7 fusion.22
  653.0 0.7 fusion.20
  653.7 0.7 fusion.18
  654.4 0.7 fusion.16
  655.1 0.7 fusion.14
  655.8 0.7 fusion.34
  656.4 0.3 copy-done
  656.7 1.3 fusion.12
  658.0 0.8 copy.30
  (59 shorter events, 0.5 us)
Async XLA Ops:
  1.4 5.4 copy-start.6
  1.4 44.5 %collective-permute-start.4 = (f32[5,1,128]{2,1,0:T(1,128)S(1)}, f32[5,1,128]{2,1,0:T(1,128)S(1)}, u32[]{:S(2)}, u32[]{:S(2)}) collective-permute-start(f32[5,1,128]{2,1,0:T(1,128)S(1)} %get-tuple-element.75), channel_id=1, source_target_pairs={{0,16},{16,32},{32,48},{48,64},{64,80},{80,96},{96,112},{112,128},... | collective-permute-start | bytes 7688 | tf_op jit(solution)/shard_map/ppermute | solution.py:17
  5.5 40.5 %collective-permute-start.5 = (f32[5,1,128]{2,1,0:T(1,128)S(1)}, f32[5,1,128]{2,1,0:T(1,128)S(1)}, u32[]{:S(2)}, u32[]{:S(2)}) collective-permute-start(f32[5,1,128]{2,1,0:T(1,128)S(1)} %get-tuple-element.76), channel_id=1, source_target_pairs={{16,0},{32,16},{48,32},{64,48},{80,64},{96,80},{112,96},{128,112},... | collective-permute-start | bytes 7688 | tf_op jit(solution)/shard_map/ppermute | solution.py:19
  6.8 0.7 copy-start.7
  7.5 0.7 copy-start.8
  9.0 0.9 copy-start.10
  9.0 0.9 copy-start.3
  9.9 36.0 %copy-start.4 = (s32[32,128]{1,0:T(8,128)S(1)}, s32[32,128]{1,0:T(8,128)}, u32[]{:S(2)}) copy-start(s32[32,128]{1,0:T(8,128)} %param.24) | copy-start | bytes 49156
  9.9 36.0 %copy-start.2 = (f32[5,32,128]{2,1,0:T(8,128)S(1)}, f32[5,32,128]{2,1,0:T(8,128)}, u32[]{:S(2)}) copy-start(f32[5,32,128]{2,1,0:T(8,128)} %param.19) | copy-start | bytes 245764
  40.6 13.5 %collective-permute-start = (f32[5,1,128]{2,1,0:T(1,128)S(1)}, f32[5,1,128]{2,1,0:T(1,128)S(1)}, u32[]{:S(2)}, u32[]{:S(2)}) collective-permute-start(f32[5,1,128]{2,1,0:T(1,128)S(1)} %get-tuple-element.73), channel_id=1, source_target_pairs={{0,16},{16,32},{32,48},{48,64},{64,80},{80,96},{96,112},{112,128},... | collective-permute-start | bytes 7688 | tf_op jit(solution)/shard_map/ppermute | solution.py:17
  44.6 9.5 %collective-permute-start.1 = (f32[5,1,128]{2,1,0:T(1,128)S(1)}, f32[5,1,128]{2,1,0:T(1,128)S(1)}, u32[]{:S(2)}, u32[]{:S(2)}) collective-permute-start(f32[5,1,128]{2,1,0:T(1,128)S(1)} %get-tuple-element.74), channel_id=1, source_target_pairs={{16,0},{32,16},{48,32},{64,48},{80,64},{96,80},{112,96},{128,112},... | collective-permute-start | bytes 7688 | tf_op jit(solution)/shard_map/ppermute | solution.py:19
  46.1 13.1 %collective-permute-start.6 = (f32[5,34,1]{2,1,0:T(8,128)S(1)}, f32[5,34,1]{2,1,0:T(8,128)S(1)}, u32[]{:S(2)}, u32[]{:S(2)}) collective-permute-start(f32[5,34,1]{2,1,0:T(8,128)S(1)} %get-tuple-element.67), channel_id=1, source_target_pairs={{0,1},{1,2},{2,3},{3,4},{4,5},{5,6},{6,7},{7,8},{8,9},{9,10},{10,1... | collective-permute-start | bytes 2048 | tf_op jit(solution)/shard_map/ppermute | solution.py:17
  51.5 7.7 %collective-permute-start.7 = (f32[5,34,1]{2,1,0:T(8,128)S(1)}, f32[5,34,1]{2,1,0:T(8,128)S(1)}, u32[]{:S(2)}, u32[]{:S(2)}) collective-permute-start(f32[5,34,1]{2,1,0:T(8,128)S(1)} %get-tuple-element.68), channel_id=1, source_target_pairs={{1,0},{2,1},{3,2},{4,3},{5,4},{6,5},{7,6},{8,7},{9,8},{10,9},{11,1... | collective-permute-start | bytes 2048 | tf_op jit(solution)/shard_map/ppermute | solution.py:19
  54.2 5.1 collective-permute-start.2
  57.2 6.0 collective-permute-start.3
  293.2 4.1 copy-start.13
  293.3 4.8 collective-permute-start.8
  296.1 4.3 collective-permute-start.9
  300.4 8.3 %copy-start.14 = (s32[32,128]{1,0:T(8,128)S(1)}, s32[32,128]{1,0:T(8,128)}, u32[]{:S(2)}) copy-start(s32[32,128]{1,0:T(8,128)} %param.28) | copy-start | bytes 49156
  300.5 8.2 %copy-start.11 = (f32[32,128]{1,0:T(8,128)S(1)}, f32[32,128]{1,0:T(8,128)}, u32[]{:S(2)}) copy-start(f32[32,128]{1,0:T(8,128)} %param.25) | copy-start | bytes 49156
  300.5 8.2 %copy-start.12 = (s32[32,128]{1,0:T(8,128)S(1)}, s32[32,128]{1,0:T(8,128)}, u32[]{:S(2)}) copy-start(s32[32,128]{1,0:T(8,128)} %param.26) | copy-start | bytes 49156
  300.6 15.1 %collective-permute-start.10 = (f32[5,34,1]{2,1,0:T(8,128)S(1)}, f32[5,34,1]{2,1,0:T(8,128)S(1)}, u32[]{:S(2)}, u32[]{:S(2)}) collective-permute-start(f32[5,34,1]{2,1,0:T(8,128)S(1)} %get-tuple-element.63), channel_id=1, source_target_pairs={{0,1},{1,2},{2,3},{3,4},{4,5},{5,6},{6,7},{7,8},{8,9},{9,10},{10,1... | collective-permute-start | bytes 2048 | tf_op jit(solution)/shard_map/ppermute | solution.py:17
  306.8 8.8 %collective-permute-start.11 = (f32[5,34,1]{2,1,0:T(8,128)S(1)}, f32[5,34,1]{2,1,0:T(8,128)S(1)}, u32[]{:S(2)}, u32[]{:S(2)}) collective-permute-start(f32[5,34,1]{2,1,0:T(8,128)S(1)} %get-tuple-element.64), channel_id=1, source_target_pairs={{1,0},{2,1},{3,2},{4,3},{5,4},{6,5},{7,6},{8,7},{9,8},{10,9},{11,1... | collective-permute-start | bytes 2048 | tf_op jit(solution)/shard_map/ppermute | solution.py:19
  313.9 225.1 %collective-permute-start.16 = (f32[1,128]{1,0:T(1,128)S(1)}, f32[1,128]{1,0:T(1,128)S(1)}, u32[]{:S(2)}, u32[]{:S(2)}) collective-permute-start(f32[1,128]{1,0:T(1,128)S(1)} %slice.563), channel_id=1, source_target_pairs={{0,16},{16,32},{32,48},{48,64},{64,80},{80,96},{96,112},{112,128},... | collective-permute-start | bytes 1544 | tf_op jit(solution)/shard_map/ppermute | solution.py:29
  418.6 120.4 %collective-permute-start.17 = (f32[32,1]{1,0:T(8,128)S(1)}, f32[32,1]{1,0:T(8,128)S(1)}, u32[]{:S(2)}, u32[]{:S(2)}) collective-permute-start(f32[32,1]{1,0:T(8,128)S(1)} %slice.565), channel_id=1, source_target_pairs={{0,1},{1,2},{2,3},{3,4},{4,5},{5,6},{6,7},{7,8},{8,9},{9,10},{10,1... | collective-permute-start | bytes 392 | tf_op jit(solution)/shard_map/ppermute | solution.py:29
  519.0 4.5 copy-start.15
  519.1 4.5 collective-permute-start.12
  522.2 4.3 collective-permute-start.13
  526.6 7.3 %collective-permute-start.14 = (f32[5,34,1]{2,1,0:T(8,128)S(1)}, f32[5,34,1]{2,1,0:T(8,128)S(1)}, u32[]{:S(2)}, u32[]{:S(2)}) collective-permute-start(f32[5,34,1]{2,1,0:T(8,128)S(1)} %get-tuple-element.61), channel_id=1, source_target_pairs={{0,1},{1,2},{2,3},{3,4},{4,5},{5,6},{6,7},{7,8},{8,9},{9,10},{10,1... | collective-permute-start | bytes 2048 | tf_op jit(solution)/shard_map/ppermute | solution.py:17
  532.0 6.0 collective-permute-start.15
  538.2 1.0 copy-start.1
  648.1 0.9 copy-start.5
  648.1 1.5 copy-start.9
  655.7 1.0 copy-start
where the time goes:
time: 661 us; the launch traced here: 659 us
  blocking collectives  502 us (76%)
  other arithmetic  66.9 us (10%)
  starting transfers between devices  53.4 us (8%)
  waiting for transfers between devices  13.2 us (2%)
  matrix products  8.62 us (1%)
  between operations  8 us (1%)
  local copies, waits for them, and re-layouts  7.02 us (1%)
    psum x3, blocking collectives, squared_total(): return lax.psum(jnp.sum(residual * residual), ('gx', 'gy'))  300 us
    psum x2, blocking collectives, on_device(): alpha = norm_now / lax.psum(jnp.sum(direction * image), ('gx', 'gy'))  202 us
    ppermute x8, starting transfers between devices, extended(): lax.ppermute(tail, axis, [(i, (i + 1) % count) for i in range(ends)])  33.9 us
    mul x1, other arithmetic, hydraulics(): conductivity = base_cond * jnp.power(1.0 + powered, -shape_m)  30.7 us
    reduce_sum x3, other arithmetic, on_device(): alpha = norm_now / lax.psum(jnp.sum(direction * image), ('gx', 'gy'))  23.1 us
    ppermute x8, starting transfers between devices, extended(): lax.ppermute(head, axis, [((i + 1) % count, i) for i in range(ends)])  13.5 us
  transfers between devices with their start and end apart: 18, of which 4 were waited for; matrix products, arithmetic and copies ran while one was open for 6% of the time, Pallas kernels for 0%

commit v1 on v0

v1 whole, which is shorter than its diff:
```python
import jax
import jax.numpy as jnp
from jax import lax
from jax.experimental import pallas as pl
from jax.experimental.pallas import tpu as pltpu
from jax.sharding import PartitionSpec as P


LAYERS = 5
STATE = 20
W = 3
X, Y = 32, 128
E = X + 8
FIELDS = 3 * LAYERS
G = 2 * W
SLAB = 48
F32 = jnp.float32


def two_sum(a, b):
    s = a + b
    t = s - a
    return s, (a - (s - t)) + (b - t)


def renorm(a, b):
    s = a + b
    return s, b - (s - a)


def halves(a):
    t = a * 4097.0
    hi = t - (t - a)
    return hi, a - hi


def two_prod(a, b):
    p = a * b
    (ah, al), (bh, bl) = halves(a), halves(b)
    return p, ((ah * bh - p) + ah * bl + al * bh) + al * bl


def pair_add(a, b):
    s, e = two_sum(a[0], b[0])
    return renorm(s, e + (a[1] + b[1]))


def pair_sub(a, b):
    return pair_add(a, (-b[0], -b[1]))


def pair_mul(a, b):
    p, e = two_prod(a[0], b[0])
    return renorm(p, e + (a[0] * b[1] + a[1] * b[0]))


def pair_div(a, b):
    q = a[0] / b[0]
    r = pair_sub(a, pair_mul((q, jnp.zeros_like(q)), b))
    q2 = r[0] / b[0]
    r = pair_sub(r, pair_mul((q2, jnp.zeros_like(q)), b))
    return pair_add(renorm(q, q2), (r[0] / b[0], jnp.zeros_like(q)))


def iota(shape, dim):
    return lax.broadcasted_iota(jnp.int32, shape, dim)


def pick(table, index):
    row = jnp.broadcast_to(table, index.shape)
    return jnp.take_along_axis(row, index, axis=1, mode="promise_in_bounds")


def call(kernel, outs, scratch=(), flops=0, nbytes=0, vmem=32):
    return pl.pallas_call(
        kernel,
        out_shape=[jax.ShapeDtypeStruct(s, F32) for s in outs],
        scratch_shapes=scratch,
        compiler_params=pltpu.CompilerParams(vmem_limit_bytes=vmem * 2**20),
        cost_estimate=pl.CostEstimate(
            flops=flops, bytes_accessed=nbytes, transcendentals=0
        ),
    )


def local_kernel(
    pressure, rhs, geology, ks, alpha, expo, land, ponding, slope_class, slope,
    flow, cond, diag, up, down, east, south, tab,
):
    for row, ref in enumerate((ks, alpha, expo)):
        tab[row : row + 1, 0:16] = ref[...]
    tab[3:4, 0:8] = slope[...]
    t_ks = tab[0:1, :]
    t_la = jnp.log(tab[1:2, :])
    t_n = tab[2:3, :]
    t_m = 1.0 - 1.0 / t_n
    t_slope = jnp.sqrt(tab[3:4, :]) / 0.03
    sea = 4.0 * (1.0 - land[...].astype(F32))
    for l in range(LAYERS):
        g = geology[l]
        p = jnp.abs(pressure[l])
        n = pick(t_n, g)
        m = pick(t_m, g)
        t = jnp.exp(n * (pick(t_la, g) + jnp.log(p)))
        one_t = 1.0 + t
        e = jnp.exp(-m * jnp.log(one_t))
        k = pick(t_ks, g) * e
        d = 0.05 + 0.4 * m * n * t * e / (p * one_t) + sea
        cond[l] = k
        diag[l] = d
        for f, x in enumerate((rhs[l], k, d)):
            q = (f * LAYERS + l) * W
            up[q : q + W, :] = x[0:W]
            down[q : q + W, :] = x[X - W : X]
    out = pick(t_slope, slope_class[...]) * jnp.exp((5.0 / 3.0) * jnp.log(ponding[...]))
    eastward = jnp.where(flow[...] == 0, out, 0.0)
    east[...] = eastward
    south[...] = out - eastward
    up[45:48, :] = jnp.zeros((3, Y), F32)
    down[45:46, :] = eastward[X - 1 : X]
    down[46:48, :] = jnp.zeros((2, Y), F32)


def pack_kernel(rhs, cond, diag, before, after, south, ext, packed):
    lane = iota((E, Y), 1)
    q_all = jnp.zeros((E, Y), F32)
    for f, ref in enumerate((rhs, cond, diag)):
        for l in range(LAYERS):
            q = f * LAYERS + l
            ext[q, 0:X, :] = ref[l]
            ext[q, X : X + W, :] = after[q * W : q * W + W, :]
            ext[q, X + W : E - W, :] = jnp.zeros((E - X - 2 * W, Y), F32)
            ext[q, E - W : E, :] = before[q * W : q * W + W, :]
            x = pltpu.roll(ext[q], (W + G * q) % Y, 1)
            q_all = jnp.where((lane >= G * q) & (lane < G * q + G), x, q_all)
    q = FIELDS
    packed[...] = q_all
    x = pltpu.roll(south[...], (W + G * q) % Y, 1)
    ln = iota((X, Y), 1)
    packed[0:X, :] = jnp.where((ln >= G * q) & (ln < G * q + G), x, q_all[0:X])


def krylov_kernel(
    ext, right, left, before, east, south, ponding, land,
    v1_out, v2_out, row_out, pond_out, fr, fc, fv, dd, v,
):
    lane = iota((E, Y), 1)
    first, last = lane == 0, lane == Y - 1

    def turn(m, h, by, edge):
        m, h = pltpu.roll(m, by, 1), pltpu.roll(h, by, 1)
        return jnp.where(edge, h, m), jnp.where(edge, m, h)

    w = jnp.where(lane % G >= W, right[...], left[...])

    def halo(q):
        return pltpu.roll(w, (-(W + G * q)) % Y, 1)

    def harmonic(a, b):
        return 2.0 * a * b / jnp.maximum(a + b, 1e-30)

    above = None
    for l in range(LAYERS):
        v[0, l], v[1, l] = ext[l], halo(l)
        k = ext[LAYERS + l], halo(LAYERS + l)
        dd[0, l], dd[1, l] = ext[2 * LAYERS + l], halo(2 * LAYERS + l)
        west = turn(*k, 1, first)
        for s in range(2):
            fr[s, l] = harmonic(k[s], pltpu.roll(k[s], 1, 0))
            fc[s, l] = harmonic(k[s], west[s])
            if l:
                fv[s, l - 1] = harmonic(k[s], above[s])
        above = k

    def product(l, flux_above):
        vm, vh = v[0, l], v[1, l]
        west = turn(vm, vh, 1, first)
        side = fc[0, l] * (vm - west[0]), fc[1, l] * (vh - west[1])
        gone = turn(*side, Y - 1, last)
        outs, flux = [], []
        for s, x in enumerate((vm, vh)):
            rows = fr[s, l] * (x - pltpu.roll(x, 1, 0))
            r = dd[s, l] * x + (rows - pltpu.roll(rows, E - 1, 0)) + (side[s] - gone[s])
            if l:
                r = r - flux_above[s]
            if l < LAYERS - 1:
                fl = fv[s, l] * (x - v[s, l + 1])
                r = r + fl
                flux.append(fl)
            outs.append(r)
        return outs, flux

    zero = jnp.zeros((8, Y), F32)
    sums = [(zero, zero)] * 6

    def add_to(j, a, b):
        for i in range(0, X, 8):
            p, e = two_prod(a[i : i + 8], b[i : i + 8])
            s, e2 = two_sum(sums[j][0], p)
            sums[j] = s, sums[j][1] + (e + e2)

    for step in range(3):
        results, flux = [], None
        for l in range(LAYERS):
            outs, flux = product(l, flux)
            old, new = v[0, l][0:X], outs[0][0:X]
            add_to(2 * step, old, old)
            add_to(2 * step + 1, old, new)
            results.append(outs)
        if step < 2:
            for l in range(LAYERS):
                v[0, l], v[1, l] = results[l]
                (v1_out, v2_out)[step][l] = results[l][0][0:X]

    sub = iota((8, Y), 0)
    ln = iota((8, Y), 1)
    total = zero, zero
    for j in range(6):
        s = renorm(*sums[j])
        for by in (4, 2, 1):
            s = pair_add(s, tuple(pltpu.roll(t, by, 0) for t in s))
        total = tuple(jnp.where(sub == j, a, b) for a, b in zip(s, total))
    for by in (64, 32, 16, 8, 4, 2, 1):
        total = pair_add(total, tuple(pltpu.roll(t, by, 1) for t in total))
    row = jnp.where(ln == sub, total[0], jnp.where(ln == sub + 8, total[1], 0.0))
    row = jnp.sum(row, axis=0, keepdims=True)
    row_out[...] = jnp.broadcast_to(row, row_out.shape)

    es, so = east[...], south[...]
    north = pltpu.roll(w, (-(W + G * FIELDS)) % Y, 1)[0:X]
    x_row, x_lane = iota((X, Y), 0), iota((X, Y), 1)
    inflow = jnp.where(x_row == 0, before[45:46, :], pltpu.roll(es, 1, 0)) + jnp.where(
        x_lane == 0, pltpu.roll(north, 1, 1), pltpu.roll(so, 1, 1)
    )
    pond_out[...] = land[...].astype(F32) * (ponding[...] + 0.2 * (inflow - (es + so)))


def rows_total(ref):
    parts = [
        (ref[i : i + 8, :], pltpu.roll(ref[i : i + 8, :], Y - 8, 1))
        for i in range(0, ref.shape[0], 8)
    ]
    while len(parts) > 1:
        parts = [pair_add(a, b) for a, b in zip(parts[::2], parts[1::2])]
    s = parts[0]
    for by in (4, 2, 1):
        s = pair_add(s, tuple(pltpu.roll(t, by, 0) for t in s))
    return s


def relay_kernel(rows, row_out):
    hi, lo = rows_total(rows)
    ln = iota((8, Y), 1)
    both = jnp.where(ln < 8, hi, pltpu.roll(lo, 8, 1))
    for i in range(0, row_out.shape[0], 8):
        row_out[i : i + 8, :] = both


def soil_kernel(state, soil_class, land, table, out):
    index = soil_class[...]
    on_land = land[...] == 1

    def one(i, carry):
        total = None
        for j in range(STATE):
            term = pick(table[pl.ds(j * STATE + i, 1), :], index) * state[j]
            total = term if total is None else total + term
        out[i] = jnp.where(on_land, total, state[i])
        return carry

    lax.fori_loop(0, STATE, one, 0)


def final_kernel(
    rows, rhs, v1, v2, base, pond, soil_class, land, table, corr_out, soil_out
):
    hi, lo = rows_total(rows)
    mu = [
        tuple(jnp.broadcast_to(t[:, j : j + 1], (8, Y)) for t in (hi, lo))
        for j in range(6)
    ]
    l21 = pair_div(mu[2], mu[1])
    l31 = pair_div(mu[3], mu[1])
    d2 = pair_sub(mu[3], pair_mul(l21, mu[2]))
    u = pair_sub(mu[4], pair_mul(l31, mu[2]))
    l32 = pair_div(u, d2)
    d3 = pair_sub(pair_sub(mu[5], pair_mul(l31, mu[3])), pair_mul(l32, u))
    y2 = pair_sub(mu[1], pair_mul(l21, mu[0]))
    y3 = pair_sub(pair_sub(mu[2], pair_mul(l31, mu[0])), pair_mul(l32, y2))
    c3 = pair_div(y3, d3)
    c2 = pair_sub(pair_div(y2, d2), pair_mul(l32, c3))
    c1 = pair_sub(
        pair_sub(pair_div(mu[0], mu[1]), pair_mul(l21, c2)), pair_mul(l31, c3)
    )
    c1, c2, c3 = (jnp.concatenate([c[0]] * (X // 8), axis=0) for c in (c1, c2, c3))
    top = None
    for l in range(LAYERS):
        x = c1 * rhs[l] + c2 * v1[l] + c3 * v2[l]
        corr_out[l] = x
        top = x if top is None else top
    half = 0.5 * land[...].astype(F32)
    water = half * pond[...]
    head = half * top
    index = soil_class[...]
    for i in range(STATE):
        soil_out[i] = (
            base[i]
            + pick(table[i : i + 1, :], index) * water
            + pick(table[STATE + i : STATE + i + 1, :], index) * head
        )


def both_ways(to_next, to_previous, axis):
    count = lax.axis_size(axis)
    forth = [(i, i + 1) for i in range(count - 1)]
    back = [(i + 1, i) for i in range(count - 1)]
    return lax.ppermute(to_next, axis, forth), lax.ppermute(to_previous, axis, back)


def everyones(rows, axis):
    count = lax.axis_size(axis)
    return lax.all_to_all(rows.reshape(count, 1, Y), axis, 0, 0).reshape(count, Y)


def on_device(
    pressure, newton_rhs, geology, saturated_conductivity, genuchten_alpha,
    genuchten_exponent, land_mask, ponding, slope_class, slope_table,
    flow_direction, soil_class, soil_inverse, soil_state,
):
    block, plane = (LAYERS, X, Y), (X, Y)
    cond, diag, up, down, east, south = call(
        local_kernel,
        [block, block, (SLAB, Y), (SLAB, Y), plane, plane],
        [pltpu.VMEM((8, Y), F32)],
    )(
        pressure, newton_rhs, geology, saturated_conductivity[None],
        genuchten_alpha[None], genuchten_exponent[None], land_mask, ponding,
        slope_class, slope_table[None], flow_direction,
    )
    before, after = both_ways(down, up, "gx")
    ext, packed = call(pack_kernel, [(FIELDS, E, Y), (E, Y)])(
        newton_rhs, cond, diag, before, after, south
    )
    left, right = both_ways(packed, packed, "gy")
    table = jnp.pad(
        soil_inverse.transpose(2, 1, 0).reshape(STATE * STATE, -1),
        ((0, 0), (0, Y - soil_inverse.shape[0])),
    )
    (base,) = call(soil_kernel, [(STATE, X, Y)], flops=20_000_000, nbytes=2_000_000)(
        soil_state, soil_class, land_mask, table
    )
    v1, v2, rows, pond = call(
        krylov_kernel,
        [block, block, (lax.axis_size("gx"), Y), plane],
        [pltpu.VMEM((2, n, E, Y), F32) for n in (5, 5, 4, 5, 5)],
    )(ext, right, left, before, east, south, ponding, land_mask)
    rows = everyones(rows, "gx")
    (rows,) = call(relay_kernel, [(lax.axis_size("gy"), Y)])(rows)
    rows = everyones(rows, "gy")
    correction, soil_next = call(final_kernel, [block, (STATE, X, Y)])(
        rows, newton_rhs, v1, v2, base, pond, soil_class, land_mask, table[: 2 * STATE]
    )
    return correction, pond, soil_next


def solution(mesh):
    cells, plane, rest = P(None, "gx", "gy"), P("gx", "gy"), P()
    return jax.shard_map(
        on_device,
        mesh=mesh,
        in_specs=(
            cells, cells, cells, rest, rest, rest, plane, plane, plane, rest, plane,
            plane, rest, cells,
        ),
        out_specs=(cells, plane, cells),
        check_vma=False,
    )
```

time: 661 us -> 70.2 us (0.11)
  blocking collectives: 502 us -> 0 us
  other arithmetic: 66.9 us -> 0 us
  starting transfers between devices: 53.4 us -> 38 us
  Pallas kernels: 0 us -> 10.4 us
  matrix products: 8.62 us -> 0 us
  between operations: 8 us -> 0.8 us
    psum x5 -> x0, blocking collectives: 502 us -> none  [the longest x3 300 us: squared_total(): return lax.psum(jnp.sum(residual * residual), ('gx', 'gy'))]
    ppermute x18 -> x4, starting transfers between devices: 53.4 us -> 14.4 us  [the longest x2 8.57 us: both_ways(): lax.ppermute(to_previous, axis, back)]
    mul x2 -> x0, other arithmetic: 30.7 us -> none  [the longest x1 30.7 us: hydraulics(): conductivity = base_cond * jnp.power(1.0 + powered, -shape_m)]
    reduce_sum x5 -> x0, other arithmetic: 24.4 us -> none  [the longest x3 23.1 us: on_device(): alpha = norm_now / lax.psum(jnp.sum(direction * image), ('gx', 'gy'))]
    all_to_all x0 -> x2, starting transfers between devices: none -> 23.6 us  [everyones(): lax.all_to_all(rows.reshape(count, 1, Y), axis, 0, 0).reshape(count, Y)]
    pallas_call x0 -> x6, Pallas kernels: none -> 10.4 us  [the longest x1 5.77 us: on_device(): call(soil_kernel, [(STATE, X, Y)], flops=20000000, nbytes=2000000)]
    ppermute x18 -> x4, waiting for transfers between devices: 13.2 us -> 4.41 us  [the longest x2 3.26 us: both_ways(): lax.ppermute(to_previous, axis, back)]
    dot_general x12 -> x0, matrix products: 8.62 us -> none  [soil_solve(): jnp.einsum('ij,jxy->ixy', soil_inverse[entry], forcing, precision=lax.Pre...]
  transfers between devices with their start and end apart: 18 -> 6, of which waited for: 4 -> 4; matrix products, arithmetic and copies ran while one was open for 6% -> 1% of each run, Pallas kernels for 0% -> 8%
where the time goes in v1:
time: 70.2 us; the launch traced here: 69.5 us
  starting transfers between devices  38 us (54%)
  waiting for transfers between devices  12.9 us (18%)
  Pallas kernels  10.4 us (15%)
  local copies, waits for them, and re-layouts  7.33 us (10%)
  between operations  0.8 us (1%)
    all_to_all x2, starting transfers between devices, everyones(): lax.all_to_all(rows.reshape(count, 1, Y), axis, 0, 0).reshape(count, Y)  23.6 us
    ppermute x2, starting transfers between devices, both_ways(): lax.ppermute(to_previous, axis, back)  8.57 us
    all_to_all x2, waiting for transfers between devices, everyones(): lax.all_to_all(rows.reshape(count, 1, Y), axis, 0, 0).reshape(count, Y)  8.51 us
    unnamed x36, local copies, waits for them, and re-layouts  6.9 us
    ppermute x2, starting transfers between devices, both_ways(): lax.ppermute(to_next, axis, forth)  5.86 us
    pallas_call x1, Pallas kernels, on_device(): call(soil_kernel, [(STATE, X, Y)], flops=20000000, nbytes=2000000)  5.77 us
    ppermute x2, waiting for transfers between devices, both_ways(): lax.ppermute(to_previous, axis, back)  3.26 us
    pallas_call x1, Pallas kernels, on_device(): call(krylov_kernel, [block, block, (lax.axis_size('gx'), Y), plane], [plt...  2.05 us
  transfers between devices with their start and end apart: 6, of which 4 were waited for; matrix products, arithmetic and copies ran while one was open for 1% of the time, Pallas kernels for 8%

profile of v1, /device:TPU:1, one launch (start us, length us, event | category | flops | bytes accessed | tf_op | source)
XLA Modules:
  0.0 69.5 jit_solution(6458607714961027974)
XLA Ops:
  0.6 0.0 copy-start.16
  0.6 0.0 copy-start.13
  0.7 0.0 copy-start.14
  0.7 0.0 copy-start.15
  0.7 0.6 copy-done.16
  1.3 0.0 copy-done.13
  1.3 0.0 copy-done.14
  1.3 0.0 copy-done.15
  1.3 0.0 copy-start
  1.3 0.9 %copy-done = f32[5,32,128]{2,1,0:T(8,128)S(1)} copy-done((f32[5,32,128]{2,1,0:T(8,128)S(1)}, f32[5,32,128]{2,1,0:T(8,128)}, u32[]{:S(2)}) %copy-start) | copy-done | bytes 81944
  2.2 0.0 copy-start.3
  2.2 0.7 %copy-done.3 = s32[32,128]{1,0:T(8,128)S(1)} copy-done((s32[32,128]{1,0:T(8,128)S(1)}, s32[32,128]{1,0:T(8,128)}, u32[]{:S(2)}) %copy-start.3) | copy-done | bytes 16408
  2.9 0.0 copy-start.5
  2.9 0.9 %copy-done.5 = f32[5,32,128]{2,1,0:T(8,128)S(1)} copy-done((f32[5,32,128]{2,1,0:T(8,128)S(1)}, f32[5,32,128]{2,1,0:T(8,128)}, u32[]{:S(2)}) %copy-start.5) | copy-done | bytes 81944
  3.8 0.0 copy-start.6
  3.8 0.9 %copy-done.6 = s32[5,32,128]{2,1,0:T(8,128)S(1)} copy-done((s32[5,32,128]{2,1,0:T(8,128)S(1)}, s32[5,32,128]{2,1,0:T(8,128)}, u32[]{:S(2)}) %copy-start.6) | copy-done | bytes 81944
  4.7 0.0 copy-start.8
  4.7 0.7 %copy-done.8 = f32[32,128]{1,0:T(8,128)S(1)} copy-done((f32[32,128]{1,0:T(8,128)S(1)}, f32[32,128]{1,0:T(8,128)}, u32[]{:S(2)}) %copy-start.8) | copy-done | bytes 16408
  5.4 0.0 copy-start.10
  5.4 0.7 %copy-done.10 = s32[32,128]{1,0:T(8,128)S(1)} copy-done((s32[32,128]{1,0:T(8,128)S(1)}, s32[32,128]{1,0:T(8,128)}, u32[]{:S(2)}) %copy-start.10) | copy-done | bytes 16408
  6.2 0.0 copy-start.11
  6.2 0.7 %copy-done.11 = s32[32,128]{1,0:T(8,128)S(1)} copy-done((s32[32,128]{1,0:T(8,128)S(1)}, s32[32,128]{1,0:T(8,128)}, u32[]{:S(2)}) %copy-start.11) | copy-done | bytes 16408
  6.9 0.0 copy-start.1
  6.9 0.3 shard_map.157
  7.2 3.9 %collective-permute-start = (f32[48,128]{1,0:T(8,128)S(1)}, f32[48,128]{1,0:T(8,128)S(1)}, u32[]{:S(2)}, u32[]{:S(2)}) collective-permute-start(f32[48,128]{1,0:T(8,128)S(1)} %get-tuple-element.19), channel_id=1, source_target_pairs={{0,16},{16,32},{32,48},{48,64},{64,80},{80,96},{96,112},{112,128},... | collective-permute-start | bytes 73736 | tf_op jit(solution)/shard_map/ppermute | solution.py:317
  11.1 1.3 %collective-permute-start.1 = (f32[48,128]{1,0:T(8,128)S(1)}, f32[48,128]{1,0:T(8,128)S(1)}, u32[]{:S(2)}, u32[]{:S(2)}) collective-permute-start(f32[48,128]{1,0:T(8,128)S(1)} %get-tuple-element.20), channel_id=1, source_target_pairs={{16,0},{32,16},{48,32},{64,48},{80,64},{96,80},{112,96},{128,112},... | collective-permute-start | bytes 73736 | tf_op jit(solution)/shard_map/ppermute | solution.py:317
  12.4 0.0 collective-permute-done.before
  12.4 3.3 %collective-permute-done.1.after = f32[48,128]{1,0:T(8,128)S(1)} collective-permute-done((f32[48,128]{1,0:T(8,128)S(1)}, f32[48,128]{1,0:T(8,128)S(1)}, u32[]{:S(2)}, u32[]{:S(2)}) %collective-permute-start.1) | collective-permute-done | bytes 24608 | tf_op jit(solution)/shard_map/ppermute | solution.py:317
  15.7 0.0 copy-done.1
  15.7 0.0 copy-start.4
  15.7 0.0 copy-start.9
  15.7 0.2 shard_map.158
  15.9 7.3 %collective-permute-start.2 = (f32[40,128]{1,0:T(8,128)S(1)}, f32[40,128]{1,0:T(8,128)S(1)}, u32[]{:S(2)}, u32[]{:S(2)}) collective-permute-start(f32[40,128]{1,0:T(8,128)S(1)} %get-tuple-element.23), channel_id=1, source_target_pairs={{1,0},{2,1},{3,2},{4,3},{5,4},{6,5},{7,6},{8,7},{9,8},{10,9},{11,1... | collective-permute-start | bytes 61448 | tf_op jit(solution)/shard_map/ppermute | solution.py:317
  23.2 1.9 %collective-permute-start.3 = (f32[40,128]{1,0:T(8,128)S(1)}, f32[40,128]{1,0:T(8,128)S(1)}, u32[]{:S(2)}, u32[]{:S(2)}) collective-permute-start(f32[40,128]{1,0:T(8,128)S(1)} %get-tuple-element.23), channel_id=1, source_target_pairs={{0,1},{1,2},{2,3},{3,4},{4,5},{5,6},{6,7},{7,8},{8,9},{9,10},{10,1... | collective-permute-start | bytes 61448 | tf_op jit(solution)/shard_map/ppermute | solution.py:317
  25.1 0.0 collective-permute-done.2.right
  25.1 1.1 %collective-permute-done.3.left = f32[40,128]{1,0:T(8,128)S(1)} collective-permute-done((f32[40,128]{1,0:T(8,128)S(1)}, f32[40,128]{1,0:T(8,128)S(1)}, u32[]{:S(2)}, u32[]{:S(2)}) %collective-permute-start.3) | collective-permute-done | bytes 20512 | tf_op jit(solution)/shard_map/ppermute | solution.py:317
  26.2 0.0 copy-done.4
  26.2 0.0 copy-done.9
  26.3 0.0 copy-start.17
  26.3 2.0 %shard_map.159 = (f32[5,32,128]{2,1,0:T(8,128)S(1)}, f32[5,32,128]{2,1,0:T(8,128)S(1)}, f32[32,128]{1,0:T(8,128)}, f32[32,128]{1,0:T(8,128)}) custom-call(f32[15,40,128]{2,1,0:T(8,128)S(1)} %get-tuple-element.22.ext, f32[40,128]{1,0:T(8,128)S(1)} %collective-permute-done.2.right, f32[40,128]{1,0:T(8,128)S(1)} %collective-permute-done.3.left, ...), custom_call_target="tpu_custom_call" | custom-call | tf_op jit(solution)/shard_map/pallas_call | solution.py:352
  28.3 10.2 %all-to-all-start = ((f32[32,1,128]{2,1,0:T(1,128)}), f32[32,1,128]{2,1,0:T(1,128)S(1)}, u32[]{:S(2)}, u32[]{:S(2)}) async-start(f32[32,1,128]{2,1,0:T(1,128)} %bitcast.5), calls=%async_computation | async-start | bytes 32768 | tf_op jit(solution)/shard_map/all_to_all | solution.py:322
  38.5 0.0 copy-done.17
  38.5 0.2 copy.22
  38.6 0.1 reshape.25
  38.7 0.1 copy.23
  38.9 8.1 %all-to-all-done = f32[32,1,128]{2,1,0:T(1,128)S(1)} async-done(((f32[32,1,128]{2,1,0:T(1,128)}), f32[32,1,128]{2,1,0:T(1,128)S(1)}, u32[]{:S(2)}, u32[]{:S(2)}) %all-to-all-start) | async-done | bytes 16416 | tf_op jit(solution)/shard_map/all_to_all | solution.py:322
  47.0 0.8 %shard_map.160 = f32[16,128]{1,0:T(8,128)} custom-call(f32[32,128]{1,0:T(8,128)S(1)} %bitcast.15), custom_call_target="tpu_custom_call" | custom-call | tf_op jit(solution)/shard_map/pallas_call | solution.py:358
  47.7 0.0 copy-start.2
  47.8 13.4 %all-to-all-start.1 = ((f32[16,1,128]{2,1,0:T(1,128)}), f32[16,1,128]{2,1,0:T(1,128)S(1)}, u32[]{:S(2)}, u32[]{:S(2)}) async-start(f32[16,1,128]{2,1,0:T(1,128)} %bitcast.8), calls=%async_computation.1 | async-start | bytes 16384 | tf_op jit(solution)/shard_map/all_to_all | solution.py:322
  61.2 0.0 copy-start.7
  61.2 0.0 copy-done.2
  61.2 0.7 copy-done.7
  61.9 0.0 copy-start.12
  61.9 5.8 %shard_map.161.base = f32[20,32,128]{2,1,0:T(8,128)S(1)} custom-call(f32[20,32,128]{2,1,0:T(8,128)S(1)} %copy-done.2, s32[32,128]{1,0:T(8,128)S(1)} %copy-done.7, s32[32,128]{1,0:T(8,128)S(1)} %copy-done.4, f32[400,128]{1,0:T(8,128)S(1)} %pad.4.table), custom_call_target="tpu_custom_call" | custom-call | flops 20000000 | bytes 2000000 | tf_op jit(solution)/shard_map/pallas_call | solution.py:349
  67.7 0.4 all-to-all-done.1
  68.1 0.0 copy-done.12
  68.1 1.4 %shard_map.162 = (f32[5,32,128]{2,1,0:T(8,128)}, f32[20,32,128]{2,1,0:T(8,128)}) custom-call(f32[16,128]{1,0:T(8,128)S(1)} %bitcast.16, f32[5,32,128]{2,1,0:T(8,128)S(1)} %copy-done.1, f32[5,32,128]{2,1,0:T(8,128)S(1)} %get-tuple-element.26.v1, f32[5,32,128]{2,1,0:T(8,128)S(1)} %get-tuple-element.27.v2, f32[20,32,128]{2,1,0:T(8,128)S(1)} %shard_map.161.base, ...), custom_call_target="tpu_custom_call" | custom-call | tf_op jit(solution)/shard_map/pallas_call | solution.py:360
  (2 shorter events, 0.0 us)
Async XLA Ops:
  0.6 0.7 copy-start.16
  0.6 0.7 copy-start.13
  0.7 0.7 copy-start.14
  0.7 0.7 copy-start.15
  1.3 0.9 %copy-start = (f32[5,32,128]{2,1,0:T(8,128)S(1)}, f32[5,32,128]{2,1,0:T(8,128)}, u32[]{:S(2)}) copy-start(f32[5,32,128]{2,1,0:T(8,128)} %rhs.5) | copy-start | bytes 245764
  2.2 0.7 %copy-start.3 = (s32[32,128]{1,0:T(8,128)S(1)}, s32[32,128]{1,0:T(8,128)}, u32[]{:S(2)}) copy-start(s32[32,128]{1,0:T(8,128)} %land.7) | copy-start | bytes 49156
  2.9 0.9 %copy-start.5 = (f32[5,32,128]{2,1,0:T(8,128)S(1)}, f32[5,32,128]{2,1,0:T(8,128)}, u32[]{:S(2)}) copy-start(f32[5,32,128]{2,1,0:T(8,128)} %pressure.1) | copy-start | bytes 245764
  3.8 0.9 %copy-start.6 = (s32[5,32,128]{2,1,0:T(8,128)S(1)}, s32[5,32,128]{2,1,0:T(8,128)}, u32[]{:S(2)}) copy-start(s32[5,32,128]{2,1,0:T(8,128)} %geology.1) | copy-start | bytes 245764
  4.7 0.7 %copy-start.8 = (f32[32,128]{1,0:T(8,128)S(1)}, f32[32,128]{1,0:T(8,128)}, u32[]{:S(2)}) copy-start(f32[32,128]{1,0:T(8,128)} %ponding.3) | copy-start | bytes 49156
  5.4 0.7 %copy-start.10 = (s32[32,128]{1,0:T(8,128)S(1)}, s32[32,128]{1,0:T(8,128)}, u32[]{:S(2)}) copy-start(s32[32,128]{1,0:T(8,128)} %slope_class.1) | copy-start | bytes 49156
  6.2 0.7 %copy-start.11 = (s32[32,128]{1,0:T(8,128)S(1)}, s32[32,128]{1,0:T(8,128)}, u32[]{:S(2)}) copy-start(s32[32,128]{1,0:T(8,128)} %flow.1) | copy-start | bytes 49156
  6.9 8.8 %copy-start.1 = (f32[5,32,128]{2,1,0:T(8,128)S(1)}, f32[5,32,128]{2,1,0:T(8,128)}, u32[]{:S(2)}) copy-start(f32[5,32,128]{2,1,0:T(8,128)} %rhs.5) | copy-start | bytes 245764
  7.2 5.3 %collective-permute-start = (f32[48,128]{1,0:T(8,128)S(1)}, f32[48,128]{1,0:T(8,128)S(1)}, u32[]{:S(2)}, u32[]{:S(2)}) collective-permute-start(f32[48,128]{1,0:T(8,128)S(1)} %get-tuple-element.19), channel_id=1, source_target_pairs={{0,16},{16,32},{32,48},{48,64},{64,80},{80,96},{96,112},{112,128},... | collective-permute-start | bytes 73736 | tf_op jit(solution)/shard_map/ppermute | solution.py:317
  11.1 4.6 %collective-permute-start.1 = (f32[48,128]{1,0:T(8,128)S(1)}, f32[48,128]{1,0:T(8,128)S(1)}, u32[]{:S(2)}, u32[]{:S(2)}) collective-permute-start(f32[48,128]{1,0:T(8,128)S(1)} %get-tuple-element.20), channel_id=1, source_target_pairs={{16,0},{32,16},{48,32},{64,48},{80,64},{96,80},{112,96},{128,112},... | collective-permute-start | bytes 73736 | tf_op jit(solution)/shard_map/ppermute | solution.py:317
  15.7 10.6 %copy-start.4 = (s32[32,128]{1,0:T(8,128)S(1)}, s32[32,128]{1,0:T(8,128)}, u32[]{:S(2)}) copy-start(s32[32,128]{1,0:T(8,128)} %land.7) | copy-start | bytes 49156
  15.7 10.6 %copy-start.9 = (f32[32,128]{1,0:T(8,128)S(1)}, f32[32,128]{1,0:T(8,128)}, u32[]{:S(2)}) copy-start(f32[32,128]{1,0:T(8,128)} %ponding.3) | copy-start | bytes 49156
  15.9 9.2 %collective-permute-start.2 = (f32[40,128]{1,0:T(8,128)S(1)}, f32[40,128]{1,0:T(8,128)S(1)}, u32[]{:S(2)}, u32[]{:S(2)}) collective-permute-start(f32[40,128]{1,0:T(8,128)S(1)} %get-tuple-element.23), channel_id=1, source_target_pairs={{1,0},{2,1},{3,2},{4,3},{5,4},{6,5},{7,6},{8,7},{9,8},{10,9},{11,1... | collective-permute-start | bytes 61448 | tf_op jit(solution)/shard_map/ppermute | solution.py:317
  23.2 3.1 %collective-permute-start.3 = (f32[40,128]{1,0:T(8,128)S(1)}, f32[40,128]{1,0:T(8,128)S(1)}, u32[]{:S(2)}, u32[]{:S(2)}) collective-permute-start(f32[40,128]{1,0:T(8,128)S(1)} %get-tuple-element.23), channel_id=1, source_target_pairs={{0,1},{1,2},{2,3},{3,4},{4,5},{5,6},{6,7},{7,8},{8,9},{9,10},{10,1... | collective-permute-start | bytes 61448 | tf_op jit(solution)/shard_map/ppermute | solution.py:317
  26.3 12.2 %copy-start.17 = (f32[12,20,20]{2,1,0:T(8,128)S(1)}, f32[12,20,20]{2,1,0:T(8,128)}, u32[]{:S(2)}) copy-start(f32[12,20,20]{2,1,0:T(8,128)} %param.26) | copy-start | bytes 57604
  28.3 18.7 %all-to-all-start = ((f32[32,1,128]{2,1,0:T(1,128)}), f32[32,1,128]{2,1,0:T(1,128)S(1)}, u32[]{:S(2)}, u32[]{:S(2)}) async-start(f32[32,1,128]{2,1,0:T(1,128)} %bitcast.5), calls=%async_computation | async-start | bytes 32768 | tf_op jit(solution)/shard_map/all_to_all | solution.py:322
  47.7 13.4 %copy-start.2 = (f32[20,32,128]{2,1,0:T(8,128)S(1)}, f32[20,32,128]{2,1,0:T(8,128)}, u32[]{:S(2)}) copy-start(f32[20,32,128]{2,1,0:T(8,128)} %state.1) | copy-start | bytes 983044
  47.8 20.3 %all-to-all-start.1 = ((f32[16,1,128]{2,1,0:T(1,128)}), f32[16,1,128]{2,1,0:T(1,128)S(1)}, u32[]{:S(2)}, u32[]{:S(2)}) async-start(f32[16,1,128]{2,1,0:T(1,128)} %bitcast.8), calls=%async_computation.1 | async-start | bytes 16384 | tf_op jit(solution)/shard_map/all_to_all | solution.py:322
  61.2 0.7 %copy-start.7 = (s32[32,128]{1,0:T(8,128)S(1)}, s32[32,128]{1,0:T(8,128)}, u32[]{:S(2)}) copy-start(s32[32,128]{1,0:T(8,128)} %soil_class.3) | copy-start | bytes 49156
  61.9 6.2 %copy-start.12 = (f32[32,128]{1,0:T(8,128)S(1)}, f32[32,128]{1,0:T(8,128)}, u32[]{:S(2)}) copy-start(f32[32,128]{1,0:T(8,128)} %get-tuple-element.15.pond) | copy-start | bytes 49156

commit v2 on v1

v2 whole, which is shorter than its diff:
```python
import jax
import jax.numpy as jnp
from jax import lax
from jax.experimental import pallas as pl
from jax.experimental.pallas import tpu as pltpu
from jax.sharding import PartitionSpec as P


LAYERS = 5
STATE = 20
CLASSES = 12
W = 3
X, Y = 32, 128
E = X + 8
FIELDS = 3 * LAYERS
G = 2 * W
PAD = 24
F32 = jnp.float32


def two_sum(a, b):
    s = a + b
    t = s - a
    return s, (a - (s - t)) + (b - t)


def renorm(a, b):
    s = a + b
    return s, b - (s - a)


def halves(a):
    t = a * 4097.0
    hi = t - (t - a)
    return hi, a - hi


def two_prod(a, b):
    p = a * b
    (ah, al), (bh, bl) = halves(a), halves(b)
    return p, ((ah * bh - p) + ah * bl + al * bh) + al * bl


def pair_add(a, b):
    s, e = two_sum(a[0], b[0])
    return renorm(s, e + (a[1] + b[1]))


def pair_sub(a, b):
    return pair_add(a, (-b[0], -b[1]))


def pair_mul(a, b):
    p, e = two_prod(a[0], b[0])
    return renorm(p, e + (a[0] * b[1] + a[1] * b[0]))


def pair_div(a, b):
    q = a[0] / b[0]
    r = pair_sub(a, pair_mul((q, jnp.zeros_like(q)), b))
    q2 = r[0] / b[0]
    r = pair_sub(r, pair_mul((q2, jnp.zeros_like(q)), b))
    return pair_add(renorm(q, q2), (r[0] / b[0], jnp.zeros_like(q)))


def iota(shape, dim):
    return lax.broadcasted_iota(jnp.int32, shape, dim)


def pick(table, index):
    row = jnp.broadcast_to(table, index.shape)
    return jnp.take_along_axis(row, index, axis=1, mode="promise_in_bounds")


def call(kernel, outs, scratch=(), specs=None, flops=0, nbytes=0):
    extra = {} if specs is None else {"in_specs": specs}
    return pl.pallas_call(
        kernel,
        out_shape=[jax.ShapeDtypeStruct(s, F32) for s in outs],
        scratch_shapes=scratch,
        compiler_params=pltpu.CompilerParams(vmem_limit_bytes=32 * 2**20),
        cost_estimate=pl.CostEstimate(
            flops=flops, bytes_accessed=nbytes, transcendentals=0
        ),
        **extra,
    )


def gather_table(ref, count):
    lane = iota((1, Y), 1)
    row = jnp.full((1, Y), 1.0, F32)
    for i in range(count):
        row = jnp.where(lane == i, ref[i], row)
    return row


def local_kernel(*refs):
    (cond, diag, slab, east, south), held, sem = refs[11:16], refs[16:27], refs[27]
    copies = [
        pltpu.make_async_copy(refs[i], held[i], sem.at[i]) for i in range(11)
    ]
    for copy in copies:
        copy.start()
    for copy in copies:
        copy.wait()
    (pressure, rhs, geology, ks, alpha, expo, land, ponding, slope_class, slope, flow) = held
    t_ks = gather_table(ks, 16)
    t_la = jnp.log(gather_table(alpha, 16))
    t_n = gather_table(expo, 16)
    t_m = 1.0 - 1.0 / t_n
    t_slope = jnp.sqrt(gather_table(slope, 8)) / 0.03
    sea = 4.0 * (1.0 - land[...].astype(F32))
    for l in range(LAYERS):
        g = geology[l]
        p = jnp.abs(pressure[l])
        n = pick(t_n, g)
        m = pick(t_m, g)
        t = jnp.exp(n * (pick(t_la, g) + jnp.log(p)))
        one_t = 1.0 + t
        e = jnp.exp(-m * jnp.log(one_t))
        k = pick(t_ks, g) * e
        d = 0.05 + 0.4 * m * n * t * e / (p * one_t) + sea
        cond[l] = k
        diag[l] = d
        for f, x in enumerate((rhs[l], k, d)):
            slab[f * LAYERS + l] = x[0 : E - X]
    out = pick(t_slope, slope_class[...]) * jnp.exp((5.0 / 3.0) * jnp.log(ponding[...]))
    eastward = jnp.where(flow[...] == 0, out, 0.0)
    east[...] = eastward
    south[...] = out - eastward


def pack_kernel(rhs, cond, diag, after, south, packed):
    for lo, rows in ((0, X), (X, E - X)):
        lane = iota((rows, Y), 1)
        total = jnp.zeros((rows, Y), F32)
        for f, ref in enumerate((rhs, cond, diag)):
            for l in range(LAYERS):
                q = f * LAYERS + l
                x = pltpu.roll(after[q] if lo else ref[l], (W + G * q) % Y, 1)
                total = jnp.where((lane >= G * q) & (lane < G * q + G), x, total)
        if not lo:
            x = pltpu.roll(south[...], (W + G * FIELDS) % Y, 1)
            total = jnp.where(lane >= G * FIELDS, x, total)
        packed[lo : lo + rows, :] = total


def krylov_kernel(
    rhs, cond, diag, after, right, left, east, v1_out, v2_out, row_out, back_out,
    fr, fc, fv, dd, v,
):
    lane, row_of = iota((E, Y), 1), iota((E, Y), 0)
    first, last = lane == 0, lane == Y - 1

    def turn(m, h, by, edge):
        m, h = pltpu.roll(m, by, 1), pltpu.roll(h, by, 1)
        return jnp.where(edge, h, m), jnp.where(edge, m, h)

    w = jnp.where(lane % G >= W, right[...], left[...])

    def both(ref, f, l):
        q = f * LAYERS + l
        return (
            jnp.concatenate([ref[l], after[q]], axis=0),
            pltpu.roll(w, (-(W + G * q)) % Y, 1),
        )

    def harmonic(a, b):
        return 2.0 * a * b / jnp.maximum(a + b, 1e-30)

    above = None
    for l in range(LAYERS):
        v[0, l], v[1, l] = both(rhs, 0, l)
        k = both(cond, 1, l)
        dd[0, l], dd[1, l] = both(diag, 2, l)
        west = turn(*k, 1, first)
        for s in range(2):
            fr[s, l] = jnp.where(row_of == 0, 0.0, harmonic(k[s], pltpu.roll(k[s], 1, 0)))
            fc[s, l] = harmonic(k[s], west[s])
            if l:
                fv[s, l - 1] = harmonic(k[s], above[s])
        above = k

    def product(l, flux_above):
        vm, vh = v[0, l], v[1, l]
        west = turn(vm, vh, 1, first)
        side = fc[0, l] * (vm - west[0]), fc[1, l] * (vh - west[1])
        gone = turn(*side, Y - 1, last)
        outs, flux = [], []
        for s, x in enumerate((vm, vh)):
            rows = fr[s, l] * (x - pltpu.roll(x, 1, 0))
            r = dd[s, l] * x + (rows - pltpu.roll(rows, E - 1, 0)) + (side[s] - gone[s])
            if l:
                r = r - flux_above[s]
            if l < LAYERS - 1:
                fl = fv[s, l] * (x - v[s, l + 1])
                r = r + fl
                flux.append(fl)
            outs.append(r)
        return outs, flux

    zero = jnp.zeros((8, Y), F32)
    sums = [(zero, zero)] * 6
    sub = iota((8, Y), 0)
    start = jnp.where(lax.axis_index("gx") == 0, 0, W)

    def add_to(j, a, b):
        p, e = two_prod(a, b)
        s, e2 = two_sum(sums[j][0], p)
        sums[j] = s, sums[j][1] + (e + e2)

    for step in range(3):
        results, flux = [], None
        for l in range(LAYERS):
            outs, flux = product(l, flux)
            old, new = v[0, l], outs[0]
            for i in range(0, E, 8):
                a, b = old[i : i + 8], new[i : i + 8]
                if i == 0 or i == X:
                    keep = sub >= start if i == 0 else sub < W
                    a, b = jnp.where(keep, a, 0.0), jnp.where(keep, b, 0.0)
                add_to(2 * step, a, a)
                add_to(2 * step + 1, a, b)
            results.append(outs)
        if step < 2:
            for l in range(LAYERS):
                m = results[l][0]
                v[0, l], v[1, l] = results[l]
                (v1_out, v2_out)[step][l] = m[0:X]
                if step:
                    back_out[LAYERS + 2 * l : LAYERS + 2 * l + 2, :] = m[X : X + 2]
                else:
                    back_out[l : l + 1, :] = m[X : X + 1]
    back_out[3 * LAYERS : 3 * LAYERS + 1, :] = east[X - 1 : X, :]

    ln = iota((8, Y), 1)
    total = zero, zero
    for j in range(6):
        s = fold(sums[j], (4, 2, 1), 0)
        total = tuple(jnp.where(sub == j, a, b) for a, b in zip(s, total))
    total = renorm(*fold(total, (64, 32, 16, 8, 4, 2, 1), 1))
    row = jnp.where(ln == sub, total[0], jnp.where(ln == sub + 8, total[1], 0.0))
    row = jnp.sum(row, axis=0, keepdims=True)
    row_out[...] = jnp.broadcast_to(row, row_out.shape)


def fold(s, steps, dim):
    for by in steps:
        hi, e = two_sum(s[0], pltpu.roll(s[0], by, dim))
        s = hi, s[1] + pltpu.roll(s[1], by, dim) + e
    return s


def rows_total(ref):
    parts = [
        (ref[i : i + 8, :], pltpu.roll(ref[i : i + 8, :], Y - 8, 1))
        for i in range(0, ref.shape[0], 8)
    ]
    while len(parts) > 1:
        parts = [pair_add(a, b) for a, b in zip(parts[::2], parts[1::2])]
    return renorm(*fold(parts[0], (4, 2, 1), 0))


def relay_kernel(rows, row_out):
    hi, lo = rows_total(rows)
    ln = iota((8, Y), 1)
    both = jnp.where(ln < 8, hi, pltpu.roll(lo, 8, 1))
    for i in range(0, row_out.shape[0], 8):
        row_out[i : i + 8, :] = both


def soil_kernel(state, soil_class, land, inverse, base, water, head, w, w01):
    w[...] = jnp.zeros(w.shape, F32)
    w01[...] = jnp.zeros(w01.shape, F32)
    for e in range(CLASSES):
        x = inverse[e]
        w[0:STATE, e * PAD : e * PAD + STATE] = x
        w01[0:STATE, e : e + 1] = x[:, 0:1]
        w01[PAD : PAD + STATE, e : e + 1] = x[:, 1:2]
    w_all, w_two = w[...], w01[...]
    zero = jnp.zeros((PAD - STATE, Y), F32)
    entry = iota((16, Y), 0)

    def dot(a, columns):
        return jnp.dot(
            a,
            jnp.concatenate(columns, axis=1),
            precision=lax.Precision.HIGHEST,
            preferred_element_type=F32,
        )

    for x0 in range(0, X, 4):
        fields, spread, hot, kinds = [], [], [], []
        for x in range(x0, x0 + 4):
            f = state[pl.ds(x, STATE, stride=X), :]
            kind = jnp.where(land[x : x + 1, :] == 1, soil_class[x : x + 1, :], -1)
            padded = jnp.concatenate([f, zero], axis=0)
            spread.append(
                jnp.concatenate(
                    [jnp.where(kind == e, padded, 0.0) for e in range(CLASSES)], axis=0
                )
            )
            hot.append(jnp.where(kind == entry, 0.5, 0.0))
            fields.append(f)
            kinds.append(kind)
        solved, two = dot(w_all, spread), dot(w_two, hot)
        for n in range(4):
            here = pl.ds(x0 + n, STATE, stride=X)
            cut = slice(n * Y, n * Y + Y)
            base[here, :] = jnp.where(kinds[n] >= 0, solved[0:STATE, cut], fields[n])
            water[here, :] = two[0:STATE, cut]
            head[here, :] = two[PAD : PAD + STATE, cut]


def final_kernel(
    rows, rhs, v1, v2, back, base, water, head, left, east, south, ponding, land,
    corr_out, pond_out, soil_out,
):
    hi, lo = rows_total(rows)
    mu = [
        tuple(jnp.broadcast_to(t[:, j : j + 1], (8, Y)) for t in (hi, lo))
        for j in range(6)
    ]
    l21 = pair_div(mu[2], mu[1])
    l31 = pair_div(mu[3], mu[1])
    d2 = pair_sub(mu[3], pair_mul(l21, mu[2]))
    u = pair_sub(mu[4], pair_mul(l31, mu[2]))
    l32 = pair_div(u, d2)
    d3 = pair_sub(pair_sub(mu[5], pair_mul(l31, mu[3])), pair_mul(l32, u))
    y2 = pair_sub(mu[1], pair_mul(l21, mu[0]))
    y3 = pair_sub(pair_sub(mu[2], pair_mul(l31, mu[0])), pair_mul(l32, y2))
    c3 = pair_div(y3, d3)
    c2 = pair_sub(pair_div(y2, d2), pair_mul(l32, c3))
    c1 = pair_sub(
        pair_sub(pair_div(mu[0], mu[1]), pair_mul(l21, c2)), pair_mul(l31, c3)
    )
    c1, c2, c3 = (jnp.concatenate([c[0]] * (X // 8), axis=0) for c in (c1, c2, c3))

    row, lane = iota((X, Y), 0), iota((X, Y), 1)
    es, so = east[...], south[...]
    north = pltpu.roll(left[0:X, :], (-(W + G * FIELDS)) % Y, 1)
    inflow = jnp.where(
        row == 0, back[3 * LAYERS : 3 * LAYERS + 1, :], pltpu.roll(es, 1, 0)
    ) + jnp.where(lane == 0, pltpu.roll(north, 1, 1), pltpu.roll(so, 1, 1))
    pond = land[...].astype(F32) * (ponding[...] + 0.2 * (inflow - (es + so)))
    pond_out[...] = pond

    given = jnp.where(lax.axis_index("gx") == 0, 0, 1)
    top = None
    for l in range(LAYERS):
        q = LAYERS + 2 * l
        a1 = jnp.where(row < given, back[l : l + 1, :], v1[l])
        a2 = jnp.where(row < given, back[q : q + 1, :], v2[l])
        a2 = jnp.where((row == 1) & (given > 0), back[q + 1 : q + 2, :], a2)
        x = c1 * rhs[l] + c2 * a1 + c3 * a2
        corr_out[l] = x
        top = x if top is None else top
    for i in range(STATE):
        here = slice(i * X, i * X + X)
        soil_out[i] = base[here, :] + water[here, :] * pond + head[here, :] * top


def ahead(x, axis):
    return lax.ppermute(x, axis, [(i, i + 1) for i in range(lax.axis_size(axis) - 1)])


def back(x, axis):
    return lax.ppermute(x, axis, [(i + 1, i) for i in range(lax.axis_size(axis) - 1)])


def everyones(rows, axis):
    count = lax.axis_size(axis)
    return lax.all_to_all(rows.reshape(count, 1, Y), axis, 0, 0).reshape(count, Y)


def on_device(
    pressure, newton_rhs, geology, saturated_conductivity, genuchten_alpha,
    genuchten_exponent, land_mask, ponding, slope_class, slope_table,
    flow_direction, soil_class, soil_inverse, soil_state,
):
    block, plane, tall = (LAYERS, X, Y), (X, Y), (STATE * X, Y)
    local = (
        pressure, newton_rhs, geology, saturated_conductivity, genuchten_alpha,
        genuchten_exponent, land_mask, ponding, slope_class, slope_table,
        flow_direction,
    )
    cond, diag, slab, east, south = call(
        local_kernel,
        [block, block, (FIELDS, E - X, Y), plane, plane],
        [(pltpu.SMEM if a.ndim == 1 else pltpu.VMEM)(a.shape, a.dtype) for a in local]
        + [pltpu.SemaphoreType.DMA((len(local),))],
        [pl.BlockSpec(memory_space=pltpu.HBM)] * len(local),
    )(*(pltpu.with_memory_space_constraint(a, pltpu.HBM) for a in local))
    after = back(slab, "gx")
    (packed,) = call(pack_kernel, [(E, Y)])(newton_rhs, cond, diag, after, south)
    left, right = ahead(packed, "gy"), back(packed, "gy")
    v1, v2, rows, edge = call(
        krylov_kernel,
        [block, block, (lax.axis_size("gx"), Y), (16, Y)],
        [pltpu.VMEM((2, n, E, Y), F32) for n in (5, 5, 4, 5, 5)],
    )(newton_rhs, cond, diag, after, right, left, east)
    edge = ahead(edge, "gx")
    base, water, head = call(
        soil_kernel,
        [tall] * 3,
        [pltpu.VMEM((PAD, CLASSES * PAD), F32), pltpu.VMEM((2 * PAD, 16), F32)],
        flops=20_000_000,
        nbytes=2_000_000,
    )(soil_state.reshape(tall), soil_class, land_mask, soil_inverse)
    rows = everyones(rows, "gx")
    rows, base, water, head = lax.optimization_barrier((rows, base, water, head))
    (rows,) = call(relay_kernel, [(lax.axis_size("gy"), Y)])(rows)
    rows = everyones(rows, "gy")
    return call(final_kernel, [block, plane, (STATE, X, Y)])(
        rows, newton_rhs, v1, v2, edge, base, water, head, left, east, south,
        ponding, land_mask,
    )


def solution(mesh):
    cells, plane, rest = P(None, "gx", "gy"), P("gx", "gy"), P()
    return jax.shard_map(
        on_device,
        mesh=mesh,
        in_specs=(
            cells, cells, cells, rest, rest, rest, plane, plane, plane, rest, plane,
            plane, rest, cells,
        ),
        out_specs=(cells, plane, cells),
        check_vma=False,
    )
```

time: 70.2 us -> 61.6 us (0.88)
  local copies, waits for them, and re-layouts: 7.33 us -> 0.02 us
  waiting for transfers between devices: 12.9 us -> 14.7 us
  starting transfers between devices: 38 us -> 36.5 us
  Pallas kernels: 10.4 us -> 9.13 us
    unnamed x36 -> x12, local copies, waits for them, and re-layouts: 6.9 us -> 0.02 us
    ppermute x4, waiting for transfers between devices: 4.41 us -> 5.84 us  [the longest x2 5.06 us: back(): lax.ppermute(x, axis, [(i + 1, i) for i in range(lax.axis_size(axis) - 1)])]
    pallas_call x5, Pallas kernels: 9.65 us -> 8.37 us  [the longest x1 3.51 us: on_device(): call(soil_kernel, [tall] * 3, [pltpu.VMEM((PAD, CLASSES * PAD), F32), plt...]
    all_to_all x2, starting transfers between devices: 23.6 us -> 22.4 us  [everyones(): lax.all_to_all(rows.reshape(count, 1, Y), axis, 0, 0).reshape(count, Y)]
  transfers between devices with their start and end apart: 6 -> 6, of which waited for: 4 -> 5; matrix products, arithmetic and copies ran while one was open for 1% -> 0% of each run, Pallas kernels for 8% -> 6%
where the time goes in v2:
time: 61.6 us; the launch traced here: 61.1 us
  starting transfers between devices  36.5 us (59%)
  waiting for transfers between devices  14.7 us (24%)
  Pallas kernels  9.13 us (15%)
  between operations  0.75 us (1%)
    all_to_all x2, starting transfers between devices, everyones(): lax.all_to_all(rows.reshape(count, 1, Y), axis, 0, 0).reshape(count, Y)  22.4 us
    all_to_all x2, waiting for transfers between devices, everyones(): lax.all_to_all(rows.reshape(count, 1, Y), axis, 0, 0).reshape(count, Y)  8.89 us
    ppermute x2, starting transfers between devices, ahead(): lax.ppermute(x, axis, [(i, i + 1) for i in range(lax.axis_size(axis) - 1)])  8.18 us
    ppermute x2, starting transfers between devices, back(): lax.ppermute(x, axis, [(i + 1, i) for i in range(lax.axis_size(axis) - 1)])  5.98 us
    ppermute x2, waiting for transfers between devices, back(): lax.ppermute(x, axis, [(i + 1, i) for i in range(lax.axis_size(axis) - 1)])  5.06 us
    pallas_call x1, Pallas kernels, on_device(): call(soil_kernel, [tall] * 3, [pltpu.VMEM((PAD, CLASSES * PAD), F32), plt...  3.51 us
    pallas_call x1, Pallas kernels, on_device(): call(krylov_kernel, [block, block, (lax.axis_size('gx'), Y), (16, Y)], [p...  2.05 us
    pallas_call x1, Pallas kernels, on_device(): call(local_kernel, [block, block, (FIELDS, E - X, Y), plane, plane], [(pl...  1.45 us
  transfers between devices with their start and end apart: 6, of which 5 were waited for; matrix products, arithmetic and copies ran while one was open for 0% of the time, Pallas kernels for 6%

profile of v2, /device:TPU:1, one launch (start us, length us, event | category | flops | bytes accessed | tf_op | source)
XLA Modules:
  0.0 61.1 jit_solution(18127342160206019872)
XLA Ops:
  0.6 0.0 copy-start
  0.6 1.4 %shard_map.157 = (f32[5,32,128]{2,1,0:T(8,128)S(1)}, f32[5,32,128]{2,1,0:T(8,128)S(1)}, f32[15,8,128]{2,1,0:T(8,128)S(1)}, f32[32,128]{1,0:T(8,128)S(1)}, f32[32,128]{1,0:T(8,128)S(1)}) custom-call(f32[5,32,128]{2,1,0:T(8,128)} %refs_0_.1, f32[5,32,128]{2,1,0:T(8,128)} %rhs.5, s32[5,32,128]{2,1,0:T(8,128)} %refs_2_.1, f32[16]{0:T(128)} %refs_3_.1, ...), custom_call_target="tpu_custom_call" | custom-call | tf_op jit(solution)/shard_map/pallas_call | solution.py:387
  2.1 1.3 %collective-permute-start = (f32[15,8,128]{2,1,0:T(8,128)S(1)}, f32[15,8,128]{2,1,0:T(8,128)S(1)}, u32[]{:S(2)}, u32[]{:S(2)}) collective-permute-start(f32[15,8,128]{2,1,0:T(8,128)S(1)} %get-tuple-element.21), channel_id=1, source_target_pairs={{16,0},{32,16},{48,32},{64,48},{80,64},{96,80},{112,96},{128,112},... | collective-permute-start | bytes 184328 | tf_op jit(solution)/shard_map/ppermute | solution.py:368
  3.4 4.3 %collective-permute-done.after = f32[15,8,128]{2,1,0:T(8,128)S(1)} collective-permute-done((f32[15,8,128]{2,1,0:T(8,128)S(1)}, f32[15,8,128]{2,1,0:T(8,128)S(1)}, u32[]{:S(2)}, u32[]{:S(2)}) %collective-permute-start) | collective-permute-done | bytes 61472 | tf_op jit(solution)/shard_map/ppermute | solution.py:368
  7.7 0.0 copy-done
  7.7 0.0 copy-start.1
  7.7 0.1 shard_map.158
  7.8 6.0 %collective-permute-start.2 = (f32[40,128]{1,0:T(8,128)S(1)}, f32[40,128]{1,0:T(8,128)S(1)}, u32[]{:S(2)}, u32[]{:S(2)}) collective-permute-start(f32[40,128]{1,0:T(8,128)S(1)} %shard_map.158), channel_id=1, source_target_pairs={{0,1},{1,2},{2,3},{3,4},{4,5},{5,6},{6,7},{7,8},{8,9},{9,10},{10,1... | collective-permute-start | bytes 61448 | tf_op jit(solution)/shard_map/ppermute | solution.py:364
  13.8 4.7 %collective-permute-start.1 = (f32[40,128]{1,0:T(8,128)S(1)}, f32[40,128]{1,0:T(8,128)S(1)}, u32[]{:S(2)}, u32[]{:S(2)}) collective-permute-start(f32[40,128]{1,0:T(8,128)S(1)} %shard_map.158), channel_id=1, source_target_pairs={{1,0},{2,1},{3,2},{4,3},{5,4},{6,5},{7,6},{8,7},{9,8},{10,9},{11,1... | collective-permute-start | bytes 61448 | tf_op jit(solution)/shard_map/ppermute | solution.py:368
  18.5 0.0 collective-permute-done.2.left
  18.5 0.8 %collective-permute-done.1.right = f32[40,128]{1,0:T(8,128)S(1)} collective-permute-done((f32[40,128]{1,0:T(8,128)S(1)}, f32[40,128]{1,0:T(8,128)S(1)}, u32[]{:S(2)}, u32[]{:S(2)}) %collective-permute-start.1) | collective-permute-done | bytes 20512 | tf_op jit(solution)/shard_map/ppermute | solution.py:368
  19.3 0.0 copy-start.2
  19.3 2.1 %shard_map.159 = (f32[5,32,128]{2,1,0:T(8,128)S(1)}, f32[5,32,128]{2,1,0:T(8,128)S(1)}, f32[32,128]{1,0:T(8,128)}, f32[16,128]{1,0:T(8,128)S(1)}) custom-call(f32[5,32,128]{2,1,0:T(8,128)S(1)} %copy-done, f32[5,32,128]{2,1,0:T(8,128)S(1)} %get-tuple-element.19.cond, f32[5,32,128]{2,1,0:T(8,128)S(1)} %get-tuple-element.20.diag, ...), custom_call_target="tpu_custom_call" | custom-call | tf_op jit(solution)/shard_map/pallas_call | solution.py:397
  21.3 0.0 copy-start.3
  21.3 0.0 copy-start.5
  21.3 11.2 %all-to-all-start = ((f32[32,1,128]{2,1,0:T(1,128)}), f32[32,1,128]{2,1,0:T(1,128)S(1)}, u32[]{:S(2)}, u32[]{:S(2)}) async-start(f32[32,1,128]{2,1,0:T(1,128)} %bitcast.1), calls=%async_computation | async-start | bytes 32768 | tf_op jit(solution)/shard_map/all_to_all | solution.py:373
  32.6 0.0 copy-done.1
  32.6 0.0 copy-done.2
  32.6 0.0 copy-done.3
  32.6 0.0 copy-done.5
  32.6 3.5 %shard_map.160 = (f32[640,128]{1,0:T(8,128)S(1)}, f32[640,128]{1,0:T(8,128)S(1)}, f32[640,128]{1,0:T(8,128)S(1)}) custom-call(f32[640,128]{1,0:T(8,128)S(1)} %bitcast.9, s32[32,128]{1,0:T(8,128)S(1)} %copy-done.5, s32[32,128]{1,0:T(8,128)S(1)} %copy-done.3, f32[12,20,20]{2,1,0:T(8,128)S(1)} %copy-done.2), custom_call_target="tpu_custom_call" | custom-call | flops 20000000 | bytes 2000000 | tf_op jit(solution)/shard_map/pallas_call | solution.py:403
  36.1 5.0 %all-to-all-done = f32[32,1,128]{2,1,0:T(1,128)S(1)} async-done(((f32[32,1,128]{2,1,0:T(1,128)}), f32[32,1,128]{2,1,0:T(1,128)S(1)}, u32[]{:S(2)}, u32[]{:S(2)}) %all-to-all-start) | async-done | bytes 16416 | tf_op jit(solution)/shard_map/all_to_all | solution.py:373
  41.1 0.8 %shard_map.161 = f32[16,128]{1,0:T(8,128)} custom-call(f32[32,128]{1,0:T(8,128)S(1)} %bitcast.10), custom_call_target="tpu_custom_call" | custom-call | tf_op jit(solution)/shard_map/pallas_call | solution.py:412
  41.9 0.0 copy-start.4
  41.9 11.1 %all-to-all-start.1 = ((f32[16,1,128]{2,1,0:T(1,128)}), f32[16,1,128]{2,1,0:T(1,128)S(1)}, u32[]{:S(2)}, u32[]{:S(2)}) async-start(f32[16,1,128]{2,1,0:T(1,128)} %bitcast.5), calls=%async_computation.1 | async-start | bytes 16384 | tf_op jit(solution)/shard_map/all_to_all | solution.py:373
  53.0 2.2 %collective-permute-start.3 = (f32[16,128]{1,0:T(8,128)S(1)}, f32[16,128]{1,0:T(8,128)S(1)}, u32[]{:S(2)}, u32[]{:S(2)}) collective-permute-start(f32[16,128]{1,0:T(8,128)S(1)} %get-tuple-element.31), channel_id=1, source_target_pairs={{0,16},{16,32},{32,48},{48,64},{64,80},{80,96},{96,112},{112,128},... | collective-permute-start | bytes 24584 | tf_op jit(solution)/shard_map/ppermute | solution.py:364
  55.2 0.8 %collective-permute-done.3.back = f32[16,128]{1,0:T(8,128)S(1)} collective-permute-done((f32[16,128]{1,0:T(8,128)S(1)}, f32[16,128]{1,0:T(8,128)S(1)}, u32[]{:S(2)}, u32[]{:S(2)}) %collective-permute-start.3) | collective-permute-done | bytes 8224 | tf_op jit(solution)/shard_map/ppermute | solution.py:364
  56.0 3.9 %all-to-all-done.1 = f32[16,1,128]{2,1,0:T(1,128)S(1)} async-done(((f32[16,1,128]{2,1,0:T(1,128)}), f32[16,1,128]{2,1,0:T(1,128)S(1)}, u32[]{:S(2)}, u32[]{:S(2)}) %all-to-all-start.1) | async-done | bytes 8224 | tf_op jit(solution)/shard_map/all_to_all | solution.py:373
  59.9 0.0 copy-done.4
  59.9 1.2 %shard_map.162 = (f32[5,32,128]{2,1,0:T(8,128)}, f32[32,128]{1,0:T(8,128)}, f32[20,32,128]{2,1,0:T(8,128)}) custom-call(f32[16,128]{1,0:T(8,128)S(1)} %bitcast.11, f32[5,32,128]{2,1,0:T(8,128)S(1)} %copy-done, f32[5,32,128]{2,1,0:T(8,128)S(1)} %get-tuple-element.29.v1, f32[5,32,128]{2,1,0:T(8,128)S(1)} %get-tuple-element.30.v2, ...), custom_call_target="tpu_custom_call" | custom-call | tf_op jit(solution)/shard_map/pallas_call | solution.py:414
Async XLA Ops:
  0.6 7.0 %copy-start = (f32[5,32,128]{2,1,0:T(8,128)S(1)}, f32[5,32,128]{2,1,0:T(8,128)}, u32[]{:S(2)}) copy-start(f32[5,32,128]{2,1,0:T(8,128)} %rhs.5) | copy-start | bytes 245764
  2.1 5.6 %collective-permute-start = (f32[15,8,128]{2,1,0:T(8,128)S(1)}, f32[15,8,128]{2,1,0:T(8,128)S(1)}, u32[]{:S(2)}, u32[]{:S(2)}) collective-permute-start(f32[15,8,128]{2,1,0:T(8,128)S(1)} %get-tuple-element.21), channel_id=1, source_target_pairs={{16,0},{32,16},{48,32},{64,48},{80,64},{96,80},{112,96},{128,112},... | collective-permute-start | bytes 184328 | tf_op jit(solution)/shard_map/ppermute | solution.py:368
  7.7 24.9 %copy-start.1 = (f32[20,32,128]{2,1,0:T(8,128)S(1)}, f32[20,32,128]{2,1,0:T(8,128)}, u32[]{:S(2)}) copy-start(f32[20,32,128]{2,1,0:T(8,128)} %param.27) | copy-start | bytes 983044
  7.8 10.7 %collective-permute-start.2 = (f32[40,128]{1,0:T(8,128)S(1)}, f32[40,128]{1,0:T(8,128)S(1)}, u32[]{:S(2)}, u32[]{:S(2)}) collective-permute-start(f32[40,128]{1,0:T(8,128)S(1)} %shard_map.158), channel_id=1, source_target_pairs={{0,1},{1,2},{2,3},{3,4},{4,5},{5,6},{6,7},{7,8},{8,9},{9,10},{10,1... | collective-permute-start | bytes 61448 | tf_op jit(solution)/shard_map/ppermute | solution.py:364
  13.8 5.5 %collective-permute-start.1 = (f32[40,128]{1,0:T(8,128)S(1)}, f32[40,128]{1,0:T(8,128)S(1)}, u32[]{:S(2)}, u32[]{:S(2)}) collective-permute-start(f32[40,128]{1,0:T(8,128)S(1)} %shard_map.158), channel_id=1, source_target_pairs={{1,0},{2,1},{3,2},{4,3},{5,4},{6,5},{7,6},{8,7},{9,8},{10,9},{11,1... | collective-permute-start | bytes 61448 | tf_op jit(solution)/shard_map/ppermute | solution.py:368
  19.3 13.3 %copy-start.2 = (f32[12,20,20]{2,1,0:T(8,128)S(1)}, f32[12,20,20]{2,1,0:T(8,128)}, u32[]{:S(2)}) copy-start(f32[12,20,20]{2,1,0:T(8,128)} %inverse.1) | copy-start | bytes 57604
  21.3 11.3 %copy-start.3 = (s32[32,128]{1,0:T(8,128)S(1)}, s32[32,128]{1,0:T(8,128)}, u32[]{:S(2)}) copy-start(s32[32,128]{1,0:T(8,128)} %land.3) | copy-start | bytes 49156
  21.3 11.3 %copy-start.5 = (s32[32,128]{1,0:T(8,128)S(1)}, s32[32,128]{1,0:T(8,128)}, u32[]{:S(2)}) copy-start(s32[32,128]{1,0:T(8,128)} %soil_class.1) | copy-start | bytes 49156
  21.3 19.7 %all-to-all-start = ((f32[32,1,128]{2,1,0:T(1,128)}), f32[32,1,128]{2,1,0:T(1,128)S(1)}, u32[]{:S(2)}, u32[]{:S(2)}) async-start(f32[32,1,128]{2,1,0:T(1,128)} %bitcast.1), calls=%async_computation | async-start | bytes 32768 | tf_op jit(solution)/shard_map/all_to_all | solution.py:373
  41.9 18.1 %copy-start.4 = (f32[32,128]{1,0:T(8,128)S(1)}, f32[32,128]{1,0:T(8,128)}, u32[]{:S(2)}) copy-start(f32[32,128]{1,0:T(8,128)} %ponding.1) | copy-start | bytes 49156
  41.9 18.1 %all-to-all-start.1 = ((f32[16,1,128]{2,1,0:T(1,128)}), f32[16,1,128]{2,1,0:T(1,128)S(1)}, u32[]{:S(2)}, u32[]{:S(2)}) async-start(f32[16,1,128]{2,1,0:T(1,128)} %bitcast.5), calls=%async_computation.1 | async-start | bytes 16384 | tf_op jit(solution)/shard_map/all_to_all | solution.py:373
  53.0 3.0 %collective-permute-start.3 = (f32[16,128]{1,0:T(8,128)S(1)}, f32[16,128]{1,0:T(8,128)S(1)}, u32[]{:S(2)}, u32[]{:S(2)}) collective-permute-start(f32[16,128]{1,0:T(8,128)S(1)} %get-tuple-element.31), channel_id=1, source_target_pairs={{0,16},{16,32},{32,48},{48,64},{64,80},{80,96},{96,112},{112,128},... | collective-permute-start | bytes 24584 | tf_op jit(solution)/shard_map/ppermute | solution.py:364

commit v3 on v2

--- a/solution.py
+++ b/solution.py
@@ -392,6 +392,14 @@
         [pl.BlockSpec(memory_space=pltpu.HBM)] * len(local),
     )(*(pltpu.with_memory_space_constraint(a, pltpu.HBM) for a in local))
     after = back(slab, "gx")
+    base, water, head = call(
+        soil_kernel,
+        [tall] * 3,
+        [pltpu.VMEM((PAD, CLASSES * PAD), F32), pltpu.VMEM((2 * PAD, 16), F32)],
+        flops=20_000_000,
+        nbytes=2_000_000,
+    )(soil_state.reshape(tall), soil_class, land_mask, soil_inverse)
+    after, base, water, head = lax.optimization_barrier((after, base, water, head))
     (packed,) = call(pack_kernel, [(E, Y)])(newton_rhs, cond, diag, after, south)
     left, right = ahead(packed, "gy"), back(packed, "gy")
     v1, v2, rows, edge = call(
@@ -400,15 +408,8 @@
         [pltpu.VMEM((2, n, E, Y), F32) for n in (5, 5, 4, 5, 5)],
     )(newton_rhs, cond, diag, after, right, left, east)
     edge = ahead(edge, "gx")
-    base, water, head = call(
-        soil_kernel,
-        [tall] * 3,
-        [pltpu.VMEM((PAD, CLASSES * PAD), F32), pltpu.VMEM((2 * PAD, 16), F32)],
-        flops=20_000_000,
-        nbytes=2_000_000,
-    )(soil_state.reshape(tall), soil_class, land_mask, soil_inverse)
+    rows, edge = lax.optimization_barrier((rows, edge))
     rows = everyones(rows, "gx")
-    rows, base, water, head = lax.optimization_barrier((rows, base, water, head))
     (rows,) = call(relay_kernel, [(lax.axis_size("gy"), Y)])(rows)
     rows = everyones(rows, "gy")
     return call(final_kernel, [block, plane, (STATE, X, Y)])(

time: 61.6 us -> 67.5 us (1.096)
  blocking collectives: 0 us -> 40.2 us
  starting transfers between devices: 36.5 us -> 15.6 us
  waiting for transfers between devices: 14.7 us -> 1.59 us
  Pallas kernels: 9.13 us -> 7.96 us
  local copies, waits for them, and re-layouts: 0.02 us -> 0.99 us
    all_to_all x0 -> x2, blocking collectives: none -> 40.2 us  [everyones(): lax.all_to_all(rows.reshape(count, 1, Y), axis, 0, 0).reshape(count, Y)]
    all_to_all x2 -> x0, starting transfers between devices: 22.4 us -> none  [everyones(): lax.all_to_all(rows.reshape(count, 1, Y), axis, 0, 0).reshape(count, Y)]
    all_to_all x2 -> x0, waiting for transfers between devices: 8.89 us -> none  [everyones(): lax.all_to_all(rows.reshape(count, 1, Y), axis, 0, 0).reshape(count, Y)]
    ppermute x2, waiting for transfers between devices: 5.06 us -> 0.81 us  [back(): lax.ppermute(x, axis, [(i + 1, i) for i in range(lax.axis_size(axis) - 1)])]
    ppermute x2, starting transfers between devices: 8.18 us -> 9.65 us  [ahead(): lax.ppermute(x, axis, [(i, i + 1) for i in range(lax.axis_size(axis) - 1)])]
    unnamed x12, local copies, waits for them, and re-layouts: 0.02 us -> 0.99 us
  transfers between devices with their start and end apart: 6 -> 4, of which waited for: 5 -> 2; matrix products, arithmetic and copies ran while one was open for 0% -> 0% of each run, Pallas kernels for 6% -> 5%
where the time goes in v3:
time: 67.5 us; the launch traced here: 67.1 us
  blocking collectives  40.2 us (60%)
  starting transfers between devices  15.6 us (23%)
  Pallas kernels  7.96 us (12%)
  waiting for transfers between devices  1.59 us (2%)
  local copies, waits for them, and re-layouts  0.99 us (1%)
  between operations  0.77 us (1%)
    all_to_all x2, blocking collectives, everyones(): lax.all_to_all(rows.reshape(count, 1, Y), axis, 0, 0).reshape(count, Y)  40.2 us
    ppermute x2, starting transfers between devices, ahead(): lax.ppermute(x, axis, [(i, i + 1) for i in range(lax.axis_size(axis) - 1)])  9.65 us
    ppermute x2, starting transfers between devices, back(): lax.ppermute(x, axis, [(i + 1, i) for i in range(lax.axis_size(axis) - 1)])  5.98 us
    pallas_call x1, Pallas kernels, on_device(): call(soil_kernel, [tall] * 3, [pltpu.VMEM((PAD, CLASSES * PAD), F32), plt...  3.51 us
    pallas_call x1, Pallas kernels, on_device(): call(krylov_kernel, [block, block, (lax.axis_size('gx'), Y), (16, Y)], [p...  1.47 us
    pallas_call x1, Pallas kernels, on_device(): call(local_kernel, [block, block, (FIELDS, E - X, Y), plane, plane], [(pl...  1.45 us
  transfers between devices with their start and end apart: 4, of which 2 were waited for; matrix products, arithmetic and copies ran while one was open for 0% of the time, Pallas kernels for 5%

profile of v3, /device:TPU:1, one launch (start us, length us, event | category | flops | bytes accessed | tf_op | source)
XLA Modules:
  0.0 67.1 jit_solution(6996817400487186920)
XLA Ops:
  0.6 0.0 copy-start.3
  0.6 0.0 copy-start.2
  0.7 0.0 copy-start.5
  0.7 1.5 %shard_map.157 = (f32[5,32,128]{2,1,0:T(8,128)S(1)}, f32[5,32,128]{2,1,0:T(8,128)S(1)}, f32[15,8,128]{2,1,0:T(8,128)S(1)}, f32[32,128]{1,0:T(8,128)S(1)}, f32[32,128]{1,0:T(8,128)S(1)}) custom-call(f32[5,32,128]{2,1,0:T(8,128)} %refs_0_.1, f32[5,32,128]{2,1,0:T(8,128)} %rhs.5, s32[5,32,128]{2,1,0:T(8,128)} %refs_2_.1, f32[16]{0:T(128)} %refs_3_.1, ...), custom_call_target="tpu_custom_call" | custom-call | tf_op jit(solution)/shard_map/pallas_call | solution.py:387
  2.1 1.3 %collective-permute-start = (f32[15,8,128]{2,1,0:T(8,128)S(1)}, f32[15,8,128]{2,1,0:T(8,128)S(1)}, u32[]{:S(2)}, u32[]{:S(2)}) collective-permute-start(f32[15,8,128]{2,1,0:T(8,128)S(1)} %get-tuple-element.23), channel_id=1, source_target_pairs={{16,0},{32,16},{48,32},{64,48},{80,64},{96,80},{112,96},{128,112},... | collective-permute-start | bytes 184328 | tf_op jit(solution)/shard_map/ppermute | solution.py:368
  3.4 0.0 copy-done.3
  3.4 0.0 copy-done.2
  3.4 0.0 copy-done.5
  3.5 0.0 copy-start.1
  3.5 1.0 %copy-done.1 = f32[20,32,128]{2,1,0:T(8,128)S(1)} copy-done((f32[20,32,128]{2,1,0:T(8,128)S(1)}, f32[20,32,128]{2,1,0:T(8,128)}, u32[]{:S(2)}) %copy-start.1) | copy-done | bytes 327704
  4.4 0.0 copy-start
  4.4 3.5 %shard_map.158 = (f32[640,128]{1,0:T(8,128)S(1)}, f32[640,128]{1,0:T(8,128)S(1)}, f32[640,128]{1,0:T(8,128)S(1)}) custom-call(f32[640,128]{1,0:T(8,128)S(1)} %bitcast.9, s32[32,128]{1,0:T(8,128)S(1)} %copy-done.5, s32[32,128]{1,0:T(8,128)S(1)} %copy-done.3, f32[12,20,20]{2,1,0:T(8,128)S(1)} %copy-done.2), custom_call_target="tpu_custom_call" | custom-call | flops 20000000 | bytes 2000000 | tf_op jit(solution)/shard_map/pallas_call | solution.py:395
  7.9 0.0 collective-permute-done.after
  8.0 0.0 copy-done
  8.0 0.1 shard_map.159
  8.1 5.7 %collective-permute-start.2 = (f32[40,128]{1,0:T(8,128)S(1)}, f32[40,128]{1,0:T(8,128)S(1)}, u32[]{:S(2)}, u32[]{:S(2)}) collective-permute-start(f32[40,128]{1,0:T(8,128)S(1)} %shard_map.159), channel_id=1, source_target_pairs={{0,1},{1,2},{2,3},{3,4},{4,5},{5,6},{6,7},{7,8},{8,9},{9,10},{10,1... | collective-permute-start | bytes 61448 | tf_op jit(solution)/shard_map/ppermute | solution.py:364
  13.8 4.7 %collective-permute-start.1 = (f32[40,128]{1,0:T(8,128)S(1)}, f32[40,128]{1,0:T(8,128)S(1)}, u32[]{:S(2)}, u32[]{:S(2)}) collective-permute-start(f32[40,128]{1,0:T(8,128)S(1)} %shard_map.159), channel_id=1, source_target_pairs={{1,0},{2,1},{3,2},{4,3},{5,4},{6,5},{7,6},{8,7},{9,8},{10,9},{11,1... | collective-permute-start | bytes 61448 | tf_op jit(solution)/shard_map/ppermute | solution.py:368
  18.5 0.0 collective-permute-done.2.left
  18.5 0.8 %collective-permute-done.1.right = f32[40,128]{1,0:T(8,128)S(1)} collective-permute-done((f32[40,128]{1,0:T(8,128)S(1)}, f32[40,128]{1,0:T(8,128)S(1)}, u32[]{:S(2)}, u32[]{:S(2)}) %collective-permute-start.1) | collective-permute-done | bytes 20512 | tf_op jit(solution)/shard_map/ppermute | solution.py:368
  19.3 1.5 %shard_map.160 = (f32[5,32,128]{2,1,0:T(8,128)S(1)}, f32[5,32,128]{2,1,0:T(8,128)S(1)}, f32[32,128]{1,0:T(8,128)S(1)}, f32[16,128]{1,0:T(8,128)S(1)}) custom-call(f32[5,32,128]{2,1,0:T(8,128)S(1)} %copy-done, f32[5,32,128]{2,1,0:T(8,128)S(1)} %get-tuple-element.21.cond, f32[5,32,128]{2,1,0:T(8,128)S(1)} %get-tuple-element.22.diag, ...), custom_call_target="tpu_custom_call" | custom-call | tf_op jit(solution)/shard_map/pallas_call | solution.py:405
  20.8 4.0 %collective-permute-start.3 = (f32[16,128]{1,0:T(8,128)S(1)}, f32[16,128]{1,0:T(8,128)S(1)}, u32[]{:S(2)}, u32[]{:S(2)}) collective-permute-start(f32[16,128]{1,0:T(8,128)S(1)} %get-tuple-element.31), channel_id=1, source_target_pairs={{0,16},{16,32},{32,48},{48,64},{64,80},{80,96},{96,112},{112,128},... | collective-permute-start | bytes 24584 | tf_op jit(solution)/shard_map/ppermute | solution.py:364
  24.8 0.8 %collective-permute-done.3.back = f32[16,128]{1,0:T(8,128)S(1)} collective-permute-done((f32[16,128]{1,0:T(8,128)S(1)}, f32[16,128]{1,0:T(8,128)S(1)}, u32[]{:S(2)}, u32[]{:S(2)}) %collective-permute-start.3) | collective-permute-done | bytes 8224 | tf_op jit(solution)/shard_map/ppermute | solution.py:364
  25.5 21.2 %all_to_all.10 = f32[32,1,128]{2,1,0:T(1,128)S(1)} all-to-all(f32[32,1,128]{2,1,0:T(1,128)S(1)} %bitcast.13), channel_id=1, replica_groups=mesh['gx'=32,'gy'=16] {'gx'}, dimensions={0} | all-to-all | bytes 32768 | tf_op jit(solution)/shard_map/all_to_all | solution.py:373
  46.7 0.2 shard_map.161
  46.9 0.0 copy-start.4
  46.9 19.0 %all_to_all.11 = f32[16,1,128]{2,1,0:T(1,128)S(1)} all-to-all(f32[16,1,128]{2,1,0:T(1,128)S(1)} %bitcast.11), channel_id=1, replica_groups=mesh['gx'=32,'gy'=16] {'gy'}, dimensions={0} | all-to-all | bytes 16384 | tf_op jit(solution)/shard_map/all_to_all | solution.py:373
  65.9 0.0 copy-done.4
  65.9 1.2 %shard_map.162 = (f32[5,32,128]{2,1,0:T(8,128)}, f32[32,128]{1,0:T(8,128)}, f32[20,32,128]{2,1,0:T(8,128)}) custom-call(f32[16,128]{1,0:T(8,128)S(1)} %bitcast.12, f32[5,32,128]{2,1,0:T(8,128)S(1)} %copy-done, f32[5,32,128]{2,1,0:T(8,128)S(1)} %get-tuple-element.33.v1, f32[5,32,128]{2,1,0:T(8,128)S(1)} %get-tuple-element.34.v2, ...), custom_call_target="tpu_custom_call" | custom-call | tf_op jit(solution)/shard_map/pallas_call | solution.py:415
Async XLA Ops:
  0.6 2.8 %copy-start.3 = (s32[32,128]{1,0:T(8,128)S(1)}, s32[32,128]{1,0:T(8,128)}, u32[]{:S(2)}) copy-start(s32[32,128]{1,0:T(8,128)} %land.3) | copy-start | bytes 49156
  0.6 2.8 %copy-start.2 = (f32[12,20,20]{2,1,0:T(8,128)S(1)}, f32[12,20,20]{2,1,0:T(8,128)}, u32[]{:S(2)}) copy-start(f32[12,20,20]{2,1,0:T(8,128)} %inverse.1) | copy-start | bytes 57604
  0.7 2.8 %copy-start.5 = (s32[32,128]{1,0:T(8,128)S(1)}, s32[32,128]{1,0:T(8,128)}, u32[]{:S(2)}) copy-start(s32[32,128]{1,0:T(8,128)} %soil_class.1) | copy-start | bytes 49156
  2.1 5.8 %collective-permute-start = (f32[15,8,128]{2,1,0:T(8,128)S(1)}, f32[15,8,128]{2,1,0:T(8,128)S(1)}, u32[]{:S(2)}, u32[]{:S(2)}) collective-permute-start(f32[15,8,128]{2,1,0:T(8,128)S(1)} %get-tuple-element.23), channel_id=1, source_target_pairs={{16,0},{32,16},{48,32},{64,48},{80,64},{96,80},{112,96},{128,112},... | collective-permute-start | bytes 184328 | tf_op jit(solution)/shard_map/ppermute | solution.py:368
  3.5 1.0 %copy-start.1 = (f32[20,32,128]{2,1,0:T(8,128)S(1)}, f32[20,32,128]{2,1,0:T(8,128)}, u32[]{:S(2)}) copy-start(f32[20,32,128]{2,1,0:T(8,128)} %param.27) | copy-start | bytes 983044
  4.4 3.5 %copy-start = (f32[5,32,128]{2,1,0:T(8,128)S(1)}, f32[5,32,128]{2,1,0:T(8,128)}, u32[]{:S(2)}) copy-start(f32[5,32,128]{2,1,0:T(8,128)} %rhs.5) | copy-start | bytes 245764
  8.1 10.4 %collective-permute-start.2 = (f32[40,128]{1,0:T(8,128)S(1)}, f32[40,128]{1,0:T(8,128)S(1)}, u32[]{:S(2)}, u32[]{:S(2)}) collective-permute-start(f32[40,128]{1,0:T(8,128)S(1)} %shard_map.159), channel_id=1, source_target_pairs={{0,1},{1,2},{2,3},{3,4},{4,5},{5,6},{6,7},{7,8},{8,9},{9,10},{10,1... | collective-permute-start | bytes 61448 | tf_op jit(solution)/shard_map/ppermute | solution.py:364
  13.8 5.5 %collective-permute-start.1 = (f32[40,128]{1,0:T(8,128)S(1)}, f32[40,128]{1,0:T(8,128)S(1)}, u32[]{:S(2)}, u32[]{:S(2)}) collective-permute-start(f32[40,128]{1,0:T(8,128)S(1)} %shard_map.159), channel_id=1, source_target_pairs={{1,0},{2,1},{3,2},{4,3},{5,4},{6,5},{7,6},{8,7},{9,8},{10,9},{11,1... | collective-permute-start | bytes 61448 | tf_op jit(solution)/shard_map/ppermute | solution.py:368
  20.8 4.8 %collective-permute-start.3 = (f32[16,128]{1,0:T(8,128)S(1)}, f32[16,128]{1,0:T(8,128)S(1)}, u32[]{:S(2)}, u32[]{:S(2)}) collective-permute-start(f32[16,128]{1,0:T(8,128)S(1)} %get-tuple-element.31), channel_id=1, source_target_pairs={{0,16},{16,32},{32,48},{48,64},{64,80},{80,96},{96,112},{112,128},... | collective-permute-start | bytes 24584 | tf_op jit(solution)/shard_map/ppermute | solution.py:364
  46.9 19.0 %copy-start.4 = (f32[32,128]{1,0:T(8,128)S(1)}, f32[32,128]{1,0:T(8,128)}, u32[]{:S(2)}) copy-start(f32[32,128]{1,0:T(8,128)} %ponding.1) | copy-start | bytes 49156

commit v4 on v3

--- a/solution.py
+++ b/solution.py
@@ -269,7 +269,11 @@
         row_out[i : i + 8, :] = both
 
 
-def soil_kernel(state, soil_class, land, inverse, base, water, head, w, w01):
+def soil_kernel(
+    state_hbm, soil_class, land, inverse, base, water, head, w, w01, state, sem
+):
+    copy = pltpu.make_async_copy(state_hbm, state, sem)
+    copy.start()
     w[...] = jnp.zeros(w.shape, F32)
     w01[...] = jnp.zeros(w01.shape, F32)
     for e in range(CLASSES):
@@ -278,6 +282,7 @@
         w01[0:STATE, e : e + 1] = x[:, 0:1]
         w01[PAD : PAD + STATE, e : e + 1] = x[:, 1:2]
     w_all, w_two = w[...], w01[...]
+    copy.wait()
     zero = jnp.zeros((PAD - STATE, Y), F32)
     entry = iota((16, Y), 0)
 
@@ -395,10 +400,19 @@
     base, water, head = call(
         soil_kernel,
         [tall] * 3,
-        [pltpu.VMEM((PAD, CLASSES * PAD), F32), pltpu.VMEM((2 * PAD, 16), F32)],
+        [
+            pltpu.VMEM((PAD, CLASSES * PAD), F32),
+            pltpu.VMEM((2 * PAD, 16), F32),
+            pltpu.VMEM(tall, F32),
+            pltpu.SemaphoreType.DMA,
+        ],
+        [pl.BlockSpec(memory_space=pltpu.HBM)] + [pl.BlockSpec()] * 3,
         flops=20_000_000,
         nbytes=2_000_000,
-    )(soil_state.reshape(tall), soil_class, land_mask, soil_inverse)
+    )(
+        pltpu.with_memory_space_constraint(soil_state.reshape(tall), pltpu.HBM),
+        soil_class, land_mask, soil_inverse,
+    )
     after, base, water, head = lax.optimization_barrier((after, base, water, head))
     (packed,) = call(pack_kernel, [(E, Y)])(newton_rhs, cond, diag, after, south)
     left, right = ahead(packed, "gy"), back(packed, "gy")
@@ -408,7 +422,6 @@
         [pltpu.VMEM((2, n, E, Y), F32) for n in (5, 5, 4, 5, 5)],
     )(newton_rhs, cond, diag, after, right, left, east)
     edge = ahead(edge, "gx")
-    rows, edge = lax.optimization_barrier((rows, edge))
     rows = everyones(rows, "gx")
     (rows,) = call(relay_kernel, [(lax.axis_size("gy"), Y)])(rows)
     rows = everyones(rows, "gy")

time: 67.5 us -> 60.6 us (0.90)
  blocking collectives: 40.2 us -> 19.5 us
  starting transfers between devices: 15.6 us -> 24.9 us
  waiting for transfers between devices: 1.59 us -> 5.53 us
  Pallas kernels: 7.96 us -> 9.6 us
  local copies, waits for them, and re-layouts: 0.99 us -> 0.02 us
    all_to_all x2 -> x1, blocking collectives: 40.2 us -> 19.5 us  [everyones(): lax.all_to_all(rows.reshape(count, 1, Y), axis, 0, 0).reshape(count, Y)]
    all_to_all x0 -> x1, starting transfers between devices: none -> 11.1 us  [everyones(): lax.all_to_all(rows.reshape(count, 1, Y), axis, 0, 0).reshape(count, Y)]
    all_to_all x0 -> x1, waiting for transfers between devices: none -> 3.93 us  [everyones(): lax.all_to_all(rows.reshape(count, 1, Y), axis, 0, 0).reshape(count, Y)]
    ppermute x2, starting transfers between devices: 9.65 us -> 7.79 us  [ahead(): lax.ppermute(x, axis, [(i, i + 1) for i in range(lax.axis_size(axis) - 1)])]
    pallas_call x1, Pallas kernels: 3.51 us -> 4.57 us  [on_device(): call(soil_kernel, [tall] * 3, [pltpu.VMEM((PAD, CLASSES * PAD), F32), plt...]
    unnamed x12 -> x10, local copies, waits for them, and re-layouts: 0.99 us -> 0.02 us
  transfers between devices with their start and end apart: 4 -> 5, of which waited for: 2 -> 3; matrix products, arithmetic and copies ran while one was open for 0% -> 0% of each run, Pallas kernels for 5% -> 8%
where the time goes in v4:
time: 60.6 us; the launch traced here: 60.3 us
  starting transfers between devices  24.9 us (41%)
  blocking collectives  19.5 us (32%)
  Pallas kernels  9.6 us (16%)
  waiting for transfers between devices  5.53 us (9%)
  between operations  0.77 us (1%)
    all_to_all x1, blocking collectives, everyones(): lax.all_to_all(rows.reshape(count, 1, Y), axis, 0, 0).reshape(count, Y)  19.5 us
    all_to_all x1, starting transfers between devices, everyones(): lax.all_to_all(rows.reshape(count, 1, Y), axis, 0, 0).reshape(count, Y)  11.1 us
    ppermute x2, starting transfers between devices, ahead(): lax.ppermute(x, axis, [(i, i + 1) for i in range(lax.axis_size(axis) - 1)])  7.79 us
    ppermute x2, starting transfers between devices, back(): lax.ppermute(x, axis, [(i + 1, i) for i in range(lax.axis_size(axis) - 1)])  5.98 us
    pallas_call x1, Pallas kernels, on_device(): call(soil_kernel, [tall] * 3, [pltpu.VMEM((PAD, CLASSES * PAD), F32), plt...  4.57 us
    all_to_all x1, waiting for transfers between devices, everyones(): lax.all_to_all(rows.reshape(count, 1, Y), axis, 0, 0).reshape(count, Y)  3.93 us
    pallas_call x1, Pallas kernels, on_device(): call(krylov_kernel, [block, block, (lax.axis_size('gx'), Y), (16, Y)], [p...  1.46 us
    pallas_call x1, Pallas kernels, on_device(): call(local_kernel, [block, block, (FIELDS, E - X, Y), plane, plane], [(pl...  1.45 us
  transfers between devices with their start and end apart: 5, of which 3 were waited for; matrix products, arithmetic and copies ran while one was open for 0% of the time, Pallas kernels for 8%

profile of v4, /device:TPU:1, one launch (start us, length us, event | category | flops | bytes accessed | tf_op | source)
XLA Modules:
  0.0 60.3 jit_solution(6116577560898944239)
XLA Ops:
  0.6 0.0 copy-start.2
  0.6 0.0 copy-start.1
  0.7 0.0 copy-start.4
  0.7 1.5 %shard_map.157 = (f32[5,32,128]{2,1,0:T(8,128)S(1)}, f32[5,32,128]{2,1,0:T(8,128)S(1)}, f32[15,8,128]{2,1,0:T(8,128)S(1)}, f32[32,128]{1,0:T(8,128)S(1)}, f32[32,128]{1,0:T(8,128)S(1)}) custom-call(f32[5,32,128]{2,1,0:T(8,128)} %refs_0_.1, f32[5,32,128]{2,1,0:T(8,128)} %rhs.5, s32[5,32,128]{2,1,0:T(8,128)} %refs_2_.1, f32[16]{0:T(128)} %refs_3_.1, ...), custom_call_target="tpu_custom_call" | custom-call | tf_op jit(solution)/shard_map/pallas_call | solution.py:392
  2.1 1.3 %collective-permute-start = (f32[15,8,128]{2,1,0:T(8,128)S(1)}, f32[15,8,128]{2,1,0:T(8,128)S(1)}, u32[]{:S(2)}, u32[]{:S(2)}) collective-permute-start(f32[15,8,128]{2,1,0:T(8,128)S(1)} %get-tuple-element.21), channel_id=1, source_target_pairs={{16,0},{32,16},{48,32},{64,48},{80,64},{96,80},{112,96},{128,112},... | collective-permute-start | bytes 184328 | tf_op jit(solution)/shard_map/ppermute | solution.py:373
  3.4 0.0 copy-done.2
  3.4 0.0 copy-done.1
  3.4 0.0 copy-done.4
  3.5 0.0 copy-start
  3.5 4.6 %shard_map.158 = (f32[640,128]{1,0:T(8,128)S(1)}, f32[640,128]{1,0:T(8,128)S(1)}, f32[640,128]{1,0:T(8,128)S(1)}) custom-call(f32[640,128]{1,0:T(8,128)} %bitcast.12, s32[32,128]{1,0:T(8,128)S(1)} %copy-done.4, s32[32,128]{1,0:T(8,128)S(1)} %copy-done.2, f32[12,20,20]{2,1,0:T(8,128)S(1)} %copy-done.1), custom_call_target="tpu_custom_call" | custom-call | flops 20000000 | bytes 2000000 | tf_op jit(solution)/shard_map/pallas_call | solution.py:400
  8.0 0.0 collective-permute-done.after
  8.1 0.0 copy-done
  8.1 0.1 shard_map.159
  8.2 5.6 %collective-permute-start.2 = (f32[40,128]{1,0:T(8,128)S(1)}, f32[40,128]{1,0:T(8,128)S(1)}, u32[]{:S(2)}, u32[]{:S(2)}) collective-permute-start(f32[40,128]{1,0:T(8,128)S(1)} %shard_map.159), channel_id=1, source_target_pairs={{0,1},{1,2},{2,3},{3,4},{4,5},{5,6},{6,7},{7,8},{8,9},{9,10},{10,1... | collective-permute-start | bytes 61448 | tf_op jit(solution)/shard_map/ppermute | solution.py:369
  13.8 4.7 %collective-permute-start.1 = (f32[40,128]{1,0:T(8,128)S(1)}, f32[40,128]{1,0:T(8,128)S(1)}, u32[]{:S(2)}, u32[]{:S(2)}) collective-permute-start(f32[40,128]{1,0:T(8,128)S(1)} %shard_map.159), channel_id=1, source_target_pairs={{1,0},{2,1},{3,2},{4,3},{5,4},{6,5},{7,6},{8,7},{9,8},{10,9},{11,1... | collective-permute-start | bytes 61448 | tf_op jit(solution)/shard_map/ppermute | solution.py:373
  18.5 0.0 collective-permute-done.2.left
  18.5 0.8 %collective-permute-done.1.right = f32[40,128]{1,0:T(8,128)S(1)} collective-permute-done((f32[40,128]{1,0:T(8,128)S(1)}, f32[40,128]{1,0:T(8,128)S(1)}, u32[]{:S(2)}, u32[]{:S(2)}) %collective-permute-start.1) | collective-permute-done | bytes 20512 | tf_op jit(solution)/shard_map/ppermute | solution.py:373
  19.3 1.5 %shard_map.160 = (f32[5,32,128]{2,1,0:T(8,128)S(1)}, f32[5,32,128]{2,1,0:T(8,128)S(1)}, f32[32,128]{1,0:T(8,128)S(1)}, f32[16,128]{1,0:T(8,128)S(1)}) custom-call(f32[5,32,128]{2,1,0:T(8,128)S(1)} %copy-done, f32[5,32,128]{2,1,0:T(8,128)S(1)} %get-tuple-element.19.cond, f32[5,32,128]{2,1,0:T(8,128)S(1)} %get-tuple-element.20.diag, ...), custom_call_target="tpu_custom_call" | custom-call | tf_op jit(solution)/shard_map/pallas_call | solution.py:419
  20.8 19.5 %all_to_all.10 = f32[32,1,128]{2,1,0:T(1,128)S(1)} all-to-all(f32[32,1,128]{2,1,0:T(1,128)S(1)} %bitcast.11), channel_id=1, replica_groups=mesh['gx'=32,'gy'=16] {'gx'}, dimensions={0} | all-to-all | bytes 32768 | tf_op jit(solution)/shard_map/all_to_all | solution.py:378
  40.2 0.8 %shard_map.161 = f32[16,128]{1,0:T(8,128)} custom-call(f32[32,128]{1,0:T(8,128)S(1)} %bitcast.9), custom_call_target="tpu_custom_call" | custom-call | tf_op jit(solution)/shard_map/pallas_call | solution.py:426
  41.0 0.0 copy-start.3
  41.0 11.1 %all-to-all-start.1 = ((f32[16,1,128]{2,1,0:T(1,128)}), f32[16,1,128]{2,1,0:T(1,128)S(1)}, u32[]{:S(2)}, u32[]{:S(2)}) async-start(f32[16,1,128]{2,1,0:T(1,128)} %bitcast.5), calls=%async_computation.1 | async-start | bytes 16384 | tf_op jit(solution)/shard_map/all_to_all | solution.py:378
  52.1 2.2 %collective-permute-start.3 = (f32[16,128]{1,0:T(8,128)S(1)}, f32[16,128]{1,0:T(8,128)S(1)}, u32[]{:S(2)}, u32[]{:S(2)}) collective-permute-start(f32[16,128]{1,0:T(8,128)S(1)} %get-tuple-element.31), channel_id=1, source_target_pairs={{0,16},{16,32},{32,48},{48,64},{64,80},{80,96},{96,112},{112,128},... | collective-permute-start | bytes 24584 | tf_op jit(solution)/shard_map/ppermute | solution.py:369
  54.4 0.8 %collective-permute-done.3.back = f32[16,128]{1,0:T(8,128)S(1)} collective-permute-done((f32[16,128]{1,0:T(8,128)S(1)}, f32[16,128]{1,0:T(8,128)S(1)}, u32[]{:S(2)}, u32[]{:S(2)}) %collective-permute-start.3) | collective-permute-done | bytes 8224 | tf_op jit(solution)/shard_map/ppermute | solution.py:369
  55.1 3.9 %all-to-all-done.1 = f32[16,1,128]{2,1,0:T(1,128)S(1)} async-done(((f32[16,1,128]{2,1,0:T(1,128)}), f32[16,1,128]{2,1,0:T(1,128)S(1)}, u32[]{:S(2)}, u32[]{:S(2)}) %all-to-all-start.1) | async-done | bytes 8224 | tf_op jit(solution)/shard_map/all_to_all | solution.py:378
  59.1 0.0 copy-done.3
  59.1 1.2 %shard_map.162 = (f32[5,32,128]{2,1,0:T(8,128)}, f32[32,128]{1,0:T(8,128)}, f32[20,32,128]{2,1,0:T(8,128)}) custom-call(f32[16,128]{1,0:T(8,128)S(1)} %bitcast.10, f32[5,32,128]{2,1,0:T(8,128)S(1)} %copy-done, f32[5,32,128]{2,1,0:T(8,128)S(1)} %get-tuple-element.29.v1, f32[5,32,128]{2,1,0:T(8,128)S(1)} %get-tuple-element.30.v2, ...), custom_call_target="tpu_custom_call" | custom-call | tf_op jit(solution)/shard_map/pallas_call | solution.py:428
Async XLA Ops:
  0.6 2.8 %copy-start.2 = (s32[32,128]{1,0:T(8,128)S(1)}, s32[32,128]{1,0:T(8,128)}, u32[]{:S(2)}) copy-start(s32[32,128]{1,0:T(8,128)} %land.3) | copy-start | bytes 49156
  0.6 2.8 %copy-start.1 = (f32[12,20,20]{2,1,0:T(8,128)S(1)}, f32[12,20,20]{2,1,0:T(8,128)}, u32[]{:S(2)}) copy-start(f32[12,20,20]{2,1,0:T(8,128)} %inverse.1) | copy-start | bytes 57604
  0.7 2.8 %copy-start.4 = (s32[32,128]{1,0:T(8,128)S(1)}, s32[32,128]{1,0:T(8,128)}, u32[]{:S(2)}) copy-start(s32[32,128]{1,0:T(8,128)} %soil_class.1) | copy-start | bytes 49156
  2.1 5.9 %collective-permute-start = (f32[15,8,128]{2,1,0:T(8,128)S(1)}, f32[15,8,128]{2,1,0:T(8,128)S(1)}, u32[]{:S(2)}, u32[]{:S(2)}) collective-permute-start(f32[15,8,128]{2,1,0:T(8,128)S(1)} %get-tuple-element.21), channel_id=1, source_target_pairs={{16,0},{32,16},{48,32},{64,48},{80,64},{96,80},{112,96},{128,112},... | collective-permute-start | bytes 184328 | tf_op jit(solution)/shard_map/ppermute | solution.py:373
  3.5 4.6 %copy-start = (f32[5,32,128]{2,1,0:T(8,128)S(1)}, f32[5,32,128]{2,1,0:T(8,128)}, u32[]{:S(2)}) copy-start(f32[5,32,128]{2,1,0:T(8,128)} %rhs.5) | copy-start | bytes 245764
  8.2 10.3 %collective-permute-start.2 = (f32[40,128]{1,0:T(8,128)S(1)}, f32[40,128]{1,0:T(8,128)S(1)}, u32[]{:S(2)}, u32[]{:S(2)}) collective-permute-start(f32[40,128]{1,0:T(8,128)S(1)} %shard_map.159), channel_id=1, source_target_pairs={{0,1},{1,2},{2,3},{3,4},{4,5},{5,6},{6,7},{7,8},{8,9},{9,10},{10,1... | collective-permute-start | bytes 61448 | tf_op jit(solution)/shard_map/ppermute | solution.py:369
  13.8 5.5 %collective-permute-start.1 = (f32[40,128]{1,0:T(8,128)S(1)}, f32[40,128]{1,0:T(8,128)S(1)}, u32[]{:S(2)}, u32[]{:S(2)}) collective-permute-start(f32[40,128]{1,0:T(8,128)S(1)} %shard_map.159), channel_id=1, source_target_pairs={{1,0},{2,1},{3,2},{4,3},{5,4},{6,5},{7,6},{8,7},{9,8},{10,9},{11,1... | collective-permute-start | bytes 61448 | tf_op jit(solution)/shard_map/ppermute | solution.py:373
  41.0 18.1 %copy-start.3 = (f32[32,128]{1,0:T(8,128)S(1)}, f32[32,128]{1,0:T(8,128)}, u32[]{:S(2)}) copy-start(f32[32,128]{1,0:T(8,128)} %ponding.1) | copy-start | bytes 49156
  41.0 18.1 %all-to-all-start.1 = ((f32[16,1,128]{2,1,0:T(1,128)}), f32[16,1,128]{2,1,0:T(1,128)S(1)}, u32[]{:S(2)}, u32[]{:S(2)}) async-start(f32[16,1,128]{2,1,0:T(1,128)} %bitcast.5), calls=%async_computation.1 | async-start | bytes 16384 | tf_op jit(solution)/shard_map/all_to_all | solution.py:378
  52.1 3.0 %collective-permute-start.3 = (f32[16,128]{1,0:T(8,128)S(1)}, f32[16,128]{1,0:T(8,128)S(1)}, u32[]{:S(2)}, u32[]{:S(2)}) collective-permute-start(f32[16,128]{1,0:T(8,128)S(1)} %get-tuple-element.31), channel_id=1, source_target_pairs={{0,16},{16,32},{32,48},{48,64},{64,80},{80,96},{96,112},{112,128},... | collective-permute-start | bytes 24584 | tf_op jit(solution)/shard_map/ppermute | solution.py:369

commit v5 on v4

--- a/solution.py
+++ b/solution.py
@@ -151,6 +151,13 @@
 ):
     lane, row_of = iota((E, Y), 1), iota((E, Y), 0)
     first, last = lane == 0, lane == Y - 1
+    x, y = lax.axis_index("gx"), lax.axis_index("gy")
+    x_end, y_end = x == lax.axis_size("gx") - 1, y == lax.axis_size("gy") - 1
+    closed_rows = (row_of == 0) | (row_of == jnp.where(x_end, X, 0))
+    closed_lanes = (
+        lane == jnp.where(y == 0, 0, -1),
+        lane == jnp.where(y_end, 0, -1),
+    )
 
     def turn(m, h, by, edge):
         m, h = pltpu.roll(m, by, 1), pltpu.roll(h, by, 1)
@@ -175,8 +182,10 @@
         dd[0, l], dd[1, l] = both(diag, 2, l)
         west = turn(*k, 1, first)
         for s in range(2):
-            fr[s, l] = jnp.where(row_of == 0, 0.0, harmonic(k[s], pltpu.roll(k[s], 1, 0)))
-            fc[s, l] = harmonic(k[s], west[s])
+            fr[s, l] = jnp.where(
+                closed_rows, 0.0, harmonic(k[s], pltpu.roll(k[s], 1, 0))
+            )
+            fc[s, l] = jnp.where(closed_lanes[s], 0.0, harmonic(k[s], west[s]))
             if l:
                 fv[s, l - 1] = harmonic(k[s], above[s])
         above = k
@@ -202,7 +211,7 @@
     zero = jnp.zeros((8, Y), F32)
     sums = [(zero, zero)] * 6
     sub = iota((8, Y), 0)
-    start = jnp.where(lax.axis_index("gx") == 0, 0, W)
+    start, stop = jnp.where(x == 0, 0, W), jnp.where(x_end, 0, W)
 
     def add_to(j, a, b):
         p, e = two_prod(a, b)
@@ -217,7 +226,7 @@
             for i in range(0, E, 8):
                 a, b = old[i : i + 8], new[i : i + 8]
                 if i == 0 or i == X:
-                    keep = sub >= start if i == 0 else sub < W
+                    keep = sub >= start if i == 0 else sub < stop
                     a, b = jnp.where(keep, a, 0.0), jnp.where(keep, b, 0.0)
                 add_to(2 * step, a, a)
                 add_to(2 * step + 1, a, b)
@@ -344,13 +353,15 @@
     row, lane = iota((X, Y), 0), iota((X, Y), 1)
     es, so = east[...], south[...]
     north = pltpu.roll(left[0:X, :], (-(W + G * FIELDS)) % Y, 1)
-    inflow = jnp.where(
-        row == 0, back[3 * LAYERS : 3 * LAYERS + 1, :], pltpu.roll(es, 1, 0)
-    ) + jnp.where(lane == 0, pltpu.roll(north, 1, 1), pltpu.roll(so, 1, 1))
+    given = jnp.where(lax.axis_index("gx") == 0, 0, 1)
+    west = jnp.where(given == 0, 0.0, back[3 * LAYERS : 3 * LAYERS + 1, :])
+    north = jnp.where(lax.axis_index("gy") == 0, 0.0, pltpu.roll(north, 1, 1))
+    inflow = jnp.where(row == 0, west, pltpu.roll(es, 1, 0)) + jnp.where(
+        lane == 0, north, pltpu.roll(so, 1, 1)
+    )
     pond = land[...].astype(F32) * (ponding[...] + 0.2 * (inflow - (es + so)))
     pond_out[...] = pond
 
-    given = jnp.where(lax.axis_index("gx") == 0, 0, 1)
     top = None
     for l in range(LAYERS):
         q = LAYERS + 2 * l
@@ -366,11 +377,13 @@
 
 
 def ahead(x, axis):
-    return lax.ppermute(x, axis, [(i, i + 1) for i in range(lax.axis_size(axis) - 1)])
+    n = lax.axis_size(axis)
+    return lax.ppermute(x, axis, [(i, (i + 1) % n) for i in range(n)])
 
 
 def back(x, axis):
-    return lax.ppermute(x, axis, [(i + 1, i) for i in range(lax.axis_size(axis) - 1)])
+    n = lax.axis_size(axis)
+    return lax.ppermute(x, axis, [((i + 1) % n, i) for i in range(n)])
 
 
 def everyones(rows, axis):
@@ -418,13 +431,13 @@
     left, right = ahead(packed, "gy"), back(packed, "gy")
     v1, v2, rows, edge = call(
         krylov_kernel,
-        [block, block, (lax.axis_size("gx"), Y), (16, Y)],
+        [block, block, (lax.axis_size("gy"), Y), (16, Y)],
         [pltpu.VMEM((2, n, E, Y), F32) for n in (5, 5, 4, 5, 5)],
     )(newton_rhs, cond, diag, after, right, left, east)
     edge = ahead(edge, "gx")
+    rows = everyones(rows, "gy")
+    (rows,) = call(relay_kernel, [(lax.axis_size("gx"), Y)])(rows)
     rows = everyones(rows, "gx")
-    (rows,) = call(relay_kernel, [(lax.axis_size("gy"), Y)])(rows)
-    rows = everyones(rows, "gy")
     return call(final_kernel, [block, plane, (STATE, X, Y)])(
         rows, newton_rhs, v1, v2, edge, base, water, head, left, east, south,
         ponding, land_mask,

time: 60.6 us -> 55.6 us (0.917)
  starting transfers between devices: 24.9 us -> 19.7 us
  waiting for transfers between devices: 5.53 us -> 8.57 us
  blocking collectives: 19.5 us -> 16.6 us
    ppermute x4, waiting for transfers between devices: 1.59 us -> 8.07 us  [the longest x2 5.77 us: ahead(): return lax.ppermute(x, axis, [(i, (i + 1) % n) for i in range(n)])]
    all_to_all x1, starting transfers between devices: 11.1 us -> 5.54 us  [everyones(): lax.all_to_all(rows.reshape(count, 1, Y), axis, 0, 0).reshape(count, Y)]
    all_to_all x1, waiting for transfers between devices: 3.93 us -> 0.5 us  [everyones(): lax.all_to_all(rows.reshape(count, 1, Y), axis, 0, 0).reshape(count, Y)]
    all_to_all x1, blocking collectives: 19.5 us -> 16.6 us  [everyones(): lax.all_to_all(rows.reshape(count, 1, Y), axis, 0, 0).reshape(count, Y)]
  transfers between devices with their start and end apart: 5 -> 5, of which waited for: 3 -> 4; matrix products, arithmetic and copies ran while one was open for 0% -> 0% of each run, Pallas kernels for 8% -> 8%
where the time goes in v5:
time: 55.6 us; the launch traced here: 55.3 us
  starting transfers between devices  19.7 us (35%)
  blocking collectives  16.6 us (30%)
  Pallas kernels  9.61 us (17%)
  waiting for transfers between devices  8.57 us (15%)
  between operations  0.76 us (1%)
    all_to_all x1, blocking collectives, everyones(): lax.all_to_all(rows.reshape(count, 1, Y), axis, 0, 0).reshape(count, Y)  16.6 us
    ppermute x2, starting transfers between devices, back(): return lax.ppermute(x, axis, [((i + 1) % n, i) for i in range(n)])  8.12 us
    ppermute x2, starting transfers between devices, ahead(): return lax.ppermute(x, axis, [(i, (i + 1) % n) for i in range(n)])  6.08 us
    ppermute x2, waiting for transfers between devices, ahead(): return lax.ppermute(x, axis, [(i, (i + 1) % n) for i in range(n)])  5.77 us
    all_to_all x1, starting transfers between devices, everyones(): lax.all_to_all(rows.reshape(count, 1, Y), axis, 0, 0).reshape(count, Y)  5.54 us
    pallas_call x1, Pallas kernels, on_device(): call(soil_kernel, [tall] * 3, [pltpu.VMEM((PAD, CLASSES * PAD), F32), plt...  4.57 us
    ppermute x2, waiting for transfers between devices, back(): return lax.ppermute(x, axis, [((i + 1) % n, i) for i in range(n)])  2.3 us
    pallas_call x1, Pallas kernels, on_device(): call(krylov_kernel, [block, block, (lax.axis_size('gy'), Y), (16, Y)], [p...  1.46 us
  transfers between devices with their start and end apart: 5, of which 4 were waited for; matrix products, arithmetic and copies ran while one was open for 0% of the time, Pallas kernels for 8%

profile of v5, /device:TPU:1, one launch (start us, length us, event | category | flops | bytes accessed | tf_op | source)
XLA Modules:
  0.0 55.3 jit_solution(4352254505371338355)
XLA Ops:
  0.6 0.0 copy-start.2
  0.6 0.0 copy-start.1
  0.7 0.0 copy-start.4
  0.7 1.5 %shard_map.157 = (f32[5,32,128]{2,1,0:T(8,128)S(1)}, f32[5,32,128]{2,1,0:T(8,128)S(1)}, f32[15,8,128]{2,1,0:T(8,128)S(1)}, f32[32,128]{1,0:T(8,128)S(1)}, f32[32,128]{1,0:T(8,128)S(1)}) custom-call(f32[5,32,128]{2,1,0:T(8,128)} %refs_0_.1, f32[5,32,128]{2,1,0:T(8,128)} %rhs.5, s32[5,32,128]{2,1,0:T(8,128)} %refs_2_.1, f32[16]{0:T(128)} %refs_3_.1, ...), custom_call_target="tpu_custom_call" | custom-call | tf_op jit(solution)/shard_map/pallas_call | solution.py:405
  2.1 8.1 %collective-permute-start = (f32[15,8,128]{2,1,0:T(8,128)S(1)}, f32[15,8,128]{2,1,0:T(8,128)S(1)}, u32[]{:S(2)}, u32[]{:S(2)}) collective-permute-start(f32[15,8,128]{2,1,0:T(8,128)S(1)} %get-tuple-element.21), channel_id=1, source_target_pairs={{16,0},{32,16},{48,32},{64,48},{80,64},{96,80},{112,96},{128,112},... | collective-permute-start | bytes 184328 | tf_op jit(solution)/shard_map/ppermute | solution.py:386
  10.3 0.0 copy-done.2
  10.3 0.0 copy-done.1
  10.3 0.0 copy-done.4
  10.3 0.0 copy-start
  10.3 4.6 %shard_map.158 = (f32[640,128]{1,0:T(8,128)S(1)}, f32[640,128]{1,0:T(8,128)S(1)}, f32[640,128]{1,0:T(8,128)S(1)}) custom-call(f32[640,128]{1,0:T(8,128)} %bitcast.12, s32[32,128]{1,0:T(8,128)S(1)} %copy-done.4, s32[32,128]{1,0:T(8,128)S(1)} %copy-done.2, f32[12,20,20]{2,1,0:T(8,128)S(1)} %copy-done.1), custom_call_target="tpu_custom_call" | custom-call | flops 20000000 | bytes 2000000 | tf_op jit(solution)/shard_map/pallas_call | solution.py:413
  14.9 0.0 collective-permute-done.after
  14.9 0.0 copy-done
  14.9 0.1 shard_map.159
  15.0 2.9 %collective-permute-start.2 = (f32[40,128]{1,0:T(8,128)S(1)}, f32[40,128]{1,0:T(8,128)S(1)}, u32[]{:S(2)}, u32[]{:S(2)}) collective-permute-start(f32[40,128]{1,0:T(8,128)S(1)} %shard_map.159), channel_id=1, source_target_pairs={{0,1},{1,2},{2,3},{3,4},{4,5},{5,6},{6,7},{7,8},{8,9},{9,10},{10,1... | collective-permute-start | bytes 61448 | tf_op jit(solution)/shard_map/ppermute | solution.py:381
  18.0 0.0 collective-permute-start.1
  18.0 0.9 %collective-permute-done.2.left = f32[40,128]{1,0:T(8,128)S(1)} collective-permute-done((f32[40,128]{1,0:T(8,128)S(1)}, f32[40,128]{1,0:T(8,128)S(1)}, u32[]{:S(2)}, u32[]{:S(2)}) %collective-permute-start.2) | collective-permute-done | bytes 20512 | tf_op jit(solution)/shard_map/ppermute | solution.py:381
  18.9 2.3 %collective-permute-done.1.right = f32[40,128]{1,0:T(8,128)S(1)} collective-permute-done((f32[40,128]{1,0:T(8,128)S(1)}, f32[40,128]{1,0:T(8,128)S(1)}, u32[]{:S(2)}, u32[]{:S(2)}) %collective-permute-start.1) | collective-permute-done | bytes 20512 | tf_op jit(solution)/shard_map/ppermute | solution.py:386
  21.2 1.5 %shard_map.160 = (f32[5,32,128]{2,1,0:T(8,128)S(1)}, f32[5,32,128]{2,1,0:T(8,128)S(1)}, f32[16,128]{1,0:T(8,128)S(1)}, f32[16,128]{1,0:T(8,128)S(1)}) custom-call(f32[5,32,128]{2,1,0:T(8,128)S(1)} %copy-done, f32[5,32,128]{2,1,0:T(8,128)S(1)} %get-tuple-element.19.cond, f32[5,32,128]{2,1,0:T(8,128)S(1)} %get-tuple-element.20.diag, ...), custom_call_target="tpu_custom_call" | custom-call | tf_op jit(solution)/shard_map/pallas_call | solution.py:432
  22.7 16.6 %all_to_all.10 = f32[16,1,128]{2,1,0:T(1,128)S(1)} all-to-all(f32[16,1,128]{2,1,0:T(1,128)S(1)} %bitcast.11), channel_id=1, replica_groups=mesh['gx'=32,'gy'=16] {'gy'}, dimensions={0} | all-to-all | bytes 16384 | tf_op jit(solution)/shard_map/all_to_all | solution.py:391
  39.3 0.8 %shard_map.161 = f32[32,128]{1,0:T(8,128)} custom-call(f32[16,128]{1,0:T(8,128)S(1)} %bitcast.10), custom_call_target="tpu_custom_call" | custom-call | tf_op jit(solution)/shard_map/pallas_call | solution.py:439
  40.0 0.0 copy-start.3
  40.0 5.5 %all-to-all-start.1 = ((f32[32,1,128]{2,1,0:T(1,128)}), f32[32,1,128]{2,1,0:T(1,128)S(1)}, u32[]{:S(2)}, u32[]{:S(2)}) async-start(f32[32,1,128]{2,1,0:T(1,128)} %bitcast.5), calls=%async_computation.1 | async-start | bytes 32768 | tf_op jit(solution)/shard_map/all_to_all | solution.py:391
  45.6 3.1 %collective-permute-start.3 = (f32[16,128]{1,0:T(8,128)S(1)}, f32[16,128]{1,0:T(8,128)S(1)}, u32[]{:S(2)}, u32[]{:S(2)}) collective-permute-start(f32[16,128]{1,0:T(8,128)S(1)} %get-tuple-element.31), channel_id=1, source_target_pairs={{0,16},{16,32},{32,48},{48,64},{64,80},{80,96},{96,112},{112,128},... | collective-permute-start | bytes 24584 | tf_op jit(solution)/shard_map/ppermute | solution.py:381
  48.7 4.9 %collective-permute-done.3.back = f32[16,128]{1,0:T(8,128)S(1)} collective-permute-done((f32[16,128]{1,0:T(8,128)S(1)}, f32[16,128]{1,0:T(8,128)S(1)}, u32[]{:S(2)}, u32[]{:S(2)}) %collective-permute-start.3) | collective-permute-done | bytes 8224 | tf_op jit(solution)/shard_map/ppermute | solution.py:381
  53.6 0.5 all-to-all-done.1
  54.1 0.0 copy-done.3
  54.1 1.2 %shard_map.162 = (f32[5,32,128]{2,1,0:T(8,128)}, f32[32,128]{1,0:T(8,128)}, f32[20,32,128]{2,1,0:T(8,128)}) custom-call(f32[32,128]{1,0:T(8,128)S(1)} %bitcast.9, f32[5,32,128]{2,1,0:T(8,128)S(1)} %copy-done, f32[5,32,128]{2,1,0:T(8,128)S(1)} %get-tuple-element.29.v1, f32[5,32,128]{2,1,0:T(8,128)S(1)} %get-tuple-element.30.v2, ...), custom_call_target="tpu_custom_call" | custom-call | tf_op jit(solution)/shard_map/pallas_call | solution.py:441
Async XLA Ops:
  0.6 9.6 %copy-start.2 = (s32[32,128]{1,0:T(8,128)S(1)}, s32[32,128]{1,0:T(8,128)}, u32[]{:S(2)}) copy-start(s32[32,128]{1,0:T(8,128)} %land.3) | copy-start | bytes 49156
  0.6 9.6 %copy-start.1 = (f32[12,20,20]{2,1,0:T(8,128)S(1)}, f32[12,20,20]{2,1,0:T(8,128)}, u32[]{:S(2)}) copy-start(f32[12,20,20]{2,1,0:T(8,128)} %inverse.1) | copy-start | bytes 57604
  0.7 9.6 %copy-start.4 = (s32[32,128]{1,0:T(8,128)S(1)}, s32[32,128]{1,0:T(8,128)}, u32[]{:S(2)}) copy-start(s32[32,128]{1,0:T(8,128)} %soil_class.1) | copy-start | bytes 49156
  2.1 12.8 %collective-permute-start = (f32[15,8,128]{2,1,0:T(8,128)S(1)}, f32[15,8,128]{2,1,0:T(8,128)S(1)}, u32[]{:S(2)}, u32[]{:S(2)}) collective-permute-start(f32[15,8,128]{2,1,0:T(8,128)S(1)} %get-tuple-element.21), channel_id=1, source_target_pairs={{16,0},{32,16},{48,32},{64,48},{80,64},{96,80},{112,96},{128,112},... | collective-permute-start | bytes 184328 | tf_op jit(solution)/shard_map/ppermute | solution.py:386
  10.3 4.6 %copy-start = (f32[5,32,128]{2,1,0:T(8,128)S(1)}, f32[5,32,128]{2,1,0:T(8,128)}, u32[]{:S(2)}) copy-start(f32[5,32,128]{2,1,0:T(8,128)} %rhs.5) | copy-start | bytes 245764
  15.0 3.9 %collective-permute-start.2 = (f32[40,128]{1,0:T(8,128)S(1)}, f32[40,128]{1,0:T(8,128)S(1)}, u32[]{:S(2)}, u32[]{:S(2)}) collective-permute-start(f32[40,128]{1,0:T(8,128)S(1)} %shard_map.159), channel_id=1, source_target_pairs={{0,1},{1,2},{2,3},{3,4},{4,5},{5,6},{6,7},{7,8},{8,9},{9,10},{10,1... | collective-permute-start | bytes 61448 | tf_op jit(solution)/shard_map/ppermute | solution.py:381
  18.0 3.2 %collective-permute-start.1 = (f32[40,128]{1,0:T(8,128)S(1)}, f32[40,128]{1,0:T(8,128)S(1)}, u32[]{:S(2)}, u32[]{:S(2)}) collective-permute-start(f32[40,128]{1,0:T(8,128)S(1)} %shard_map.159), channel_id=1, source_target_pairs={{1,0},{2,1},{3,2},{4,3},{5,4},{6,5},{7,6},{8,7},{9,8},{10,9},{11,1... | collective-permute-start | bytes 61448 | tf_op jit(solution)/shard_map/ppermute | solution.py:386
  40.0 14.1 %copy-start.3 = (f32[32,128]{1,0:T(8,128)S(1)}, f32[32,128]{1,0:T(8,128)}, u32[]{:S(2)}) copy-start(f32[32,128]{1,0:T(8,128)} %ponding.1) | copy-start | bytes 49156
  40.0 14.1 %all-to-all-start.1 = ((f32[32,1,128]{2,1,0:T(1,128)}), f32[32,1,128]{2,1,0:T(1,128)S(1)}, u32[]{:S(2)}, u32[]{:S(2)}) async-start(f32[32,1,128]{2,1,0:T(1,128)} %bitcast.5), calls=%async_computation.1 | async-start | bytes 32768 | tf_op jit(solution)/shard_map/all_to_all | solution.py:391
  45.6 8.0 %collective-permute-start.3 = (f32[16,128]{1,0:T(8,128)S(1)}, f32[16,128]{1,0:T(8,128)S(1)}, u32[]{:S(2)}, u32[]{:S(2)}) collective-permute-start(f32[16,128]{1,0:T(8,128)S(1)} %get-tuple-element.31), channel_id=1, source_target_pairs={{0,16},{16,32},{32,48},{48,64},{64,80},{80,96},{96,112},{112,128},... | collective-permute-start | bytes 24584 | tf_op jit(solution)/shard_map/ppermute | solution.py:381

commit v6 on v5

--- a/solution.py
+++ b/solution.py
@@ -410,6 +410,17 @@
         [pl.BlockSpec(memory_space=pltpu.HBM)] * len(local),
     )(*(pltpu.with_memory_space_constraint(a, pltpu.HBM) for a in local))
     after = back(slab, "gx")
+    (packed,) = call(pack_kernel, [(E, Y)])(newton_rhs, cond, diag, after, south)
+    left, right = ahead(packed, "gy"), back(packed, "gy")
+    v1, v2, rows, edge = call(
+        krylov_kernel,
+        [block, block, (lax.axis_size("gy"), Y), (16, Y)],
+        [pltpu.VMEM((2, n, E, Y), F32) for n in (5, 5, 4, 5, 5)],
+    )(newton_rhs, cond, diag, after, right, left, east)
+    edge = ahead(edge, "gx")
+    rows = everyones(rows, "gy")
+    (rows,) = call(relay_kernel, [(lax.axis_size("gx"), Y)])(rows)
+    rows, kinds = lax.optimization_barrier((rows, soil_class))
     base, water, head = call(
         soil_kernel,
         [tall] * 3,
@@ -424,19 +435,8 @@
         nbytes=2_000_000,
     )(
         pltpu.with_memory_space_constraint(soil_state.reshape(tall), pltpu.HBM),
-        soil_class, land_mask, soil_inverse,
-    )
-    after, base, water, head = lax.optimization_barrier((after, base, water, head))
-    (packed,) = call(pack_kernel, [(E, Y)])(newton_rhs, cond, diag, after, south)
-    left, right = ahead(packed, "gy"), back(packed, "gy")
-    v1, v2, rows, edge = call(
-        krylov_kernel,
-        [block, block, (lax.axis_size("gy"), Y), (16, Y)],
-        [pltpu.VMEM((2, n, E, Y), F32) for n in (5, 5, 4, 5, 5)],
-    )(newton_rhs, cond, diag, after, right, left, east)
-    edge = ahead(edge, "gx")
-    rows = everyones(rows, "gy")
-    (rows,) = call(relay_kernel, [(lax.axis_size("gx"), Y)])(rows)
+        kinds, land_mask, soil_inverse,
+    )
     rows = everyones(rows, "gx")
     return call(final_kernel, [block, plane, (STATE, X, Y)])(
         rows, newton_rhs, v1, v2, edge, base, water, head, left, east, south,

time: 55.6 us -> 55.7 us (level)
  starting transfers between devices: 19.7 us -> 23.2 us
  waiting for transfers between devices: 8.57 us -> 5.1 us
    ppermute x2, waiting for transfers between devices: 5.77 us -> 1.04 us  [ahead(): return lax.ppermute(x, axis, [(i, (i + 1) % n) for i in range(n)])]
    all_to_all x1, starting transfers between devices: 5.54 us -> 8.34 us  [everyones(): lax.all_to_all(rows.reshape(count, 1, Y), axis, 0, 0).reshape(count, Y)]
    ppermute x2, waiting for transfers between devices: 2.3 us -> 3.57 us  [back(): return lax.ppermute(x, axis, [((i + 1) % n, i) for i in range(n)])]
    ppermute x2, starting transfers between devices: 6.08 us -> 6.66 us  [ahead(): return lax.ppermute(x, axis, [(i, (i + 1) % n) for i in range(n)])]
  transfers between devices with their start and end apart: 5 -> 5, of which waited for: 4 -> 5; matrix products, arithmetic and copies ran while one was open for 0% -> 0% of each run, Pallas kernels for 8% -> 8%
where the time goes in v6:
time: 55.7 us; the launch traced here: 55.3 us
  starting transfers between devices  23.2 us (42%)
  blocking collectives  16.6 us (30%)
  Pallas kernels  9.59 us (17%)
  waiting for transfers between devices  5.1 us (9%)
  between operations  0.73 us (1%)
    all_to_all x1, blocking collectives, everyones(): lax.all_to_all(rows.reshape(count, 1, Y), axis, 0, 0).reshape(count, Y)  16.6 us
    all_to_all x1, starting transfers between devices, everyones(): lax.all_to_all(rows.reshape(count, 1, Y), axis, 0, 0).reshape(count, Y)  8.34 us
    ppermute x2, starting transfers between devices, back(): return lax.ppermute(x, axis, [((i + 1) % n, i) for i in range(n)])  8.23 us
    ppermute x2, starting transfers between devices, ahead(): return lax.ppermute(x, axis, [(i, (i + 1) % n) for i in range(n)])  6.66 us
    pallas_call x1, Pallas kernels, on_device(): call(soil_kernel, [tall] * 3, [pltpu.VMEM((PAD, CLASSES * PAD), F32), plt...  4.57 us
    ppermute x2, waiting for transfers between devices, back(): return lax.ppermute(x, axis, [((i + 1) % n, i) for i in range(n)])  3.57 us
    pallas_call x1, Pallas kernels, on_device(): call(krylov_kernel, [block, block, (lax.axis_size('gy'), Y), (16, Y)], [p...  1.45 us
    pallas_call x1, Pallas kernels, on_device(): call(local_kernel, [block, block, (FIELDS, E - X, Y), plane, plane], [(pl...  1.45 us
  transfers between devices with their start and end apart: 5, of which 5 were waited for; matrix products, arithmetic and copies ran while one was open for 0% of the time, Pallas kernels for 8%

profile of v6, /device:TPU:1, one launch (start us, length us, event | category | flops | bytes accessed | tf_op | source)
XLA Modules:
  0.0 55.3 jit_solution(6297522988897468889)
XLA Ops:
  0.6 0.0 copy-start
  0.6 1.4 %shard_map.157 = (f32[5,32,128]{2,1,0:T(8,128)S(1)}, f32[5,32,128]{2,1,0:T(8,128)S(1)}, f32[15,8,128]{2,1,0:T(8,128)S(1)}, f32[32,128]{1,0:T(8,128)S(1)}, f32[32,128]{1,0:T(8,128)S(1)}) custom-call(f32[5,32,128]{2,1,0:T(8,128)} %refs_0_.1, f32[5,32,128]{2,1,0:T(8,128)} %rhs.5, s32[5,32,128]{2,1,0:T(8,128)} %refs_2_.1, f32[16]{0:T(128)} %refs_3_.1, ...), custom_call_target="tpu_custom_call" | custom-call | tf_op jit(solution)/shard_map/pallas_call | solution.py:405
  2.1 8.1 %collective-permute-start = (f32[15,8,128]{2,1,0:T(8,128)S(1)}, f32[15,8,128]{2,1,0:T(8,128)S(1)}, u32[]{:S(2)}, u32[]{:S(2)}) collective-permute-start(f32[15,8,128]{2,1,0:T(8,128)S(1)} %get-tuple-element.19), channel_id=1, source_target_pairs={{16,0},{32,16},{48,32},{64,48},{80,64},{96,80},{112,96},{128,112},... | collective-permute-start | bytes 184328 | tf_op jit(solution)/shard_map/ppermute | solution.py:386
  10.2 1.3 %collective-permute-done.after = f32[15,8,128]{2,1,0:T(8,128)S(1)} collective-permute-done((f32[15,8,128]{2,1,0:T(8,128)S(1)}, f32[15,8,128]{2,1,0:T(8,128)S(1)}, u32[]{:S(2)}, u32[]{:S(2)}) %collective-permute-start) | collective-permute-done | bytes 61472 | tf_op jit(solution)/shard_map/ppermute | solution.py:386
  11.5 0.0 copy-done
  11.5 0.1 shard_map.158
  11.7 3.5 %collective-permute-start.2 = (f32[40,128]{1,0:T(8,128)S(1)}, f32[40,128]{1,0:T(8,128)S(1)}, u32[]{:S(2)}, u32[]{:S(2)}) collective-permute-start(f32[40,128]{1,0:T(8,128)S(1)} %shard_map.158), channel_id=1, source_target_pairs={{0,1},{1,2},{2,3},{3,4},{4,5},{5,6},{6,7},{7,8},{8,9},{9,10},{10,1... | collective-permute-start | bytes 61448 | tf_op jit(solution)/shard_map/ppermute | solution.py:381
  15.2 0.1 collective-permute-start.1
  15.3 0.8 %collective-permute-done.2.left = f32[40,128]{1,0:T(8,128)S(1)} collective-permute-done((f32[40,128]{1,0:T(8,128)S(1)}, f32[40,128]{1,0:T(8,128)S(1)}, u32[]{:S(2)}, u32[]{:S(2)}) %collective-permute-start.2) | collective-permute-done | bytes 20512 | tf_op jit(solution)/shard_map/ppermute | solution.py:381
  16.1 2.3 %collective-permute-done.1.right = f32[40,128]{1,0:T(8,128)S(1)} collective-permute-done((f32[40,128]{1,0:T(8,128)S(1)}, f32[40,128]{1,0:T(8,128)S(1)}, u32[]{:S(2)}, u32[]{:S(2)}) %collective-permute-start.1) | collective-permute-done | bytes 20512 | tf_op jit(solution)/shard_map/ppermute | solution.py:386
  18.4 0.0 copy-start.1
  18.4 1.5 %shard_map.159 = (f32[5,32,128]{2,1,0:T(8,128)S(1)}, f32[5,32,128]{2,1,0:T(8,128)S(1)}, f32[16,128]{1,0:T(8,128)S(1)}, f32[16,128]{1,0:T(8,128)S(1)}) custom-call(f32[5,32,128]{2,1,0:T(8,128)S(1)} %copy-done, f32[5,32,128]{2,1,0:T(8,128)S(1)} %get-tuple-element.17.cond, f32[5,32,128]{2,1,0:T(8,128)S(1)} %get-tuple-element.18.diag, ...), custom_call_target="tpu_custom_call" | custom-call | tf_op jit(solution)/shard_map/pallas_call | solution.py:415
  19.8 16.6 %all_to_all.10 = f32[16,1,128]{2,1,0:T(1,128)S(1)} all-to-all(f32[16,1,128]{2,1,0:T(1,128)S(1)} %bitcast.11), channel_id=1, replica_groups=mesh['gx'=32,'gy'=16] {'gy'}, dimensions={0} | all-to-all | bytes 16384 | tf_op jit(solution)/shard_map/all_to_all | solution.py:391
  36.5 0.8 %shard_map.160 = f32[32,128]{1,0:T(8,128)} custom-call(f32[16,128]{1,0:T(8,128)S(1)} %bitcast.10), custom_call_target="tpu_custom_call" | custom-call | tf_op jit(solution)/shard_map/pallas_call | solution.py:422
  37.2 0.0 copy-start.2
  37.2 0.0 copy-start.4
  37.2 8.3 %all-to-all-start.1 = ((f32[32,1,128]{2,1,0:T(1,128)}), f32[32,1,128]{2,1,0:T(1,128)S(1)}, u32[]{:S(2)}, u32[]{:S(2)}) async-start(f32[32,1,128]{2,1,0:T(1,128)} %bitcast.4), calls=%async_computation.1 | async-start | bytes 32768 | tf_op jit(solution)/shard_map/all_to_all | solution.py:391
  45.6 3.1 %collective-permute-start.3 = (f32[16,128]{1,0:T(8,128)S(1)}, f32[16,128]{1,0:T(8,128)S(1)}, u32[]{:S(2)}, u32[]{:S(2)}) collective-permute-start(f32[16,128]{1,0:T(8,128)S(1)} %get-tuple-element.26), channel_id=1, source_target_pairs={{0,16},{16,32},{32,48},{48,64},{64,80},{80,96},{96,112},{112,128},... | collective-permute-start | bytes 24584 | tf_op jit(solution)/shard_map/ppermute | solution.py:381
  48.7 0.0 copy-done.1
  48.7 0.0 copy-done.2
  48.7 0.0 copy-done.4
  48.7 0.0 copy-start.3
  48.8 4.6 %shard_map.161 = (f32[640,128]{1,0:T(8,128)S(1)}, f32[640,128]{1,0:T(8,128)S(1)}, f32[640,128]{1,0:T(8,128)S(1)}) custom-call(f32[640,128]{1,0:T(8,128)} %bitcast.12, s32[32,128]{1,0:T(8,128)S(1)} %copy-done.4, s32[32,128]{1,0:T(8,128)S(1)} %copy-done.2, f32[12,20,20]{2,1,0:T(8,128)S(1)} %copy-done.1), custom_call_target="tpu_custom_call" | custom-call | flops 20000000 | bytes 2000000 | tf_op jit(solution)/shard_map/pallas_call | solution.py:424
  53.3 0.2 collective-permute-done.3.back
  53.6 0.5 all-to-all-done.1
  54.1 0.0 copy-done.3
  54.1 1.2 %shard_map.162 = (f32[5,32,128]{2,1,0:T(8,128)}, f32[32,128]{1,0:T(8,128)}, f32[20,32,128]{2,1,0:T(8,128)}) custom-call(f32[32,128]{1,0:T(8,128)S(1)} %bitcast.9, f32[5,32,128]{2,1,0:T(8,128)S(1)} %copy-done, f32[5,32,128]{2,1,0:T(8,128)S(1)} %get-tuple-element.24.v1, f32[5,32,128]{2,1,0:T(8,128)S(1)} %get-tuple-element.25.v2, ...), custom_call_target="tpu_custom_call" | custom-call | tf_op jit(solution)/shard_map/pallas_call | solution.py:441
Async XLA Ops:
  0.6 10.9 %copy-start = (f32[5,32,128]{2,1,0:T(8,128)S(1)}, f32[5,32,128]{2,1,0:T(8,128)}, u32[]{:S(2)}) copy-start(f32[5,32,128]{2,1,0:T(8,128)} %rhs.5) | copy-start | bytes 245764
  2.1 9.4 %collective-permute-start = (f32[15,8,128]{2,1,0:T(8,128)S(1)}, f32[15,8,128]{2,1,0:T(8,128)S(1)}, u32[]{:S(2)}, u32[]{:S(2)}) collective-permute-start(f32[15,8,128]{2,1,0:T(8,128)S(1)} %get-tuple-element.19), channel_id=1, source_target_pairs={{16,0},{32,16},{48,32},{64,48},{80,64},{96,80},{112,96},{128,112},... | collective-permute-start | bytes 184328 | tf_op jit(solution)/shard_map/ppermute | solution.py:386
  11.7 4.4 %collective-permute-start.2 = (f32[40,128]{1,0:T(8,128)S(1)}, f32[40,128]{1,0:T(8,128)S(1)}, u32[]{:S(2)}, u32[]{:S(2)}) collective-permute-start(f32[40,128]{1,0:T(8,128)S(1)} %shard_map.158), channel_id=1, source_target_pairs={{0,1},{1,2},{2,3},{3,4},{4,5},{5,6},{6,7},{7,8},{8,9},{9,10},{10,1... | collective-permute-start | bytes 61448 | tf_op jit(solution)/shard_map/ppermute | solution.py:381
  15.2 3.2 %collective-permute-start.1 = (f32[40,128]{1,0:T(8,128)S(1)}, f32[40,128]{1,0:T(8,128)S(1)}, u32[]{:S(2)}, u32[]{:S(2)}) collective-permute-start(f32[40,128]{1,0:T(8,128)S(1)} %shard_map.158), channel_id=1, source_target_pairs={{1,0},{2,1},{3,2},{4,3},{5,4},{6,5},{7,6},{8,7},{9,8},{10,9},{11,1... | collective-permute-start | bytes 61448 | tf_op jit(solution)/shard_map/ppermute | solution.py:386
  18.4 30.3 %copy-start.1 = (f32[12,20,20]{2,1,0:T(8,128)S(1)}, f32[12,20,20]{2,1,0:T(8,128)}, u32[]{:S(2)}) copy-start(f32[12,20,20]{2,1,0:T(8,128)} %inverse.1) | copy-start | bytes 57604
  37.2 11.5 %copy-start.2 = (s32[32,128]{1,0:T(8,128)S(1)}, s32[32,128]{1,0:T(8,128)}, u32[]{:S(2)}) copy-start(s32[32,128]{1,0:T(8,128)} %land.3) | copy-start | bytes 49156
  37.2 11.5 %copy-start.4 = (s32[32,128]{1,0:T(8,128)S(1)}, s32[32,128]{1,0:T(8,128)}, u32[]{:S(2)}) copy-start(s32[32,128]{1,0:T(8,128)} %soil_class) | copy-start | bytes 49156
  37.2 16.9 %all-to-all-start.1 = ((f32[32,1,128]{2,1,0:T(1,128)}), f32[32,1,128]{2,1,0:T(1,128)S(1)}, u32[]{:S(2)}, u32[]{:S(2)}) async-start(f32[32,1,128]{2,1,0:T(1,128)} %bitcast.4), calls=%async_computation.1 | async-start | bytes 32768 | tf_op jit(solution)/shard_map/all_to_all | solution.py:391
  45.6 8.0 %collective-permute-start.3 = (f32[16,128]{1,0:T(8,128)S(1)}, f32[16,128]{1,0:T(8,128)S(1)}, u32[]{:S(2)}, u32[]{:S(2)}) collective-permute-start(f32[16,128]{1,0:T(8,128)S(1)} %get-tuple-element.26), channel_id=1, source_target_pairs={{0,16},{16,32},{32,48},{48,64},{64,80},{80,96},{96,112},{112,128},... | collective-permute-start | bytes 24584 | tf_op jit(solution)/shard_map/ppermute | solution.py:381
  48.7 5.3 %copy-start.3 = (f32[32,128]{1,0:T(8,128)S(1)}, f32[32,128]{1,0:T(8,128)}, u32[]{:S(2)}) copy-start(f32[32,128]{1,0:T(8,128)} %ponding.1) | copy-start | bytes 49156

commit v7 on v6

--- a/solution.py
+++ b/solution.py
@@ -278,11 +278,7 @@
         row_out[i : i + 8, :] = both
 
 
-def soil_kernel(
-    state_hbm, soil_class, land, inverse, base, water, head, w, w01, state, sem
-):
-    copy = pltpu.make_async_copy(state_hbm, state, sem)
-    copy.start()
+def soil_kernel(state, soil_class, land, inverse, base, water, head, w, w01):
     w[...] = jnp.zeros(w.shape, F32)
     w01[...] = jnp.zeros(w01.shape, F32)
     for e in range(CLASSES):
@@ -291,7 +287,6 @@
         w01[0:STATE, e : e + 1] = x[:, 0:1]
         w01[PAD : PAD + STATE, e : e + 1] = x[:, 1:2]
     w_all, w_two = w[...], w01[...]
-    copy.wait()
     zero = jnp.zeros((PAD - STATE, Y), F32)
     entry = iota((16, Y), 0)
 
@@ -427,16 +422,10 @@
         [
             pltpu.VMEM((PAD, CLASSES * PAD), F32),
             pltpu.VMEM((2 * PAD, 16), F32),
-            pltpu.VMEM(tall, F32),
-            pltpu.SemaphoreType.DMA,
         ],
-        [pl.BlockSpec(memory_space=pltpu.HBM)] + [pl.BlockSpec()] * 3,
         flops=20_000_000,
         nbytes=2_000_000,
-    )(
-        pltpu.with_memory_space_constraint(soil_state.reshape(tall), pltpu.HBM),
-        kinds, land_mask, soil_inverse,
-    )
+    )(soil_state.reshape(tall), kinds, land_mask, soil_inverse)
     rows = everyones(rows, "gx")
     return call(final_kernel, [block, plane, (STATE, X, Y)])(
         rows, newton_rhs, v1, v2, edge, base, water, head, left, east, south,

time: 55.7 us -> 55.6 us (level)
  Pallas kernels: 9.59 us -> 8.53 us
  waiting for transfers between devices: 5.1 us -> 6.16 us
    pallas_call x1, Pallas kernels: 4.57 us -> 3.51 us  [on_device(): call(soil_kernel, [tall] * 3, [pltpu.VMEM((PAD, CLASSES * PAD), F32), plt...]
    ppermute x2, waiting for transfers between devices: 1.04 us -> 2.09 us  [ahead(): return lax.ppermute(x, axis, [(i, (i + 1) % n) for i in range(n)])]
  transfers between devices with their start and end apart: 5 -> 5, of which waited for: 5 -> 5; matrix products, arithmetic and copies ran while one was open for 0% -> 0% of each run, Pallas kernels for 8% -> 6%
where the time goes in v7:
time: 55.6 us; the launch traced here: 55.3 us
  starting transfers between devices  23.2 us (42%)
  blocking collectives  16.6 us (30%)
  Pallas kernels  8.53 us (15%)
  waiting for transfers between devices  6.16 us (11%)
  between operations  0.73 us (1%)
    all_to_all x1, blocking collectives, everyones(): lax.all_to_all(rows.reshape(count, 1, Y), axis, 0, 0).reshape(count, Y)  16.6 us
    all_to_all x1, starting transfers between devices, everyones(): lax.all_to_all(rows.reshape(count, 1, Y), axis, 0, 0).reshape(count, Y)  8.34 us
    ppermute x2, starting transfers between devices, back(): return lax.ppermute(x, axis, [((i + 1) % n, i) for i in range(n)])  8.23 us
    ppermute x2, starting transfers between devices, ahead(): return lax.ppermute(x, axis, [(i, (i + 1) % n) for i in range(n)])  6.66 us
    ppermute x2, waiting for transfers between devices, back(): return lax.ppermute(x, axis, [((i + 1) % n, i) for i in range(n)])  3.57 us
    pallas_call x1, Pallas kernels, on_device(): call(soil_kernel, [tall] * 3, [pltpu.VMEM((PAD, CLASSES * PAD), F32), plt...  3.51 us
    ppermute x2, waiting for transfers between devices, ahead(): return lax.ppermute(x, axis, [(i, (i + 1) % n) for i in range(n)])  2.09 us
    pallas_call x1, Pallas kernels, on_device(): call(krylov_kernel, [block, block, (lax.axis_size('gy'), Y), (16, Y)], [p...  1.45 us
  transfers between devices with their start and end apart: 5, of which 5 were waited for; matrix products, arithmetic and copies ran while one was open for 0% of the time, Pallas kernels for 6%

profile of v7, /device:TPU:1, one launch (start us, length us, event | category | flops | bytes accessed | tf_op | source)
XLA Modules:
  0.0 55.3 jit_solution(14673559091992034153)
XLA Ops:
  0.6 0.0 copy-start
  0.6 1.4 %shard_map.157 = (f32[5,32,128]{2,1,0:T(8,128)S(1)}, f32[5,32,128]{2,1,0:T(8,128)S(1)}, f32[15,8,128]{2,1,0:T(8,128)S(1)}, f32[32,128]{1,0:T(8,128)S(1)}, f32[32,128]{1,0:T(8,128)S(1)}) custom-call(f32[5,32,128]{2,1,0:T(8,128)} %refs_0_.1, f32[5,32,128]{2,1,0:T(8,128)} %rhs.5, s32[5,32,128]{2,1,0:T(8,128)} %refs_2_.1, f32[16]{0:T(128)} %refs_3_.1, ...), custom_call_target="tpu_custom_call" | custom-call | tf_op jit(solution)/shard_map/pallas_call | solution.py:400
  2.1 8.1 %collective-permute-start = (f32[15,8,128]{2,1,0:T(8,128)S(1)}, f32[15,8,128]{2,1,0:T(8,128)S(1)}, u32[]{:S(2)}, u32[]{:S(2)}) collective-permute-start(f32[15,8,128]{2,1,0:T(8,128)S(1)} %get-tuple-element.19), channel_id=1, source_target_pairs={{16,0},{32,16},{48,32},{64,48},{80,64},{96,80},{112,96},{128,112},... | collective-permute-start | bytes 184328 | tf_op jit(solution)/shard_map/ppermute | solution.py:381
  10.2 1.3 %collective-permute-done.after = f32[15,8,128]{2,1,0:T(8,128)S(1)} collective-permute-done((f32[15,8,128]{2,1,0:T(8,128)S(1)}, f32[15,8,128]{2,1,0:T(8,128)S(1)}, u32[]{:S(2)}, u32[]{:S(2)}) %collective-permute-start) | collective-permute-done | bytes 61472 | tf_op jit(solution)/shard_map/ppermute | solution.py:381
  11.5 0.0 copy-done
  11.5 0.0 copy-start.1
  11.5 0.1 shard_map.158
  11.7 3.5 %collective-permute-start.2 = (f32[40,128]{1,0:T(8,128)S(1)}, f32[40,128]{1,0:T(8,128)S(1)}, u32[]{:S(2)}, u32[]{:S(2)}) collective-permute-start(f32[40,128]{1,0:T(8,128)S(1)} %shard_map.158), channel_id=1, source_target_pairs={{0,1},{1,2},{2,3},{3,4},{4,5},{5,6},{6,7},{7,8},{8,9},{9,10},{10,1... | collective-permute-start | bytes 61448 | tf_op jit(solution)/shard_map/ppermute | solution.py:376
  15.2 0.1 collective-permute-start.1
  15.3 0.8 %collective-permute-done.2.left = f32[40,128]{1,0:T(8,128)S(1)} collective-permute-done((f32[40,128]{1,0:T(8,128)S(1)}, f32[40,128]{1,0:T(8,128)S(1)}, u32[]{:S(2)}, u32[]{:S(2)}) %collective-permute-start.2) | collective-permute-done | bytes 20512 | tf_op jit(solution)/shard_map/ppermute | solution.py:376
  16.1 2.3 %collective-permute-done.1.right = f32[40,128]{1,0:T(8,128)S(1)} collective-permute-done((f32[40,128]{1,0:T(8,128)S(1)}, f32[40,128]{1,0:T(8,128)S(1)}, u32[]{:S(2)}, u32[]{:S(2)}) %collective-permute-start.1) | collective-permute-done | bytes 20512 | tf_op jit(solution)/shard_map/ppermute | solution.py:381
  18.4 0.0 copy-start.2
  18.4 1.5 %shard_map.159 = (f32[5,32,128]{2,1,0:T(8,128)S(1)}, f32[5,32,128]{2,1,0:T(8,128)S(1)}, f32[16,128]{1,0:T(8,128)S(1)}, f32[16,128]{1,0:T(8,128)S(1)}) custom-call(f32[5,32,128]{2,1,0:T(8,128)S(1)} %copy-done, f32[5,32,128]{2,1,0:T(8,128)S(1)} %get-tuple-element.17.cond, f32[5,32,128]{2,1,0:T(8,128)S(1)} %get-tuple-element.18.diag, ...), custom_call_target="tpu_custom_call" | custom-call | tf_op jit(solution)/shard_map/pallas_call | solution.py:410
  19.8 16.6 %all_to_all.10 = f32[16,1,128]{2,1,0:T(1,128)S(1)} all-to-all(f32[16,1,128]{2,1,0:T(1,128)S(1)} %bitcast.12), channel_id=1, replica_groups=mesh['gx'=32,'gy'=16] {'gy'}, dimensions={0} | all-to-all | bytes 16384 | tf_op jit(solution)/shard_map/all_to_all | solution.py:386
  36.5 0.8 %shard_map.160 = f32[32,128]{1,0:T(8,128)} custom-call(f32[16,128]{1,0:T(8,128)S(1)} %bitcast.11), custom_call_target="tpu_custom_call" | custom-call | tf_op jit(solution)/shard_map/pallas_call | solution.py:417
  37.2 0.0 copy-start.3
  37.2 0.0 copy-start.5
  37.2 8.3 %all-to-all-start.1 = ((f32[32,1,128]{2,1,0:T(1,128)}), f32[32,1,128]{2,1,0:T(1,128)S(1)}, u32[]{:S(2)}, u32[]{:S(2)}) async-start(f32[32,1,128]{2,1,0:T(1,128)} %bitcast.4), calls=%async_computation.1 | async-start | bytes 32768 | tf_op jit(solution)/shard_map/all_to_all | solution.py:386
  45.6 3.1 %collective-permute-start.3 = (f32[16,128]{1,0:T(8,128)S(1)}, f32[16,128]{1,0:T(8,128)S(1)}, u32[]{:S(2)}, u32[]{:S(2)}) collective-permute-start(f32[16,128]{1,0:T(8,128)S(1)} %get-tuple-element.26), channel_id=1, source_target_pairs={{0,16},{16,32},{32,48},{48,64},{64,80},{80,96},{96,112},{112,128},... | collective-permute-start | bytes 24584 | tf_op jit(solution)/shard_map/ppermute | solution.py:376
  48.7 0.0 copy-done.1
  48.7 0.0 copy-done.2
  48.7 0.0 copy-done.3
  48.7 0.0 copy-done.5
  48.8 0.0 copy-start.4
  48.8 3.5 %shard_map.161 = (f32[640,128]{1,0:T(8,128)S(1)}, f32[640,128]{1,0:T(8,128)S(1)}, f32[640,128]{1,0:T(8,128)S(1)}) custom-call(f32[640,128]{1,0:T(8,128)S(1)} %bitcast.9, s32[32,128]{1,0:T(8,128)S(1)} %copy-done.5, s32[32,128]{1,0:T(8,128)S(1)} %copy-done.3, f32[12,20,20]{2,1,0:T(8,128)S(1)} %copy-done.2), custom_call_target="tpu_custom_call" | custom-call | flops 20000000 | bytes 2000000 | tf_op jit(solution)/shard_map/pallas_call | solution.py:419
  52.3 1.3 %collective-permute-done.3.back = f32[16,128]{1,0:T(8,128)S(1)} collective-permute-done((f32[16,128]{1,0:T(8,128)S(1)}, f32[16,128]{1,0:T(8,128)S(1)}, u32[]{:S(2)}, u32[]{:S(2)}) %collective-permute-start.3) | collective-permute-done | bytes 8224 | tf_op jit(solution)/shard_map/ppermute | solution.py:376
  53.6 0.5 all-to-all-done.1
  54.1 0.0 copy-done.4
  54.1 1.2 %shard_map.162 = (f32[5,32,128]{2,1,0:T(8,128)}, f32[32,128]{1,0:T(8,128)}, f32[20,32,128]{2,1,0:T(8,128)}) custom-call(f32[32,128]{1,0:T(8,128)S(1)} %bitcast.10, f32[5,32,128]{2,1,0:T(8,128)S(1)} %copy-done, f32[5,32,128]{2,1,0:T(8,128)S(1)} %get-tuple-element.24.v1, f32[5,32,128]{2,1,0:T(8,128)S(1)} %get-tuple-element.25.v2, ...), custom_call_target="tpu_custom_call" | custom-call | tf_op jit(solution)/shard_map/pallas_call | solution.py:430
Async XLA Ops:
  0.6 10.9 %copy-start = (f32[5,32,128]{2,1,0:T(8,128)S(1)}, f32[5,32,128]{2,1,0:T(8,128)}, u32[]{:S(2)}) copy-start(f32[5,32,128]{2,1,0:T(8,128)} %rhs.5) | copy-start | bytes 245764
  2.1 9.4 %collective-permute-start = (f32[15,8,128]{2,1,0:T(8,128)S(1)}, f32[15,8,128]{2,1,0:T(8,128)S(1)}, u32[]{:S(2)}, u32[]{:S(2)}) collective-permute-start(f32[15,8,128]{2,1,0:T(8,128)S(1)} %get-tuple-element.19), channel_id=1, source_target_pairs={{16,0},{32,16},{48,32},{64,48},{80,64},{96,80},{112,96},{128,112},... | collective-permute-start | bytes 184328 | tf_op jit(solution)/shard_map/ppermute | solution.py:381
  11.5 37.2 %copy-start.1 = (f32[20,32,128]{2,1,0:T(8,128)S(1)}, f32[20,32,128]{2,1,0:T(8,128)}, u32[]{:S(2)}) copy-start(f32[20,32,128]{2,1,0:T(8,128)} %param.27) | copy-start | bytes 983044
  11.7 4.4 %collective-permute-start.2 = (f32[40,128]{1,0:T(8,128)S(1)}, f32[40,128]{1,0:T(8,128)S(1)}, u32[]{:S(2)}, u32[]{:S(2)}) collective-permute-start(f32[40,128]{1,0:T(8,128)S(1)} %shard_map.158), channel_id=1, source_target_pairs={{0,1},{1,2},{2,3},{3,4},{4,5},{5,6},{6,7},{7,8},{8,9},{9,10},{10,1... | collective-permute-start | bytes 61448 | tf_op jit(solution)/shard_map/ppermute | solution.py:376
  15.2 3.2 %collective-permute-start.1 = (f32[40,128]{1,0:T(8,128)S(1)}, f32[40,128]{1,0:T(8,128)S(1)}, u32[]{:S(2)}, u32[]{:S(2)}) collective-permute-start(f32[40,128]{1,0:T(8,128)S(1)} %shard_map.158), channel_id=1, source_target_pairs={{1,0},{2,1},{3,2},{4,3},{5,4},{6,5},{7,6},{8,7},{9,8},{10,9},{11,1... | collective-permute-start | bytes 61448 | tf_op jit(solution)/shard_map/ppermute | solution.py:381
  18.4 30.3 %copy-start.2 = (f32[12,20,20]{2,1,0:T(8,128)S(1)}, f32[12,20,20]{2,1,0:T(8,128)}, u32[]{:S(2)}) copy-start(f32[12,20,20]{2,1,0:T(8,128)} %inverse.1) | copy-start | bytes 57604
  37.2 11.5 %copy-start.3 = (s32[32,128]{1,0:T(8,128)S(1)}, s32[32,128]{1,0:T(8,128)}, u32[]{:S(2)}) copy-start(s32[32,128]{1,0:T(8,128)} %land.3) | copy-start | bytes 49156
  37.2 11.5 %copy-start.5 = (s32[32,128]{1,0:T(8,128)S(1)}, s32[32,128]{1,0:T(8,128)}, u32[]{:S(2)}) copy-start(s32[32,128]{1,0:T(8,128)} %soil_class) | copy-start | bytes 49156
  37.2 16.9 %all-to-all-start.1 = ((f32[32,1,128]{2,1,0:T(1,128)}), f32[32,1,128]{2,1,0:T(1,128)S(1)}, u32[]{:S(2)}, u32[]{:S(2)}) async-start(f32[32,1,128]{2,1,0:T(1,128)} %bitcast.4), calls=%async_computation.1 | async-start | bytes 32768 | tf_op jit(solution)/shard_map/all_to_all | solution.py:386
  45.6 8.0 %collective-permute-start.3 = (f32[16,128]{1,0:T(8,128)S(1)}, f32[16,128]{1,0:T(8,128)S(1)}, u32[]{:S(2)}, u32[]{:S(2)}) collective-permute-start(f32[16,128]{1,0:T(8,128)S(1)} %get-tuple-element.26), channel_id=1, source_target_pairs={{0,16},{16,32},{32,48},{48,64},{64,80},{80,96},{96,112},{112,128},... | collective-permute-start | bytes 24584 | tf_op jit(solution)/shard_map/ppermute | solution.py:376
  48.8 5.3 %copy-start.4 = (f32[32,128]{1,0:T(8,128)S(1)}, f32[32,128]{1,0:T(8,128)}, u32[]{:S(2)}) copy-start(f32[32,128]{1,0:T(8,128)} %ponding.1) | copy-start | bytes 49156

commit v8 on v7

--- a/solution.py
+++ b/solution.py
@@ -95,13 +95,13 @@
 
 
 def local_kernel(*refs):
-    (cond, diag, slab, east, south), held, sem = refs[11:16], refs[16:27], refs[27]
+    (cond, diag, slab, east, south, state), held, sem = refs[12:18], refs[18:29], refs[29]
     copies = [
-        pltpu.make_async_copy(refs[i], held[i], sem.at[i]) for i in range(11)
+        pltpu.make_async_copy(refs[i], (*held, state)[i], sem.at[i]) for i in range(12)
     ]
     for copy in copies:
         copy.start()
-    for copy in copies:
+    for copy in copies[:11]:
         copy.wait()
     (pressure, rhs, geology, ks, alpha, expo, land, ponding, slope_class, slope, flow) = held
     t_ks = gather_table(ks, 16)
@@ -128,6 +128,7 @@
     eastward = jnp.where(flow[...] == 0, out, 0.0)
     east[...] = eastward
     south[...] = out - eastward
+    copies[11].wait()
 
 
 def pack_kernel(rhs, cond, diag, after, south, packed):
@@ -278,47 +279,49 @@
         row_out[i : i + 8, :] = both
 
 
-def soil_kernel(state, soil_class, land, inverse, base, water, head, w, w01):
+def soil_kernel(state, soil_class, land, inverse, base, w):
     w[...] = jnp.zeros(w.shape, F32)
-    w01[...] = jnp.zeros(w01.shape, F32)
     for e in range(CLASSES):
         x = inverse[e]
-        w[0:STATE, e * PAD : e * PAD + STATE] = x
-        w01[0:STATE, e : e + 1] = x[:, 0:1]
-        w01[PAD : PAD + STATE, e : e + 1] = x[:, 1:2]
-    w_all, w_two = w[...], w01[...]
-    zero = jnp.zeros((PAD - STATE, Y), F32)
-    entry = iota((16, Y), 0)
-
-    def dot(a, columns):
-        return jnp.dot(
-            a,
-            jnp.concatenate(columns, axis=1),
+        w[0:STATE, 16 * e : 16 * e + 16] = x[:, 0:16]
+        w[0:STATE, 192 + 4 * e : 196 + 4 * e] = x[:, 16:STATE]
+    w_all = w[...]
+    half = (iota((8, Y), 0) >= 4).astype(jnp.int32)
+    for x0 in range(0, X, 4):
+        fields, spread, kinds = [], [], []
+        for x in range(x0, x0 + 4):
+            f = state[pl.ds(x, STATE, stride=X), :]
+            kind = jnp.where(land[x : x + 1, :] == 1, soil_class[x : x + 1, :], -1)
+            twice = jnp.concatenate([f[16:STATE], f[16:STATE]], axis=0)
+            parts = [jnp.where(kind == e, f[0:16], 0.0) for e in range(CLASSES)]
+            for e in range(0, CLASSES, 2):
+                parts.append(jnp.where(kind == e + half, twice, 0.0))
+            spread.append(jnp.concatenate(parts, axis=0))
+            fields.append(f)
+            kinds.append(kind)
+        solved = jnp.dot(
+            w_all,
+            jnp.concatenate(spread, axis=1),
             precision=lax.Precision.HIGHEST,
             preferred_element_type=F32,
         )
-
-    for x0 in range(0, X, 4):
-        fields, spread, hot, kinds = [], [], [], []
-        for x in range(x0, x0 + 4):
-            f = state[pl.ds(x, STATE, stride=X), :]
-            kind = jnp.where(land[x : x + 1, :] == 1, soil_class[x : x + 1, :], -1)
-            padded = jnp.concatenate([f, zero], axis=0)
-            spread.append(
-                jnp.concatenate(
-                    [jnp.where(kind == e, padded, 0.0) for e in range(CLASSES)], axis=0
-                )
+        for n in range(4):
+            base[pl.ds(x0 + n, STATE, stride=X), :] = jnp.where(
+                kinds[n] >= 0, solved[0:STATE, n * Y : n * Y + Y], fields[n]
             )
-            hot.append(jnp.where(kind == entry, 0.5, 0.0))
-            fields.append(f)
-            kinds.append(kind)
-        solved, two = dot(w_all, spread), dot(w_two, hot)
-        for n in range(4):
-            here = pl.ds(x0 + n, STATE, stride=X)
-            cut = slice(n * Y, n * Y + Y)
-            base[here, :] = jnp.where(kinds[n] >= 0, solved[0:STATE, cut], fields[n])
-            water[here, :] = two[0:STATE, cut]
-            head[here, :] = two[PAD : PAD + STATE, cut]
+
+
+def unit_kernel(soil_class, land, inverse, water, head, table):
+    for e in range(CLASSES):
+        x = inverse[e]
+        table[0:STATE, e : e + 1] = x[:, 0:1]
+        table[PAD : PAD + STATE, e : e + 1] = x[:, 1:2]
+    index = soil_class[...]
+    half = 0.5 * land[...].astype(F32)
+    for i in range(STATE):
+        here = slice(i * X, i * X + X)
+        water[here, :] = half * pick(table[i : i + 1, :], index)
+        head[here, :] = half * pick(table[PAD + i : PAD + i + 1, :], index)
 
 
 def final_kernel(
@@ -395,16 +398,23 @@
     local = (
         pressure, newton_rhs, geology, saturated_conductivity, genuchten_alpha,
         genuchten_exponent, land_mask, ponding, slope_class, slope_table,
-        flow_direction,
-    )
-    cond, diag, slab, east, south = call(
+        flow_direction, soil_state.reshape(tall),
+    )
+    cond, diag, slab, east, south, state = call(
         local_kernel,
-        [block, block, (FIELDS, E - X, Y), plane, plane],
-        [(pltpu.SMEM if a.ndim == 1 else pltpu.VMEM)(a.shape, a.dtype) for a in local]
+        [block, block, (FIELDS, E - X, Y), plane, plane, tall],
+        [
+            (pltpu.SMEM if a.ndim == 1 else pltpu.VMEM)(a.shape, a.dtype)
+            for a in local[:-1]
+        ]
         + [pltpu.SemaphoreType.DMA((len(local),))],
         [pl.BlockSpec(memory_space=pltpu.HBM)] * len(local),
     )(*(pltpu.with_memory_space_constraint(a, pltpu.HBM) for a in local))
     after = back(slab, "gx")
+    (base,) = call(
+        soil_kernel, [tall], [pltpu.VMEM((PAD, 240), F32)], flops=20_000_000
+    )(state, soil_class, land_mask, soil_inverse)
+    after, base = lax.optimization_barrier((after, base))
     (packed,) = call(pack_kernel, [(E, Y)])(newton_rhs, cond, diag, after, south)
     left, right = ahead(packed, "gy"), back(packed, "gy")
     v1, v2, rows, edge = call(
@@ -416,16 +426,9 @@
     rows = everyones(rows, "gy")
     (rows,) = call(relay_kernel, [(lax.axis_size("gx"), Y)])(rows)
     rows, kinds = lax.optimization_barrier((rows, soil_class))
-    base, water, head = call(
-        soil_kernel,
-        [tall] * 3,
-        [
-            pltpu.VMEM((PAD, CLASSES * PAD), F32),
-            pltpu.VMEM((2 * PAD, 16), F32),
-        ],
-        flops=20_000_000,
-        nbytes=2_000_000,
-    )(soil_state.reshape(tall), kinds, land_mask, soil_inverse)
+    water, head = call(unit_kernel, [tall] * 2, [pltpu.VMEM((2 * PAD, Y), F32)])(
+        kinds, land_mask, soil_inverse
+    )
     rows = everyones(rows, "gx")
     return call(final_kernel, [block, plane, (STATE, X, Y)])(
         rows, newton_rhs, v1, v2, edge, base, water, head, left, east, south,

time: 55.6 us -> 55.5 us (level)
  waiting for transfers between devices: 6.16 us -> 7.91 us
  starting transfers between devices: 23.2 us -> 21.9 us
    ppermute x2, waiting for transfers between devices: 2.09 us -> 5.12 us  [ahead(): return lax.ppermute(x, axis, [(i, (i + 1) % n) for i in range(n)])]
    ppermute x2, waiting for transfers between devices: 3.57 us -> 2.3 us  [back(): return lax.ppermute(x, axis, [((i + 1) % n, i) for i in range(n)])]
    all_to_all x1, starting transfers between devices: 8.34 us -> 7.69 us  [everyones(): lax.all_to_all(rows.reshape(count, 1, Y), axis, 0, 0).reshape(count, Y)]
    ppermute x2, starting transfers between devices: 6.66 us -> 6.08 us  [ahead(): return lax.ppermute(x, axis, [(i, (i + 1) % n) for i in range(n)])]
    pallas_call x2 -> x3, Pallas kernels: 4.95 us -> 4.42 us  [the longest x1 2.29 us: on_device(): call(soil_kernel, [tall], [pltpu.VMEM((PAD, 240), F32)], flops=20000000)]
  transfers between devices with their start and end apart: 5 -> 5, of which waited for: 5 -> 4; matrix products, arithmetic and copies ran while one was open for 0% -> 0% of each run, Pallas kernels for 6% -> 5%
where the time goes in v8:
time: 55.5 us; the launch traced here: 55.2 us
  starting transfers between devices  21.9 us (39%)
  blocking collectives  16.6 us (30%)
  Pallas kernels  8 us (14%)
  waiting for transfers between devices  7.91 us (14%)
  between operations  0.77 us (1%)
    all_to_all x1, blocking collectives, everyones(): lax.all_to_all(rows.reshape(count, 1, Y), axis, 0, 0).reshape(count, Y)  16.6 us
    ppermute x2, starting transfers between devices, back(): return lax.ppermute(x, axis, [((i + 1) % n, i) for i in range(n)])  8.12 us
    all_to_all x1, starting transfers between devices, everyones(): lax.all_to_all(rows.reshape(count, 1, Y), axis, 0, 0).reshape(count, Y)  7.69 us
    ppermute x2, starting transfers between devices, ahead(): return lax.ppermute(x, axis, [(i, (i + 1) % n) for i in range(n)])  6.08 us
    ppermute x2, waiting for transfers between devices, ahead(): return lax.ppermute(x, axis, [(i, (i + 1) % n) for i in range(n)])  5.12 us
    ppermute x2, waiting for transfers between devices, back(): return lax.ppermute(x, axis, [((i + 1) % n, i) for i in range(n)])  2.3 us
    pallas_call x1, Pallas kernels, on_device(): call(soil_kernel, [tall], [pltpu.VMEM((PAD, 240), F32)], flops=20000000)  2.29 us
    pallas_call x1, Pallas kernels, on_device(): call(local_kernel, [block, block, (FIELDS, E - X, Y), plane, plane, tall]...  1.49 us
  transfers between devices with their start and end apart: 5, of which 4 were waited for; matrix products, arithmetic and copies ran while one was open for 0% of the time, Pallas kernels for 5%

profile of v8, /device:TPU:1, one launch (start us, length us, event | category | flops | bytes accessed | tf_op | source)
XLA Modules:
  0.0 55.2 jit_solution(14214362267935901902)
XLA Ops:
  0.6 0.0 copy-start.1
  0.6 0.0 copy-start.2
  0.7 0.0 copy-start.3
  0.7 1.5 %shard_map.157 = (f32[5,32,128]{2,1,0:T(8,128)S(1)}, f32[5,32,128]{2,1,0:T(8,128)S(1)}, f32[15,8,128]{2,1,0:T(8,128)S(1)}, f32[32,128]{1,0:T(8,128)S(1)}, f32[32,128]{1,0:T(8,128)S(1)}, /*index=5*/f32[640,128]{1,0:T(8,128)S(1)}) custom-call(f32[5,32,128]{2,1,0:T(8,128)} %refs_0_.1, f32[5,32,128]{2,1,0:T(8,128)} %rhs.5, s32[5,32,128]{2,1,0:T(8,128)} %refs_2_.1, ...), custom_call_target="tpu_custom_call" | custom-call | tf_op jit(solution)/shard_map/pallas_call | solution.py:403
  2.2 8.1 %collective-permute-start = (f32[15,8,128]{2,1,0:T(8,128)S(1)}, f32[15,8,128]{2,1,0:T(8,128)S(1)}, u32[]{:S(2)}, u32[]{:S(2)}) collective-permute-start(f32[15,8,128]{2,1,0:T(8,128)S(1)} %get-tuple-element.21), channel_id=1, source_target_pairs={{16,0},{32,16},{48,32},{64,48},{80,64},{96,80},{112,96},{128,112},... | collective-permute-start | bytes 184328 | tf_op jit(solution)/shard_map/ppermute | solution.py:384
  10.3 0.0 copy-done.1
  10.3 0.0 copy-done.2
  10.3 0.0 copy-done.3
  10.3 0.0 copy-start
  10.3 2.3 %shard_map.158.base = f32[640,128]{1,0:T(8,128)S(1)} custom-call(f32[640,128]{1,0:T(8,128)S(1)} %get-tuple-element.22.state, s32[32,128]{1,0:T(8,128)S(1)} %copy-done.3, s32[32,128]{1,0:T(8,128)S(1)} %copy-done.2, f32[12,20,20]{2,1,0:T(8,128)S(1)} %copy-done.1), custom_call_target="tpu_custom_call" | custom-call | flops 20000000 | tf_op jit(solution)/shard_map/pallas_call | solution.py:414
  12.6 0.0 collective-permute-done.after
  12.6 0.0 copy-done
  12.7 0.1 shard_map.159
  12.8 2.9 %collective-permute-start.2 = (f32[40,128]{1,0:T(8,128)S(1)}, f32[40,128]{1,0:T(8,128)S(1)}, u32[]{:S(2)}, u32[]{:S(2)}) collective-permute-start(f32[40,128]{1,0:T(8,128)S(1)} %shard_map.159), channel_id=1, source_target_pairs={{0,1},{1,2},{2,3},{3,4},{4,5},{5,6},{6,7},{7,8},{8,9},{9,10},{10,1... | collective-permute-start | bytes 61448 | tf_op jit(solution)/shard_map/ppermute | solution.py:379
  15.8 0.0 collective-permute-start.1
  15.8 0.9 %collective-permute-done.2.left = f32[40,128]{1,0:T(8,128)S(1)} collective-permute-done((f32[40,128]{1,0:T(8,128)S(1)}, f32[40,128]{1,0:T(8,128)S(1)}, u32[]{:S(2)}, u32[]{:S(2)}) %collective-permute-start.2) | collective-permute-done | bytes 20512 | tf_op jit(solution)/shard_map/ppermute | solution.py:379
  16.7 2.3 %collective-permute-done.1.right = f32[40,128]{1,0:T(8,128)S(1)} collective-permute-done((f32[40,128]{1,0:T(8,128)S(1)}, f32[40,128]{1,0:T(8,128)S(1)}, u32[]{:S(2)}, u32[]{:S(2)}) %collective-permute-start.1) | collective-permute-done | bytes 20512 | tf_op jit(solution)/shard_map/ppermute | solution.py:384
  19.0 1.5 %shard_map.160 = (f32[5,32,128]{2,1,0:T(8,128)S(1)}, f32[5,32,128]{2,1,0:T(8,128)S(1)}, f32[16,128]{1,0:T(8,128)S(1)}, f32[16,128]{1,0:T(8,128)S(1)}) custom-call(f32[5,32,128]{2,1,0:T(8,128)S(1)} %copy-done, f32[5,32,128]{2,1,0:T(8,128)S(1)} %get-tuple-element.19.cond, f32[5,32,128]{2,1,0:T(8,128)S(1)} %get-tuple-element.20.diag, ...), custom_call_target="tpu_custom_call" | custom-call | tf_op jit(solution)/shard_map/pallas_call | solution.py:420
  20.4 16.6 %all_to_all.10 = f32[16,1,128]{2,1,0:T(1,128)S(1)} all-to-all(f32[16,1,128]{2,1,0:T(1,128)S(1)} %bitcast.11), channel_id=1, replica_groups=mesh['gx'=32,'gy'=16] {'gy'}, dimensions={0} | all-to-all | bytes 16384 | tf_op jit(solution)/shard_map/all_to_all | solution.py:389
  37.0 0.8 %shard_map.161 = f32[32,128]{1,0:T(8,128)} custom-call(f32[16,128]{1,0:T(8,128)S(1)} %bitcast.10), custom_call_target="tpu_custom_call" | custom-call | tf_op jit(solution)/shard_map/pallas_call | solution.py:427
  37.8 7.7 %all-to-all-start.1 = ((f32[32,1,128]{2,1,0:T(1,128)}), f32[32,1,128]{2,1,0:T(1,128)S(1)}, u32[]{:S(2)}, u32[]{:S(2)}) async-start(f32[32,1,128]{2,1,0:T(1,128)} %bitcast.5), calls=%async_computation.1 | async-start | bytes 32768 | tf_op jit(solution)/shard_map/all_to_all | solution.py:389
  45.5 3.1 %collective-permute-start.3 = (f32[16,128]{1,0:T(8,128)S(1)}, f32[16,128]{1,0:T(8,128)S(1)}, u32[]{:S(2)}, u32[]{:S(2)}) collective-permute-start(f32[16,128]{1,0:T(8,128)S(1)} %get-tuple-element.30), channel_id=1, source_target_pairs={{0,16},{16,32},{32,48},{48,64},{64,80},{80,96},{96,112},{112,128},... | collective-permute-start | bytes 24584 | tf_op jit(solution)/shard_map/ppermute | solution.py:379
  48.6 0.0 copy-start.4
  48.7 0.6 %shard_map.162 = (f32[640,128]{1,0:T(8,128)S(1)}, f32[640,128]{1,0:T(8,128)S(1)}) custom-call(s32[32,128]{1,0:T(8,128)S(1)} %copy-done.3, s32[32,128]{1,0:T(8,128)S(1)} %copy-done.2, f32[12,20,20]{2,1,0:T(8,128)S(1)} %copy-done.1), custom_call_target="tpu_custom_call" | custom-call | tf_op jit(solution)/shard_map/pallas_call | solution.py:429
  49.3 4.2 %collective-permute-done.3.back = f32[16,128]{1,0:T(8,128)S(1)} collective-permute-done((f32[16,128]{1,0:T(8,128)S(1)}, f32[16,128]{1,0:T(8,128)S(1)}, u32[]{:S(2)}, u32[]{:S(2)}) %collective-permute-start.3) | collective-permute-done | bytes 8224 | tf_op jit(solution)/shard_map/ppermute | solution.py:379
  53.5 0.5 all-to-all-done.1
  54.0 0.0 copy-done.4
  54.0 1.2 %shard_map.163 = (f32[5,32,128]{2,1,0:T(8,128)}, f32[32,128]{1,0:T(8,128)}, f32[20,32,128]{2,1,0:T(8,128)}) custom-call(f32[32,128]{1,0:T(8,128)S(1)} %bitcast.9, f32[5,32,128]{2,1,0:T(8,128)S(1)} %copy-done, f32[5,32,128]{2,1,0:T(8,128)S(1)} %get-tuple-element.28.v1, f32[5,32,128]{2,1,0:T(8,128)S(1)} %get-tuple-element.29.v2, ...), custom_call_target="tpu_custom_call" | custom-call | tf_op jit(solution)/shard_map/pallas_call | solution.py:433
Async XLA Ops:
  0.6 9.7 %copy-start.1 = (f32[12,20,20]{2,1,0:T(8,128)S(1)}, f32[12,20,20]{2,1,0:T(8,128)}, u32[]{:S(2)}) copy-start(f32[12,20,20]{2,1,0:T(8,128)} %inverse.3) | copy-start | bytes 57604
  0.6 9.7 %copy-start.2 = (s32[32,128]{1,0:T(8,128)S(1)}, s32[32,128]{1,0:T(8,128)}, u32[]{:S(2)}) copy-start(s32[32,128]{1,0:T(8,128)} %land.5) | copy-start | bytes 49156
  0.7 9.7 %copy-start.3 = (s32[32,128]{1,0:T(8,128)S(1)}, s32[32,128]{1,0:T(8,128)}, u32[]{:S(2)}) copy-start(s32[32,128]{1,0:T(8,128)} %soil_class.2) | copy-start | bytes 49156
  2.2 10.5 %collective-permute-start = (f32[15,8,128]{2,1,0:T(8,128)S(1)}, f32[15,8,128]{2,1,0:T(8,128)S(1)}, u32[]{:S(2)}, u32[]{:S(2)}) collective-permute-start(f32[15,8,128]{2,1,0:T(8,128)S(1)} %get-tuple-element.21), channel_id=1, source_target_pairs={{16,0},{32,16},{48,32},{64,48},{80,64},{96,80},{112,96},{128,112},... | collective-permute-start | bytes 184328 | tf_op jit(solution)/shard_map/ppermute | solution.py:384
  10.3 2.3 %copy-start = (f32[5,32,128]{2,1,0:T(8,128)S(1)}, f32[5,32,128]{2,1,0:T(8,128)}, u32[]{:S(2)}) copy-start(f32[5,32,128]{2,1,0:T(8,128)} %rhs.5) | copy-start | bytes 245764
  12.8 3.9 %collective-permute-start.2 = (f32[40,128]{1,0:T(8,128)S(1)}, f32[40,128]{1,0:T(8,128)S(1)}, u32[]{:S(2)}, u32[]{:S(2)}) collective-permute-start(f32[40,128]{1,0:T(8,128)S(1)} %shard_map.159), channel_id=1, source_target_pairs={{0,1},{1,2},{2,3},{3,4},{4,5},{5,6},{6,7},{7,8},{8,9},{9,10},{10,1... | collective-permute-start | bytes 61448 | tf_op jit(solution)/shard_map/ppermute | solution.py:379
  15.8 3.2 %collective-permute-start.1 = (f32[40,128]{1,0:T(8,128)S(1)}, f32[40,128]{1,0:T(8,128)S(1)}, u32[]{:S(2)}, u32[]{:S(2)}) collective-permute-start(f32[40,128]{1,0:T(8,128)S(1)} %shard_map.159), channel_id=1, source_target_pairs={{1,0},{2,1},{3,2},{4,3},{5,4},{6,5},{7,6},{8,7},{9,8},{10,9},{11,1... | collective-permute-start | bytes 61448 | tf_op jit(solution)/shard_map/ppermute | solution.py:384
  37.8 16.2 %all-to-all-start.1 = ((f32[32,1,128]{2,1,0:T(1,128)}), f32[32,1,128]{2,1,0:T(1,128)S(1)}, u32[]{:S(2)}, u32[]{:S(2)}) async-start(f32[32,1,128]{2,1,0:T(1,128)} %bitcast.5), calls=%async_computation.1 | async-start | bytes 32768 | tf_op jit(solution)/shard_map/all_to_all | solution.py:389
  45.5 8.0 %collective-permute-start.3 = (f32[16,128]{1,0:T(8,128)S(1)}, f32[16,128]{1,0:T(8,128)S(1)}, u32[]{:S(2)}, u32[]{:S(2)}) collective-permute-start(f32[16,128]{1,0:T(8,128)S(1)} %get-tuple-element.30), channel_id=1, source_target_pairs={{0,16},{16,32},{32,48},{48,64},{64,80},{80,96},{96,112},{112,128},... | collective-permute-start | bytes 24584 | tf_op jit(solution)/shard_map/ppermute | solution.py:379
  48.6 5.4 %copy-start.4 = (f32[32,128]{1,0:T(8,128)S(1)}, f32[32,128]{1,0:T(8,128)}, u32[]{:S(2)}) copy-start(f32[32,128]{1,0:T(8,128)} %ponding.1) | copy-start | bytes 49156

commit v9 on v8

--- a/solution.py
+++ b/solution.py
@@ -131,24 +131,21 @@
     copies[11].wait()
 
 
-def pack_kernel(rhs, cond, diag, after, south, packed):
+def pack_kernel(rhs, cond, diag, after, packed):
     for lo, rows in ((0, X), (X, E - X)):
         lane = iota((rows, Y), 1)
         total = jnp.zeros((rows, Y), F32)
         for f, ref in enumerate((rhs, cond, diag)):
             for l in range(LAYERS):
                 q = f * LAYERS + l
-                x = pltpu.roll(after[q] if lo else ref[l], (W + G * q) % Y, 1)
+                x = pltpu.roll(after[q] if lo else ref[l], (G * q) % Y, 1)
                 total = jnp.where((lane >= G * q) & (lane < G * q + G), x, total)
-        if not lo:
-            x = pltpu.roll(south[...], (W + G * FIELDS) % Y, 1)
-            total = jnp.where(lane >= G * FIELDS, x, total)
         packed[lo : lo + rows, :] = total
 
 
 def krylov_kernel(
-    rhs, cond, diag, after, right, left, east, v1_out, v2_out, row_out, back_out,
-    fr, fc, fv, dd, v,
+    rhs, cond, diag, after, right, east, south, v1_out, v2_out, row_out, back_out,
+    strip_out, fr, fc, fv, dd, v,
 ):
     lane, row_of = iota((E, Y), 1), iota((E, Y), 0)
     first, last = lane == 0, lane == Y - 1
@@ -156,7 +153,7 @@
     x_end, y_end = x == lax.axis_size("gx") - 1, y == lax.axis_size("gy") - 1
     closed_rows = (row_of == 0) | (row_of == jnp.where(x_end, X, 0))
     closed_lanes = (
-        lane == jnp.where(y == 0, 0, -1),
+        lane == 0,
         lane == jnp.where(y_end, 0, -1),
     )
 
@@ -164,13 +161,13 @@
         m, h = pltpu.roll(m, by, 1), pltpu.roll(h, by, 1)
         return jnp.where(edge, h, m), jnp.where(edge, m, h)
 
-    w = jnp.where(lane % G >= W, right[...], left[...])
+    w = right[...]
 
     def both(ref, f, l):
         q = f * LAYERS + l
         return (
             jnp.concatenate([ref[l], after[q]], axis=0),
-            pltpu.roll(w, (-(W + G * q)) % Y, 1),
+            pltpu.roll(w, (-G * q) % Y, 1),
         )
 
     def harmonic(a, b):
@@ -186,7 +183,7 @@
             fr[s, l] = jnp.where(
                 closed_rows, 0.0, harmonic(k[s], pltpu.roll(k[s], 1, 0))
             )
-            fc[s, l] = jnp.where(closed_lanes[s], 0.0, harmonic(k[s], west[s]))
+            fc[s, l] = harmonic(k[s], west[s])
             if l:
                 fv[s, l - 1] = harmonic(k[s], above[s])
         above = k
@@ -194,7 +191,10 @@
     def product(l, flux_above):
         vm, vh = v[0, l], v[1, l]
         west = turn(vm, vh, 1, first)
-        side = fc[0, l] * (vm - west[0]), fc[1, l] * (vh - west[1])
+        side = [
+            jnp.where(closed_lanes[s], 0.0, fc[s, l] * (x - west[s]))
+            for s, x in enumerate((vm, vh))
+        ]
         gone = turn(*side, Y - 1, last)
         outs, flux = [], []
         for s, x in enumerate((vm, vh)):
@@ -219,29 +219,46 @@
         s, e2 = two_sum(sums[j][0], p)
         sums[j] = s, sums[j][1] + (e + e2)
 
+    def count(step, old, new):
+        for i in range(0, E, 8):
+            a, b = old[i : i + 8], new[i : i + 8]
+            if i == 0 or i == X:
+                keep = sub >= start if i == 0 else sub < stop
+                a, b = jnp.where(keep, a, 0.0), jnp.where(keep, b, 0.0)
+            add_to(2 * step, a, a)
+            add_to(2 * step + 1, a, b)
+
+    def counted(m, h):
+        return jnp.where(lane >= W, m, jnp.where(y_end, 0.0, h))
+
+    strip = jnp.zeros((E, Y), F32)
     for step in range(3):
         results, flux = [], None
+        head = [jnp.zeros((E, Y), F32)] * 2
         for l in range(LAYERS):
             outs, flux = product(l, flux)
-            old, new = v[0, l], outs[0]
-            for i in range(0, E, 8):
-                a, b = old[i : i + 8], new[i : i + 8]
-                if i == 0 or i == X:
-                    keep = sub >= start if i == 0 else sub < stop
-                    a, b = jnp.where(keep, a, 0.0), jnp.where(keep, b, 0.0)
-                add_to(2 * step, a, a)
-                add_to(2 * step + 1, a, b)
+            old, new = (v[0, l], v[1, l]), outs
+            count(step, counted(*old), counted(*new))
+            here = (lane >= W * l) & (lane < W * l + W) & (y == 0)
+            head = [
+                jnp.where(here, pltpu.roll(t[0], W * l, 1), h)
+                for t, h in zip((old, new), head)
+            ]
             results.append(outs)
+        count(step, *head)
         if step < 2:
             for l in range(LAYERS):
-                m = results[l][0]
-                v[0, l], v[1, l] = results[l]
+                m, h = results[l]
+                v[0, l], v[1, l] = m, h
                 (v1_out, v2_out)[step][l] = m[0:X]
-                if step:
-                    back_out[LAYERS + 2 * l : LAYERS + 2 * l + 2, :] = m[X : X + 2]
-                else:
-                    back_out[l : l + 1, :] = m[X : X + 1]
+                q, n = (LAYERS + 2 * l, 2) if step else (l, 1)
+                back_out[q : q + n, :] = m[X : X + n]
+                strip = jnp.where(
+                    (lane >= q) & (lane < q + n), pltpu.roll(h, q, 1), strip
+                )
     back_out[3 * LAYERS : 3 * LAYERS + 1, :] = east[X - 1 : X, :]
+    back_out[16:24, :] = strip[X:E]
+    strip_out[...] = jnp.where(lane[0:X] == Y - 1, south[...], strip[0:X])
 
     ln = iota((8, Y), 1)
     total = zero, zero
@@ -271,7 +288,13 @@
     return renorm(*fold(parts[0], (4, 2, 1), 0))
 
 
-def relay_kernel(rows, row_out):
+def relay_kernel(rows, edge, strip, row_out, west_out):
+    row, lane = iota((X, Y), 0), iota((X, Y), 1)
+    given = jnp.where(lax.axis_index("gx") == 0, 0, 3 * LAYERS)
+    west = jnp.where((row == 0) & (lane < given), edge[16:17, :], strip[...])
+    west_out[...] = jnp.where(
+        (row == 1) & (lane >= LAYERS) & (lane < given), edge[17:18, :], west
+    )
     hi, lo = rows_total(rows)
     ln = iota((8, Y), 1)
     both = jnp.where(ln < 8, hi, pltpu.roll(lo, 8, 1))
@@ -325,7 +348,7 @@
 
 
 def final_kernel(
-    rows, rhs, v1, v2, back, base, water, head, left, east, south, ponding, land,
+    rows, rhs, v1, v2, back, base, water, head, strip, east, south, ponding, land,
     corr_out, pond_out, soil_out,
 ):
     hi, lo = rows_total(rows)
@@ -350,22 +373,25 @@
 
     row, lane = iota((X, Y), 0), iota((X, Y), 1)
     es, so = east[...], south[...]
-    north = pltpu.roll(left[0:X, :], (-(W + G * FIELDS)) % Y, 1)
+    side = strip[...]
     given = jnp.where(lax.axis_index("gx") == 0, 0, 1)
     west = jnp.where(given == 0, 0.0, back[3 * LAYERS : 3 * LAYERS + 1, :])
-    north = jnp.where(lax.axis_index("gy") == 0, 0.0, pltpu.roll(north, 1, 1))
+    north = jnp.where(lax.axis_index("gy") == 0, 0.0, pltpu.roll(side, 1, 1))
     inflow = jnp.where(row == 0, west, pltpu.roll(es, 1, 0)) + jnp.where(
         lane == 0, north, pltpu.roll(so, 1, 1)
     )
     pond = land[...].astype(F32) * (ponding[...] + 0.2 * (inflow - (es + so)))
     pond_out[...] = pond
 
+    lanes = jnp.where(lax.axis_index("gy") == 0, 0, 1)
     top = None
     for l in range(LAYERS):
         q = LAYERS + 2 * l
         a1 = jnp.where(row < given, back[l : l + 1, :], v1[l])
         a2 = jnp.where(row < given, back[q : q + 1, :], v2[l])
         a2 = jnp.where((row == 1) & (given > 0), back[q + 1 : q + 2, :], a2)
+        a1 = jnp.where(lane < lanes, pltpu.roll(side, (-l) % Y, 1), a1)
+        a2 = jnp.where(lane < 2 * lanes, pltpu.roll(side, (-q) % Y, 1), a2)
         x = c1 * rhs[l] + c2 * a1 + c3 * a2
         corr_out[l] = x
         top = x if top is None else top
@@ -415,23 +441,26 @@
         soil_kernel, [tall], [pltpu.VMEM((PAD, 240), F32)], flops=20_000_000
     )(state, soil_class, land_mask, soil_inverse)
     after, base = lax.optimization_barrier((after, base))
-    (packed,) = call(pack_kernel, [(E, Y)])(newton_rhs, cond, diag, after, south)
-    left, right = ahead(packed, "gy"), back(packed, "gy")
-    v1, v2, rows, edge = call(
+    (packed,) = call(pack_kernel, [(E, Y)])(newton_rhs, cond, diag, after)
+    right = back(packed, "gy")
+    v1, v2, rows, edge, strip = call(
         krylov_kernel,
-        [block, block, (lax.axis_size("gy"), Y), (16, Y)],
+        [block, block, (lax.axis_size("gy"), Y), (24, Y), plane],
         [pltpu.VMEM((2, n, E, Y), F32) for n in (5, 5, 4, 5, 5)],
-    )(newton_rhs, cond, diag, after, right, left, east)
+    )(newton_rhs, cond, diag, after, right, east, south)
     edge = ahead(edge, "gx")
     rows = everyones(rows, "gy")
-    (rows,) = call(relay_kernel, [(lax.axis_size("gx"), Y)])(rows)
-    rows, kinds = lax.optimization_barrier((rows, soil_class))
     water, head = call(unit_kernel, [tall] * 2, [pltpu.VMEM((2 * PAD, Y), F32)])(
-        kinds, land_mask, soil_inverse
-    )
+        soil_class, land_mask, soil_inverse
+    )
+    rows, edge, water, head = lax.optimization_barrier((rows, edge, water, head))
+    rows, strip = call(relay_kernel, [(lax.axis_size("gx"), Y), plane])(
+        rows, edge, strip
+    )
+    strip = ahead(strip, "gy")
     rows = everyones(rows, "gx")
     return call(final_kernel, [block, plane, (STATE, X, Y)])(
-        rows, newton_rhs, v1, v2, edge, base, water, head, left, east, south,
+        rows, newton_rhs, v1, v2, edge, base, water, head, strip, east, south,
         ponding, land_mask,
     )
 

time: 55.5 us -> 54.7 us (0.986)
  blocking collectives: 16.6 us -> 0 us
  starting transfers between devices: 21.9 us -> 30.4 us
  waiting for transfers between devices: 7.91 us -> 14.4 us
  Pallas kernels: 8 us -> 8.83 us
    all_to_all x1 -> x0, blocking collectives: 16.6 us -> none  [everyones(): lax.all_to_all(rows.reshape(count, 1, Y), axis, 0, 0).reshape(count, Y)]
    all_to_all x1 -> x2, starting transfers between devices: 7.69 us -> 16.6 us  [everyones(): lax.all_to_all(rows.reshape(count, 1, Y), axis, 0, 0).reshape(count, Y)]
    all_to_all x1 -> x2, waiting for transfers between devices: 0.5 us -> 6.39 us  [everyones(): lax.all_to_all(rows.reshape(count, 1, Y), axis, 0, 0).reshape(count, Y)]
    ppermute x2, starting transfers between devices: 6.08 us -> 3.16 us  [ahead(): return lax.ppermute(x, axis, [(i, (i + 1) % n) for i in range(n)])]
    ppermute x2, starting transfers between devices: 8.12 us -> 10.6 us  [back(): return lax.ppermute(x, axis, [((i + 1) % n, i) for i in range(n)])]
    ppermute x2, waiting for transfers between devices: 5.12 us -> 6.09 us  [ahead(): return lax.ppermute(x, axis, [(i, (i + 1) % n) for i in range(n)])]
    pallas_call x3, Pallas kernels: 2.36 us -> 3.18 us  [the longest x1 2.28 us: on_device(): call(krylov_kernel, [block, block, (lax.axis_size('gy'), Y), (24, Y), pla...]
  transfers between devices with their start and end apart: 5 -> 6, of which waited for: 4 -> 4; matrix products, arithmetic and copies ran while one was open for 0% -> 0% of each run, Pallas kernels for 5% -> 5%
where the time goes in v9:
time: 54.7 us; the launch traced here: 54.4 us
  starting transfers between devices  30.4 us (56%)
  waiting for transfers between devices  14.4 us (26%)
  Pallas kernels  8.83 us (16%)
  between operations  0.76 us (1%)
    all_to_all x2, starting transfers between devices, everyones(): lax.all_to_all(rows.reshape(count, 1, Y), axis, 0, 0).reshape(count, Y)  16.6 us
    ppermute x2, starting transfers between devices, back(): return lax.ppermute(x, axis, [((i + 1) % n, i) for i in range(n)])  10.6 us
    all_to_all x2, waiting for transfers between devices, everyones(): lax.all_to_all(rows.reshape(count, 1, Y), axis, 0, 0).reshape(count, Y)  6.39 us
    ppermute x2, waiting for transfers between devices, ahead(): return lax.ppermute(x, axis, [(i, (i + 1) % n) for i in range(n)])  6.09 us
    ppermute x2, starting transfers between devices, ahead(): return lax.ppermute(x, axis, [(i, (i + 1) % n) for i in range(n)])  3.16 us
    pallas_call x1, Pallas kernels, on_device(): call(soil_kernel, [tall], [pltpu.VMEM((PAD, 240), F32)], flops=20000000)  2.29 us
    pallas_call x1, Pallas kernels, on_device(): call(krylov_kernel, [block, block, (lax.axis_size('gy'), Y), (24, Y), pla...  2.28 us
    ppermute x2, waiting for transfers between devices, back(): return lax.ppermute(x, axis, [((i + 1) % n, i) for i in range(n)])  1.9 us
  transfers between devices with their start and end apart: 6, of which 4 were waited for; matrix products, arithmetic and copies ran while one was open for 0% of the time, Pallas kernels for 5%

profile of v9, /device:TPU:1, one launch (start us, length us, event | category | flops | bytes accessed | tf_op | source)
XLA Modules:
  0.0 54.4 jit_solution(17820498641320210126)
XLA Ops:
  0.6 0.0 copy-start.1
  0.6 0.0 copy-start.2
  0.7 0.0 copy-start.3
  0.7 1.5 %shard_map.157 = (f32[5,32,128]{2,1,0:T(8,128)S(1)}, f32[5,32,128]{2,1,0:T(8,128)S(1)}, f32[15,8,128]{2,1,0:T(8,128)S(1)}, f32[32,128]{1,0:T(8,128)S(1)}, f32[32,128]{1,0:T(8,128)S(1)}, /*index=5*/f32[640,128]{1,0:T(8,128)S(1)}) custom-call(f32[5,32,128]{2,1,0:T(8,128)} %refs_0_.1, f32[5,32,128]{2,1,0:T(8,128)} %rhs.5, s32[5,32,128]{2,1,0:T(8,128)} %refs_2_.1, ...), custom_call_target="tpu_custom_call" | custom-call | tf_op jit(solution)/shard_map/pallas_call | solution.py:429
  2.2 8.1 %collective-permute-start = (f32[15,8,128]{2,1,0:T(8,128)S(1)}, f32[15,8,128]{2,1,0:T(8,128)S(1)}, u32[]{:S(2)}, u32[]{:S(2)}) collective-permute-start(f32[15,8,128]{2,1,0:T(8,128)S(1)} %get-tuple-element.26), channel_id=1, source_target_pairs={{16,0},{32,16},{48,32},{64,48},{80,64},{96,80},{112,96},{128,112},... | collective-permute-start | bytes 184328 | tf_op jit(solution)/shard_map/ppermute | solution.py:410
  10.3 0.0 copy-done.1
  10.3 0.0 copy-done.2
  10.3 0.0 copy-done.3
  10.3 0.0 copy-start
  10.3 2.3 %shard_map.158.base = f32[640,128]{1,0:T(8,128)S(1)} custom-call(f32[640,128]{1,0:T(8,128)S(1)} %get-tuple-element.27.state, s32[32,128]{1,0:T(8,128)S(1)} %copy-done.3, s32[32,128]{1,0:T(8,128)S(1)} %copy-done.2, f32[12,20,20]{2,1,0:T(8,128)S(1)} %copy-done.1), custom_call_target="tpu_custom_call" | custom-call | flops 20000000 | tf_op jit(solution)/shard_map/pallas_call | solution.py:440
  12.6 0.0 collective-permute-done.after
  12.6 0.0 copy-done
  12.7 0.1 shard_map.159
  12.8 2.5 %collective-permute-start.1 = (f32[40,128]{1,0:T(8,128)S(1)}, f32[40,128]{1,0:T(8,128)S(1)}, u32[]{:S(2)}, u32[]{:S(2)}) collective-permute-start(f32[40,128]{1,0:T(8,128)S(1)} %shard_map.159), channel_id=1, source_target_pairs={{1,0},{2,1},{3,2},{4,3},{5,4},{6,5},{7,6},{8,7},{9,8},{10,9},{11,1... | collective-permute-start | bytes 61448 | tf_op jit(solution)/shard_map/ppermute | solution.py:410
  15.3 1.9 %collective-permute-done.1.right = f32[40,128]{1,0:T(8,128)S(1)} collective-permute-done((f32[40,128]{1,0:T(8,128)S(1)}, f32[40,128]{1,0:T(8,128)S(1)}, u32[]{:S(2)}, u32[]{:S(2)}) %collective-permute-start.1) | collective-permute-done | bytes 20512 | tf_op jit(solution)/shard_map/ppermute | solution.py:410
  17.2 2.3 %shard_map.160 = (f32[5,32,128]{2,1,0:T(8,128)S(1)}, f32[5,32,128]{2,1,0:T(8,128)S(1)}, f32[16,128]{1,0:T(8,128)}, f32[24,128]{1,0:T(8,128)S(1)}, f32[32,128]{1,0:T(8,128)S(1)}) custom-call(f32[5,32,128]{2,1,0:T(8,128)S(1)} %copy-done, f32[5,32,128]{2,1,0:T(8,128)S(1)} %get-tuple-element.24.cond, f32[5,32,128]{2,1,0:T(8,128)S(1)} %get-tuple-element.25.diag, ...), custom_call_target="tpu_custom_call" | custom-call | tf_op jit(solution)/shard_map/pallas_call | solution.py:446
  19.5 10.5 %all-to-all-start = ((f32[16,1,128]{2,1,0:T(1,128)}), f32[16,1,128]{2,1,0:T(1,128)S(1)}, u32[]{:S(2)}, u32[]{:S(2)}) async-start(f32[16,1,128]{2,1,0:T(1,128)} %bitcast.2), calls=%async_computation | async-start | bytes 16384 | tf_op jit(solution)/shard_map/all_to_all | solution.py:415
  29.9 1.9 %collective-permute-start.2 = (f32[24,128]{1,0:T(8,128)S(1)}, f32[24,128]{1,0:T(8,128)S(1)}, u32[]{:S(2)}, u32[]{:S(2)}) collective-permute-start(f32[24,128]{1,0:T(8,128)S(1)} %get-tuple-element.32), channel_id=1, source_target_pairs={{0,16},{16,32},{32,48},{48,64},{64,80},{80,96},{96,112},{112,128},... | collective-permute-start | bytes 36872 | tf_op jit(solution)/shard_map/ppermute | solution.py:405
  31.9 0.6 %shard_map.161 = (f32[640,128]{1,0:T(8,128)S(1)}, f32[640,128]{1,0:T(8,128)S(1)}) custom-call(s32[32,128]{1,0:T(8,128)S(1)} %copy-done.3, s32[32,128]{1,0:T(8,128)S(1)} %copy-done.2, f32[12,20,20]{2,1,0:T(8,128)S(1)} %copy-done.1), custom_call_target="tpu_custom_call" | custom-call | tf_op jit(solution)/shard_map/pallas_call | solution.py:453
  32.5 5.2 %collective-permute-done.2.edge.back = f32[24,128]{1,0:T(8,128)S(1)} collective-permute-done((f32[24,128]{1,0:T(8,128)S(1)}, f32[24,128]{1,0:T(8,128)S(1)}, u32[]{:S(2)}, u32[]{:S(2)}) %collective-permute-start.2) | collective-permute-done | bytes 12320 | tf_op jit(solution)/shard_map/ppermute | solution.py:405
  37.7 0.0 all-to-all-done
  37.7 0.8 %shard_map.162 = (f32[32,128]{1,0:T(8,128)}, f32[32,128]{1,0:T(8,128)S(1)}) custom-call(f32[16,128]{1,0:T(8,128)S(1)} %bitcast.10, f32[24,128]{1,0:T(8,128)S(1)} %collective-permute-done.2.edge.back, f32[32,128]{1,0:T(8,128)S(1)} %get-tuple-element.37.strip), custom_call_target="tpu_custom_call" | custom-call | tf_op jit(solution)/shard_map/pallas_call | solution.py:457
  38.5 0.0 copy-start.4
  38.5 6.1 %all-to-all-start.1 = ((f32[32,1,128]{2,1,0:T(1,128)}), f32[32,1,128]{2,1,0:T(1,128)S(1)}, u32[]{:S(2)}, u32[]{:S(2)}) async-start(f32[32,1,128]{2,1,0:T(1,128)} %bitcast.5), calls=%async_computation.1 | async-start | bytes 32768 | tf_op jit(solution)/shard_map/all_to_all | solution.py:415
  44.6 1.3 %collective-permute-start.3 = (f32[32,128]{1,0:T(8,128)S(1)}, f32[32,128]{1,0:T(8,128)S(1)}, u32[]{:S(2)}, u32[]{:S(2)}) collective-permute-start(f32[32,128]{1,0:T(8,128)S(1)} %get-tuple-element.44), channel_id=1, source_target_pairs={{0,1},{1,2},{2,3},{3,4},{4,5},{5,6},{6,7},{7,8},{8,9},{9,10},{10,1... | collective-permute-start | bytes 49160 | tf_op jit(solution)/shard_map/ppermute | solution.py:405
  45.9 0.9 %collective-permute-done.3.strip = f32[32,128]{1,0:T(8,128)S(1)} collective-permute-done((f32[32,128]{1,0:T(8,128)S(1)}, f32[32,128]{1,0:T(8,128)S(1)}, u32[]{:S(2)}, u32[]{:S(2)}) %collective-permute-start.3) | collective-permute-done | bytes 16416 | tf_op jit(solution)/shard_map/ppermute | solution.py:405
  46.7 6.4 %all-to-all-done.1 = f32[32,1,128]{2,1,0:T(1,128)S(1)} async-done(((f32[32,1,128]{2,1,0:T(1,128)}), f32[32,1,128]{2,1,0:T(1,128)S(1)}, u32[]{:S(2)}, u32[]{:S(2)}) %all-to-all-start.1) | async-done | bytes 16416 | tf_op jit(solution)/shard_map/all_to_all | solution.py:415
  53.1 0.0 copy-done.4
  53.1 1.2 %shard_map.163 = (f32[5,32,128]{2,1,0:T(8,128)}, f32[32,128]{1,0:T(8,128)}, f32[20,32,128]{2,1,0:T(8,128)}) custom-call(f32[32,128]{1,0:T(8,128)S(1)} %bitcast.9, f32[5,32,128]{2,1,0:T(8,128)S(1)} %copy-done, f32[5,32,128]{2,1,0:T(8,128)S(1)} %get-tuple-element.39.v1, f32[5,32,128]{2,1,0:T(8,128)S(1)} %get-tuple-element.40.v2, ...), custom_call_target="tpu_custom_call" | custom-call | tf_op jit(solution)/shard_map/pallas_call | solution.py:462
Async XLA Ops:
  0.6 9.7 %copy-start.1 = (f32[12,20,20]{2,1,0:T(8,128)S(1)}, f32[12,20,20]{2,1,0:T(8,128)}, u32[]{:S(2)}) copy-start(f32[12,20,20]{2,1,0:T(8,128)} %inverse.3) | copy-start | bytes 57604
  0.6 9.7 %copy-start.2 = (s32[32,128]{1,0:T(8,128)S(1)}, s32[32,128]{1,0:T(8,128)}, u32[]{:S(2)}) copy-start(s32[32,128]{1,0:T(8,128)} %land.5) | copy-start | bytes 49156
  0.7 9.7 %copy-start.3 = (s32[32,128]{1,0:T(8,128)S(1)}, s32[32,128]{1,0:T(8,128)}, u32[]{:S(2)}) copy-start(s32[32,128]{1,0:T(8,128)} %soil_class.3) | copy-start | bytes 49156
  2.2 10.5 %collective-permute-start = (f32[15,8,128]{2,1,0:T(8,128)S(1)}, f32[15,8,128]{2,1,0:T(8,128)S(1)}, u32[]{:S(2)}, u32[]{:S(2)}) collective-permute-start(f32[15,8,128]{2,1,0:T(8,128)S(1)} %get-tuple-element.26), channel_id=1, source_target_pairs={{16,0},{32,16},{48,32},{64,48},{80,64},{96,80},{112,96},{128,112},... | collective-permute-start | bytes 184328 | tf_op jit(solution)/shard_map/ppermute | solution.py:410
  10.3 2.3 %copy-start = (f32[5,32,128]{2,1,0:T(8,128)S(1)}, f32[5,32,128]{2,1,0:T(8,128)}, u32[]{:S(2)}) copy-start(f32[5,32,128]{2,1,0:T(8,128)} %rhs.5) | copy-start | bytes 245764
  12.8 4.4 %collective-permute-start.1 = (f32[40,128]{1,0:T(8,128)S(1)}, f32[40,128]{1,0:T(8,128)S(1)}, u32[]{:S(2)}, u32[]{:S(2)}) collective-permute-start(f32[40,128]{1,0:T(8,128)S(1)} %shard_map.159), channel_id=1, source_target_pairs={{1,0},{2,1},{3,2},{4,3},{5,4},{6,5},{7,6},{8,7},{9,8},{10,9},{11,1... | collective-permute-start | bytes 61448 | tf_op jit(solution)/shard_map/ppermute | solution.py:410
  19.5 18.2 %all-to-all-start = ((f32[16,1,128]{2,1,0:T(1,128)}), f32[16,1,128]{2,1,0:T(1,128)S(1)}, u32[]{:S(2)}, u32[]{:S(2)}) async-start(f32[16,1,128]{2,1,0:T(1,128)} %bitcast.2), calls=%async_computation | async-start | bytes 16384 | tf_op jit(solution)/shard_map/all_to_all | solution.py:415
  29.9 7.8 %collective-permute-start.2 = (f32[24,128]{1,0:T(8,128)S(1)}, f32[24,128]{1,0:T(8,128)S(1)}, u32[]{:S(2)}, u32[]{:S(2)}) collective-permute-start(f32[24,128]{1,0:T(8,128)S(1)} %get-tuple-element.32), channel_id=1, source_target_pairs={{0,16},{16,32},{32,48},{48,64},{64,80},{80,96},{96,112},{112,128},... | collective-permute-start | bytes 36872 | tf_op jit(solution)/shard_map/ppermute | solution.py:405
  38.5 14.6 %copy-start.4 = (f32[32,128]{1,0:T(8,128)S(1)}, f32[32,128]{1,0:T(8,128)}, u32[]{:S(2)}) copy-start(f32[32,128]{1,0:T(8,128)} %ponding.1) | copy-start | bytes 49156
  38.5 14.6 %all-to-all-start.1 = ((f32[32,1,128]{2,1,0:T(1,128)}), f32[32,1,128]{2,1,0:T(1,128)S(1)}, u32[]{:S(2)}, u32[]{:S(2)}) async-start(f32[32,1,128]{2,1,0:T(1,128)} %bitcast.5), calls=%async_computation.1 | async-start | bytes 32768 | tf_op jit(solution)/shard_map/all_to_all | solution.py:415
  44.6 2.1 %collective-permute-start.3 = (f32[32,128]{1,0:T(8,128)S(1)}, f32[32,128]{1,0:T(8,128)S(1)}, u32[]{:S(2)}, u32[]{:S(2)}) collective-permute-start(f32[32,128]{1,0:T(8,128)S(1)} %get-tuple-element.44), channel_id=1, source_target_pairs={{0,1},{1,2},{2,3},{3,4},{4,5},{5,6},{6,7},{7,8},{8,9},{9,10},{10,1... | collective-permute-start | bytes 49160 | tf_op jit(solution)/shard_map/ppermute | solution.py:405

commit v10 on v9

--- a/solution.py
+++ b/solution.py
@@ -58,9 +58,7 @@
 def pair_div(a, b):
     q = a[0] / b[0]
     r = pair_sub(a, pair_mul((q, jnp.zeros_like(q)), b))
-    q2 = r[0] / b[0]
-    r = pair_sub(r, pair_mul((q2, jnp.zeros_like(q)), b))
-    return pair_add(renorm(q, q2), (r[0] / b[0], jnp.zeros_like(q)))
+    return renorm(q, r[0] / b[0])
 
 
 def iota(shape, dim):
@@ -437,12 +435,12 @@
         [pl.BlockSpec(memory_space=pltpu.HBM)] * len(local),
     )(*(pltpu.with_memory_space_constraint(a, pltpu.HBM) for a in local))
     after = back(slab, "gx")
-    (base,) = call(
-        soil_kernel, [tall], [pltpu.VMEM((PAD, 240), F32)], flops=20_000_000
-    )(state, soil_class, land_mask, soil_inverse)
-    after, base = lax.optimization_barrier((after, base))
     (packed,) = call(pack_kernel, [(E, Y)])(newton_rhs, cond, diag, after)
     right = back(packed, "gy")
+    water, head = call(unit_kernel, [tall] * 2, [pltpu.VMEM((2 * PAD, Y), F32)])(
+        soil_class, land_mask, soil_inverse
+    )
+    right, water, head = lax.optimization_barrier((right, water, head))
     v1, v2, rows, edge, strip = call(
         krylov_kernel,
         [block, block, (lax.axis_size("gy"), Y), (24, Y), plane],
@@ -450,14 +448,14 @@
     )(newton_rhs, cond, diag, after, right, east, south)
     edge = ahead(edge, "gx")
     rows = everyones(rows, "gy")
-    water, head = call(unit_kernel, [tall] * 2, [pltpu.VMEM((2 * PAD, Y), F32)])(
-        soil_class, land_mask, soil_inverse
-    )
-    rows, edge, water, head = lax.optimization_barrier((rows, edge, water, head))
     rows, strip = call(relay_kernel, [(lax.axis_size("gx"), Y), plane])(
         rows, edge, strip
     )
     strip = ahead(strip, "gy")
+    rows, kinds = lax.optimization_barrier((rows, soil_class))
+    (base,) = call(
+        soil_kernel, [tall], [pltpu.VMEM((PAD, 240), F32)], flops=20_000_000
+    )(state, kinds, land_mask, soil_inverse)
     rows = everyones(rows, "gx")
     return call(final_kernel, [block, plane, (STATE, X, Y)])(
         rows, newton_rhs, v1, v2, edge, base, water, head, strip, east, south,

time: 54.7 us -> 54.4 us (level)
  waiting for transfers between devices: 14.4 us -> 13.3 us
  starting transfers between devices: 30.4 us -> 31.4 us
    all_to_all x2, waiting for transfers between devices: 6.39 us -> 5.1 us  [everyones(): lax.all_to_all(rows.reshape(count, 1, Y), axis, 0, 0).reshape(count, Y)]
    ppermute x2, starting transfers between devices: 10.6 us -> 11.7 us  [back(): return lax.ppermute(x, axis, [((i + 1) % n, i) for i in range(n)])]
where the time goes in v10:
time: 54.4 us; the launch traced here: 54.1 us
  starting transfers between devices  31.4 us (58%)
  waiting for transfers between devices  13.3 us (24%)
  Pallas kernels  8.71 us (16%)
  between operations  0.71 us (1%)
    all_to_all x2, starting transfers between devices, everyones(): lax.all_to_all(rows.reshape(count, 1, Y), axis, 0, 0).reshape(count, Y)  16.7 us
    ppermute x2, starting transfers between devices, back(): return lax.ppermute(x, axis, [((i + 1) % n, i) for i in range(n)])  11.7 us
    ppermute x2, waiting for transfers between devices, ahead(): return lax.ppermute(x, axis, [(i, (i + 1) % n) for i in range(n)])  6.16 us
    all_to_all x2, waiting for transfers between devices, everyones(): lax.all_to_all(rows.reshape(count, 1, Y), axis, 0, 0).reshape(count, Y)  5.1 us
    ppermute x2, starting transfers between devices, ahead(): return lax.ppermute(x, axis, [(i, (i + 1) % n) for i in range(n)])  3.01 us
    pallas_call x1, Pallas kernels, on_device(): call(soil_kernel, [tall], [pltpu.VMEM((PAD, 240), F32)], flops=20000000)  2.29 us
    pallas_call x1, Pallas kernels, on_device(): call(krylov_kernel, [block, block, (lax.axis_size('gy'), Y), (24, Y), pla...  2.28 us
    ppermute x2, waiting for transfers between devices, back(): return lax.ppermute(x, axis, [((i + 1) % n, i) for i in range(n)])  2 us
  transfers between devices with their start and end apart: 6, of which 4 were waited for; matrix products, arithmetic and copies ran while one was open for 0% of the time, Pallas kernels for 5%

profile of v10, /device:TPU:1, one launch (start us, length us, event | category | flops | bytes accessed | tf_op | source)
XLA Modules:
  0.0 54.1 jit_solution(11564173967590179950)
XLA Ops:
  0.6 0.0 copy-start
  0.6 1.5 %shard_map.157 = (f32[5,32,128]{2,1,0:T(8,128)S(1)}, f32[5,32,128]{2,1,0:T(8,128)S(1)}, f32[15,8,128]{2,1,0:T(8,128)S(1)}, f32[32,128]{1,0:T(8,128)S(1)}, f32[32,128]{1,0:T(8,128)S(1)}, /*index=5*/f32[640,128]{1,0:T(8,128)S(1)}) custom-call(f32[5,32,128]{2,1,0:T(8,128)} %refs_0_.1, f32[5,32,128]{2,1,0:T(8,128)} %rhs.5, s32[5,32,128]{2,1,0:T(8,128)} %refs_2_.1, ...), custom_call_target="tpu_custom_call" | custom-call | tf_op jit(solution)/shard_map/pallas_call | solution.py:427
  2.1 8.1 %collective-permute-start = (f32[15,8,128]{2,1,0:T(8,128)S(1)}, f32[15,8,128]{2,1,0:T(8,128)S(1)}, u32[]{:S(2)}, u32[]{:S(2)}) collective-permute-start(f32[15,8,128]{2,1,0:T(8,128)S(1)} %get-tuple-element.25), channel_id=1, source_target_pairs={{16,0},{32,16},{48,32},{64,48},{80,64},{96,80},{112,96},{128,112},... | collective-permute-start | bytes 184328 | tf_op jit(solution)/shard_map/ppermute | solution.py:408
  10.2 1.3 %collective-permute-done.after = f32[15,8,128]{2,1,0:T(8,128)S(1)} collective-permute-done((f32[15,8,128]{2,1,0:T(8,128)S(1)}, f32[15,8,128]{2,1,0:T(8,128)S(1)}, u32[]{:S(2)}, u32[]{:S(2)}) %collective-permute-start) | collective-permute-done | bytes 61472 | tf_op jit(solution)/shard_map/ppermute | solution.py:408
  11.5 0.0 copy-done
  11.5 0.0 copy-start.1
  11.5 0.0 copy-start.2
  11.5 0.0 copy-start.3
  11.5 0.1 shard_map.158
  11.7 3.6 %collective-permute-start.1 = (f32[40,128]{1,0:T(8,128)S(1)}, f32[40,128]{1,0:T(8,128)S(1)}, u32[]{:S(2)}, u32[]{:S(2)}) collective-permute-start(f32[40,128]{1,0:T(8,128)S(1)} %shard_map.158), channel_id=1, source_target_pairs={{1,0},{2,1},{3,2},{4,3},{5,4},{6,5},{7,6},{8,7},{9,8},{10,9},{11,1... | collective-permute-start | bytes 61448 | tf_op jit(solution)/shard_map/ppermute | solution.py:408
  15.3 0.0 copy-done.1
  15.3 0.0 copy-done.2
  15.3 0.0 copy-done.3
  15.3 0.6 %shard_map.159 = (f32[640,128]{1,0:T(8,128)S(1)}, f32[640,128]{1,0:T(8,128)S(1)}) custom-call(s32[32,128]{1,0:T(8,128)S(1)} %copy-done.3, s32[32,128]{1,0:T(8,128)S(1)} %copy-done.2, f32[12,20,20]{2,1,0:T(8,128)S(1)} %copy-done.1), custom_call_target="tpu_custom_call" | custom-call | tf_op jit(solution)/shard_map/pallas_call | solution.py:440
  15.9 0.7 %collective-permute-done.1.right = f32[40,128]{1,0:T(8,128)S(1)} collective-permute-done((f32[40,128]{1,0:T(8,128)S(1)}, f32[40,128]{1,0:T(8,128)S(1)}, u32[]{:S(2)}, u32[]{:S(2)}) %collective-permute-start.1) | collective-permute-done | bytes 20512 | tf_op jit(solution)/shard_map/ppermute | solution.py:408
  16.7 2.3 %shard_map.160 = (f32[5,32,128]{2,1,0:T(8,128)S(1)}, f32[5,32,128]{2,1,0:T(8,128)S(1)}, f32[16,128]{1,0:T(8,128)}, f32[24,128]{1,0:T(8,128)S(1)}, f32[32,128]{1,0:T(8,128)S(1)}) custom-call(f32[5,32,128]{2,1,0:T(8,128)S(1)} %copy-done, f32[5,32,128]{2,1,0:T(8,128)S(1)} %get-tuple-element.23.cond, f32[5,32,128]{2,1,0:T(8,128)S(1)} %get-tuple-element.24.diag, ...), custom_call_target="tpu_custom_call" | custom-call | tf_op jit(solution)/shard_map/pallas_call | solution.py:444
  18.9 9.9 %all-to-all-start = ((f32[16,1,128]{2,1,0:T(1,128)}), f32[16,1,128]{2,1,0:T(1,128)S(1)}, u32[]{:S(2)}, u32[]{:S(2)}) async-start(f32[16,1,128]{2,1,0:T(1,128)} %bitcast.2), calls=%async_computation | async-start | bytes 16384 | tf_op jit(solution)/shard_map/all_to_all | solution.py:413
  28.8 1.9 %collective-permute-start.2 = (f32[24,128]{1,0:T(8,128)S(1)}, f32[24,128]{1,0:T(8,128)S(1)}, u32[]{:S(2)}, u32[]{:S(2)}) collective-permute-start(f32[24,128]{1,0:T(8,128)S(1)} %get-tuple-element.32), channel_id=1, source_target_pairs={{0,16},{16,32},{32,48},{48,64},{64,80},{80,96},{96,112},{112,128},... | collective-permute-start | bytes 36872 | tf_op jit(solution)/shard_map/ppermute | solution.py:403
  30.7 6.2 %collective-permute-done.2.edge.back = f32[24,128]{1,0:T(8,128)S(1)} collective-permute-done((f32[24,128]{1,0:T(8,128)S(1)}, f32[24,128]{1,0:T(8,128)S(1)}, u32[]{:S(2)}, u32[]{:S(2)}) %collective-permute-start.2) | collective-permute-done | bytes 12320 | tf_op jit(solution)/shard_map/ppermute | solution.py:403
  36.9 0.0 all-to-all-done
  36.9 0.8 %shard_map.161 = (f32[32,128]{1,0:T(8,128)}, f32[32,128]{1,0:T(8,128)S(1)}) custom-call(f32[16,128]{1,0:T(8,128)S(1)} %bitcast.10, f32[24,128]{1,0:T(8,128)S(1)} %collective-permute-done.2.edge.back, f32[32,128]{1,0:T(8,128)S(1)} %get-tuple-element.33.strip), custom_call_target="tpu_custom_call" | custom-call | tf_op jit(solution)/shard_map/pallas_call | solution.py:451
  37.7 6.8 %all-to-all-start.1 = ((f32[32,1,128]{2,1,0:T(1,128)}), f32[32,1,128]{2,1,0:T(1,128)S(1)}, u32[]{:S(2)}, u32[]{:S(2)}) async-start(f32[32,1,128]{2,1,0:T(1,128)} %bitcast.5), calls=%async_computation.1 | async-start | bytes 32768 | tf_op jit(solution)/shard_map/all_to_all | solution.py:413
  44.4 1.1 %collective-permute-start.3 = (f32[32,128]{1,0:T(8,128)S(1)}, f32[32,128]{1,0:T(8,128)S(1)}, u32[]{:S(2)}, u32[]{:S(2)}) collective-permute-start(f32[32,128]{1,0:T(8,128)S(1)} %get-tuple-element.42), channel_id=1, source_target_pairs={{0,1},{1,2},{2,3},{3,4},{4,5},{5,6},{6,7},{7,8},{8,9},{9,10},{10,1... | collective-permute-start | bytes 49160 | tf_op jit(solution)/shard_map/ppermute | solution.py:403
  45.5 0.0 copy-start.4
  45.5 2.3 %shard_map.162.base = f32[640,128]{1,0:T(8,128)S(1)} custom-call(f32[640,128]{1,0:T(8,128)S(1)} %get-tuple-element.38.state, s32[32,128]{1,0:T(8,128)S(1)} %copy-done.3, s32[32,128]{1,0:T(8,128)S(1)} %copy-done.2, f32[12,20,20]{2,1,0:T(8,128)S(1)} %copy-done.1), custom_call_target="tpu_custom_call" | custom-call | flops 20000000 | tf_op jit(solution)/shard_map/pallas_call | solution.py:456
  47.8 0.0 collective-permute-done.3.strip
  47.9 5.1 %all-to-all-done.1 = f32[32,1,128]{2,1,0:T(1,128)S(1)} async-done(((f32[32,1,128]{2,1,0:T(1,128)}), f32[32,1,128]{2,1,0:T(1,128)S(1)}, u32[]{:S(2)}, u32[]{:S(2)}) %all-to-all-start.1) | async-done | bytes 16416 | tf_op jit(solution)/shard_map/all_to_all | solution.py:413
  53.0 0.0 copy-done.4
  53.0 1.1 %shard_map.163 = (f32[5,32,128]{2,1,0:T(8,128)}, f32[32,128]{1,0:T(8,128)}, f32[20,32,128]{2,1,0:T(8,128)}) custom-call(f32[32,128]{1,0:T(8,128)S(1)} %bitcast.9, f32[5,32,128]{2,1,0:T(8,128)S(1)} %copy-done, f32[5,32,128]{2,1,0:T(8,128)S(1)} %get-tuple-element.36.v1, f32[5,32,128]{2,1,0:T(8,128)S(1)} %get-tuple-element.37.v2, ...), custom_call_target="tpu_custom_call" | custom-call | tf_op jit(solution)/shard_map/pallas_call | solution.py:460
Async XLA Ops:
  0.6 10.9 %copy-start = (f32[5,32,128]{2,1,0:T(8,128)S(1)}, f32[5,32,128]{2,1,0:T(8,128)}, u32[]{:S(2)}) copy-start(f32[5,32,128]{2,1,0:T(8,128)} %rhs.5) | copy-start | bytes 245764
  2.1 9.4 %collective-permute-start = (f32[15,8,128]{2,1,0:T(8,128)S(1)}, f32[15,8,128]{2,1,0:T(8,128)S(1)}, u32[]{:S(2)}, u32[]{:S(2)}) collective-permute-start(f32[15,8,128]{2,1,0:T(8,128)S(1)} %get-tuple-element.25), channel_id=1, source_target_pairs={{16,0},{32,16},{48,32},{64,48},{80,64},{96,80},{112,96},{128,112},... | collective-permute-start | bytes 184328 | tf_op jit(solution)/shard_map/ppermute | solution.py:408
  11.5 3.8 %copy-start.1 = (f32[12,20,20]{2,1,0:T(8,128)S(1)}, f32[12,20,20]{2,1,0:T(8,128)}, u32[]{:S(2)}) copy-start(f32[12,20,20]{2,1,0:T(8,128)} %inverse.3) | copy-start | bytes 57604
  11.5 3.8 %copy-start.2 = (s32[32,128]{1,0:T(8,128)S(1)}, s32[32,128]{1,0:T(8,128)}, u32[]{:S(2)}) copy-start(s32[32,128]{1,0:T(8,128)} %land.5) | copy-start | bytes 49156
  11.5 3.8 %copy-start.3 = (s32[32,128]{1,0:T(8,128)S(1)}, s32[32,128]{1,0:T(8,128)}, u32[]{:S(2)}) copy-start(s32[32,128]{1,0:T(8,128)} %soil_class.2) | copy-start | bytes 49156
  11.7 5.0 %collective-permute-start.1 = (f32[40,128]{1,0:T(8,128)S(1)}, f32[40,128]{1,0:T(8,128)S(1)}, u32[]{:S(2)}, u32[]{:S(2)}) collective-permute-start(f32[40,128]{1,0:T(8,128)S(1)} %shard_map.158), channel_id=1, source_target_pairs={{1,0},{2,1},{3,2},{4,3},{5,4},{6,5},{7,6},{8,7},{9,8},{10,9},{11,1... | collective-permute-start | bytes 61448 | tf_op jit(solution)/shard_map/ppermute | solution.py:408
  18.9 18.0 %all-to-all-start = ((f32[16,1,128]{2,1,0:T(1,128)}), f32[16,1,128]{2,1,0:T(1,128)S(1)}, u32[]{:S(2)}, u32[]{:S(2)}) async-start(f32[16,1,128]{2,1,0:T(1,128)} %bitcast.2), calls=%async_computation | async-start | bytes 16384 | tf_op jit(solution)/shard_map/all_to_all | solution.py:413
  28.8 8.1 %collective-permute-start.2 = (f32[24,128]{1,0:T(8,128)S(1)}, f32[24,128]{1,0:T(8,128)S(1)}, u32[]{:S(2)}, u32[]{:S(2)}) collective-permute-start(f32[24,128]{1,0:T(8,128)S(1)} %get-tuple-element.32), channel_id=1, source_target_pairs={{0,16},{16,32},{32,48},{48,64},{64,80},{80,96},{96,112},{112,128},... | collective-permute-start | bytes 36872 | tf_op jit(solution)/shard_map/ppermute | solution.py:403
  37.7 15.3 %all-to-all-start.1 = ((f32[32,1,128]{2,1,0:T(1,128)}), f32[32,1,128]{2,1,0:T(1,128)S(1)}, u32[]{:S(2)}, u32[]{:S(2)}) async-start(f32[32,1,128]{2,1,0:T(1,128)} %bitcast.5), calls=%async_computation.1 | async-start | bytes 32768 | tf_op jit(solution)/shard_map/all_to_all | solution.py:413
  44.4 3.4 %collective-permute-start.3 = (f32[32,128]{1,0:T(8,128)S(1)}, f32[32,128]{1,0:T(8,128)S(1)}, u32[]{:S(2)}, u32[]{:S(2)}) collective-permute-start(f32[32,128]{1,0:T(8,128)S(1)} %get-tuple-element.42), channel_id=1, source_target_pairs={{0,1},{1,2},{2,3},{3,4},{4,5},{5,6},{6,7},{7,8},{8,9},{9,10},{10,1... | collective-permute-start | bytes 49160 | tf_op jit(solution)/shard_map/ppermute | solution.py:403
  45.5 7.4 %copy-start.4 = (f32[32,128]{1,0:T(8,128)S(1)}, f32[32,128]{1,0:T(8,128)}, u32[]{:S(2)}) copy-start(f32[32,128]{1,0:T(8,128)} %ponding.1) | copy-start | bytes 49156

commit v11 on v10

--- a/solution.py
+++ b/solution.py
@@ -286,13 +286,16 @@
     return renorm(*fold(parts[0], (4, 2, 1), 0))
 
 
-def relay_kernel(rows, edge, strip, row_out, west_out):
+def mend_kernel(edge, strip, west_out):
     row, lane = iota((X, Y), 0), iota((X, Y), 1)
     given = jnp.where(lax.axis_index("gx") == 0, 0, 3 * LAYERS)
     west = jnp.where((row == 0) & (lane < given), edge[16:17, :], strip[...])
     west_out[...] = jnp.where(
         (row == 1) & (lane >= LAYERS) & (lane < given), edge[17:18, :], west
     )
+
+
+def relay_kernel(rows, row_out):
     hi, lo = rows_total(rows)
     ln = iota((8, Y), 1)
     both = jnp.where(ln < 8, hi, pltpu.roll(lo, 8, 1))
@@ -448,9 +451,8 @@
     )(newton_rhs, cond, diag, after, right, east, south)
     edge = ahead(edge, "gx")
     rows = everyones(rows, "gy")
-    rows, strip = call(relay_kernel, [(lax.axis_size("gx"), Y), plane])(
-        rows, edge, strip
-    )
+    (rows,) = call(relay_kernel, [(lax.axis_size("gx"), Y)])(rows)
+    (strip,) = call(mend_kernel, [plane])(edge, strip)
     strip = ahead(strip, "gy")
     rows, kinds = lax.optimization_barrier((rows, soil_class))
     (base,) = call(

time: 54.4 us -> 57.8 us (1.062)
  blocking collectives: 0 us -> 16.7 us
  starting transfers between devices: 31.4 us -> 24.7 us
  waiting for transfers between devices: 13.3 us -> 6.91 us
  Pallas kernels: 8.71 us -> 8.12 us
    all_to_all x0 -> x1, blocking collectives: none -> 16.7 us  [everyones(): lax.all_to_all(rows.reshape(count, 1, Y), axis, 0, 0).reshape(count, Y)]
    all_to_all x2 -> x1, starting transfers between devices: 16.7 us -> 7.91 us  [everyones(): lax.all_to_all(rows.reshape(count, 1, Y), axis, 0, 0).reshape(count, Y)]
    all_to_all x2 -> x1, waiting for transfers between devices: 5.1 us -> 0.01 us  [everyones(): lax.all_to_all(rows.reshape(count, 1, Y), axis, 0, 0).reshape(count, Y)]
    ppermute x2, starting transfers between devices: 3.01 us -> 5.1 us  [ahead(): return lax.ppermute(x, axis, [(i, (i + 1) % n) for i in range(n)])]
    ppermute x2, waiting for transfers between devices: 6.16 us -> 4.91 us  [ahead(): return lax.ppermute(x, axis, [(i, (i + 1) % n) for i in range(n)])]
    pallas_call x1, Pallas kernels: 2.28 us -> 1.68 us  [on_device(): call(krylov_kernel, [block, block, (lax.axis_size('gy'), Y), (24, Y), pla...]
  transfers between devices with their start and end apart: 6 -> 5, of which waited for: 4 -> 3; matrix products, arithmetic and copies ran while one was open for 0% -> 0% of each run, Pallas kernels for 5% -> 5%
where the time goes in v11:
time: 57.8 us; the launch traced here: 57.2 us
  starting transfers between devices  24.7 us (43%)
  blocking collectives  16.7 us (29%)
  Pallas kernels  8.12 us (14%)
  waiting for transfers between devices  6.91 us (12%)
  between operations  0.73 us (1%)
    all_to_all x1, blocking collectives, everyones(): lax.all_to_all(rows.reshape(count, 1, Y), axis, 0, 0).reshape(count, Y)  16.7 us
    ppermute x2, starting transfers between devices, back(): return lax.ppermute(x, axis, [((i + 1) % n, i) for i in range(n)])  11.7 us
    all_to_all x1, starting transfers between devices, everyones(): lax.all_to_all(rows.reshape(count, 1, Y), axis, 0, 0).reshape(count, Y)  7.91 us
    ppermute x2, starting transfers between devices, ahead(): return lax.ppermute(x, axis, [(i, (i + 1) % n) for i in range(n)])  5.1 us
    ppermute x2, waiting for transfers between devices, ahead(): return lax.ppermute(x, axis, [(i, (i + 1) % n) for i in range(n)])  4.91 us
    pallas_call x1, Pallas kernels, on_device(): call(soil_kernel, [tall], [pltpu.VMEM((PAD, 240), F32)], flops=20000000)  2.29 us
    ppermute x2, waiting for transfers between devices, back(): return lax.ppermute(x, axis, [((i + 1) % n, i) for i in range(n)])  2 us
    pallas_call x1, Pallas kernels, on_device(): call(krylov_kernel, [block, block, (lax.axis_size('gy'), Y), (24, Y), pla...  1.68 us
  transfers between devices with their start and end apart: 5, of which 3 were waited for; matrix products, arithmetic and copies ran while one was open for 0% of the time, Pallas kernels for 5%

profile of v11, /device:TPU:1, one launch (start us, length us, event | category | flops | bytes accessed | tf_op | source)
XLA Modules:
  0.0 57.2 jit_solution(10596322394981431040)
XLA Ops:
  0.6 0.0 copy-start
  0.6 1.5 %shard_map.157 = (f32[5,32,128]{2,1,0:T(8,128)S(1)}, f32[5,32,128]{2,1,0:T(8,128)S(1)}, f32[15,8,128]{2,1,0:T(8,128)S(1)}, f32[32,128]{1,0:T(8,128)S(1)}, f32[32,128]{1,0:T(8,128)S(1)}, /*index=5*/f32[640,128]{1,0:T(8,128)S(1)}) custom-call(f32[5,32,128]{2,1,0:T(8,128)} %refs_0_.1, f32[5,32,128]{2,1,0:T(8,128)} %rhs.5, s32[5,32,128]{2,1,0:T(8,128)} %refs_2_.1, ...), custom_call_target="tpu_custom_call" | custom-call | tf_op jit(solution)/shard_map/pallas_call | solution.py:430
  2.1 8.1 %collective-permute-start = (f32[15,8,128]{2,1,0:T(8,128)S(1)}, f32[15,8,128]{2,1,0:T(8,128)S(1)}, u32[]{:S(2)}, u32[]{:S(2)}) collective-permute-start(f32[15,8,128]{2,1,0:T(8,128)S(1)} %get-tuple-element.23), channel_id=1, source_target_pairs={{16,0},{32,16},{48,32},{64,48},{80,64},{96,80},{112,96},{128,112},... | collective-permute-start | bytes 184328 | tf_op jit(solution)/shard_map/ppermute | solution.py:411
  10.2 1.3 %collective-permute-done.after = f32[15,8,128]{2,1,0:T(8,128)S(1)} collective-permute-done((f32[15,8,128]{2,1,0:T(8,128)S(1)}, f32[15,8,128]{2,1,0:T(8,128)S(1)}, u32[]{:S(2)}, u32[]{:S(2)}) %collective-permute-start) | collective-permute-done | bytes 61472 | tf_op jit(solution)/shard_map/ppermute | solution.py:411
  11.5 0.0 copy-done
  11.5 0.0 copy-start.1
  11.5 0.0 copy-start.2
  11.5 0.0 copy-start.3
  11.5 0.1 shard_map.158
  11.7 3.6 %collective-permute-start.1 = (f32[40,128]{1,0:T(8,128)S(1)}, f32[40,128]{1,0:T(8,128)S(1)}, u32[]{:S(2)}, u32[]{:S(2)}) collective-permute-start(f32[40,128]{1,0:T(8,128)S(1)} %shard_map.158), channel_id=1, source_target_pairs={{1,0},{2,1},{3,2},{4,3},{5,4},{6,5},{7,6},{8,7},{9,8},{10,9},{11,1... | collective-permute-start | bytes 61448 | tf_op jit(solution)/shard_map/ppermute | solution.py:411
  15.3 0.0 copy-done.1
  15.3 0.0 copy-done.2
  15.3 0.0 copy-done.3
  15.3 0.6 %shard_map.159 = (f32[640,128]{1,0:T(8,128)S(1)}, f32[640,128]{1,0:T(8,128)S(1)}) custom-call(s32[32,128]{1,0:T(8,128)S(1)} %copy-done.3, s32[32,128]{1,0:T(8,128)S(1)} %copy-done.2, f32[12,20,20]{2,1,0:T(8,128)S(1)} %copy-done.1), custom_call_target="tpu_custom_call" | custom-call | tf_op jit(solution)/shard_map/pallas_call | solution.py:443
  15.9 0.7 %collective-permute-done.1.right = f32[40,128]{1,0:T(8,128)S(1)} collective-permute-done((f32[40,128]{1,0:T(8,128)S(1)}, f32[40,128]{1,0:T(8,128)S(1)}, u32[]{:S(2)}, u32[]{:S(2)}) %collective-permute-start.1) | collective-permute-done | bytes 20512 | tf_op jit(solution)/shard_map/ppermute | solution.py:411
  16.7 1.7 %shard_map.160 = (f32[5,32,128]{2,1,0:T(8,128)S(1)}, f32[5,32,128]{2,1,0:T(8,128)S(1)}, f32[16,128]{1,0:T(8,128)S(1)}, f32[24,128]{1,0:T(8,128)S(1)}, f32[32,128]{1,0:T(8,128)S(1)}) custom-call(f32[5,32,128]{2,1,0:T(8,128)S(1)} %copy-done, f32[5,32,128]{2,1,0:T(8,128)S(1)} %get-tuple-element.21.cond, f32[5,32,128]{2,1,0:T(8,128)S(1)} %get-tuple-element.22.diag, ...), custom_call_target="tpu_custom_call" | custom-call | tf_op jit(solution)/shard_map/pallas_call | solution.py:447
  18.3 16.7 %all_to_all.10 = f32[16,1,128]{2,1,0:T(1,128)S(1)} all-to-all(f32[16,1,128]{2,1,0:T(1,128)S(1)} %bitcast.11), channel_id=1, replica_groups=mesh['gx'=32,'gy'=16] {'gy'}, dimensions={0} | all-to-all | bytes 16384 | tf_op jit(solution)/shard_map/all_to_all | solution.py:416
  35.0 0.8 %shard_map.161 = f32[32,128]{1,0:T(8,128)} custom-call(f32[16,128]{1,0:T(8,128)S(1)} %bitcast.10), custom_call_target="tpu_custom_call" | custom-call | tf_op jit(solution)/shard_map/pallas_call | solution.py:454
  35.8 7.9 %all-to-all-start.1 = ((f32[32,1,128]{2,1,0:T(1,128)}), f32[32,1,128]{2,1,0:T(1,128)S(1)}, u32[]{:S(2)}, u32[]{:S(2)}) async-start(f32[32,1,128]{2,1,0:T(1,128)} %bitcast.5), calls=%async_computation.1 | async-start | bytes 32768 | tf_op jit(solution)/shard_map/all_to_all | solution.py:416
  43.7 3.1 %collective-permute-start.2 = (f32[24,128]{1,0:T(8,128)S(1)}, f32[24,128]{1,0:T(8,128)S(1)}, u32[]{:S(2)}, u32[]{:S(2)}) collective-permute-start(f32[24,128]{1,0:T(8,128)S(1)} %get-tuple-element.33), channel_id=1, source_target_pairs={{0,16},{16,32},{32,48},{48,64},{64,80},{80,96},{96,112},{112,128},... | collective-permute-start | bytes 36872 | tf_op jit(solution)/shard_map/ppermute | solution.py:406
  46.9 4.9 %collective-permute-done.2.edge.back = f32[24,128]{1,0:T(8,128)S(1)} collective-permute-done((f32[24,128]{1,0:T(8,128)S(1)}, f32[24,128]{1,0:T(8,128)S(1)}, u32[]{:S(2)}, u32[]{:S(2)}) %collective-permute-start.2) | collective-permute-done | bytes 12320 | tf_op jit(solution)/shard_map/ppermute | solution.py:406
  51.8 2.0 %collective-permute-start.3 = (f32[32,128]{1,0:T(8,128)S(1)}, f32[32,128]{1,0:T(8,128)S(1)}, u32[]{:S(2)}, u32[]{:S(2)}) collective-permute-start(f32[32,128]{1,0:T(8,128)S(1)} %shard_map.163), channel_id=1, source_target_pairs={{0,1},{1,2},{2,3},{3,4},{4,5},{5,6},{6,7},{7,8},{8,9},{9,10},{10,1... | collective-permute-start | bytes 49160 | tf_op jit(solution)/shard_map/ppermute | solution.py:406
  53.7 0.0 copy-start.4
  53.7 2.3 %shard_map.162.base = f32[640,128]{1,0:T(8,128)S(1)} custom-call(f32[640,128]{1,0:T(8,128)S(1)} %get-tuple-element.34.state, s32[32,128]{1,0:T(8,128)S(1)} %copy-done.3, s32[32,128]{1,0:T(8,128)S(1)} %copy-done.2, f32[12,20,20]{2,1,0:T(8,128)S(1)} %copy-done.1), custom_call_target="tpu_custom_call" | custom-call | flops 20000000 | tf_op jit(solution)/shard_map/pallas_call | solution.py:458
  56.0 0.0 collective-permute-done.3.strip
  56.1 0.0 all-to-all-done.1
  56.1 0.0 copy-done.4
  56.1 1.2 %shard_map.164 = (f32[5,32,128]{2,1,0:T(8,128)}, f32[32,128]{1,0:T(8,128)}, f32[20,32,128]{2,1,0:T(8,128)}) custom-call(f32[32,128]{1,0:T(8,128)S(1)} %bitcast.9, f32[5,32,128]{2,1,0:T(8,128)S(1)} %copy-done, f32[5,32,128]{2,1,0:T(8,128)S(1)} %get-tuple-element.31.v1, f32[5,32,128]{2,1,0:T(8,128)S(1)} %get-tuple-element.32.v2, ...), custom_call_target="tpu_custom_call" | custom-call | tf_op jit(solution)/shard_map/pallas_call | solution.py:462
  (1 shorter events, 0.0 us)
Async XLA Ops:
  0.6 10.9 %copy-start = (f32[5,32,128]{2,1,0:T(8,128)S(1)}, f32[5,32,128]{2,1,0:T(8,128)}, u32[]{:S(2)}) copy-start(f32[5,32,128]{2,1,0:T(8,128)} %rhs.5) | copy-start | bytes 245764
  2.1 9.4 %collective-permute-start = (f32[15,8,128]{2,1,0:T(8,128)S(1)}, f32[15,8,128]{2,1,0:T(8,128)S(1)}, u32[]{:S(2)}, u32[]{:S(2)}) collective-permute-start(f32[15,8,128]{2,1,0:T(8,128)S(1)} %get-tuple-element.23), channel_id=1, source_target_pairs={{16,0},{32,16},{48,32},{64,48},{80,64},{96,80},{112,96},{128,112},... | collective-permute-start | bytes 184328 | tf_op jit(solution)/shard_map/ppermute | solution.py:411
  11.5 3.8 %copy-start.1 = (f32[12,20,20]{2,1,0:T(8,128)S(1)}, f32[12,20,20]{2,1,0:T(8,128)}, u32[]{:S(2)}) copy-start(f32[12,20,20]{2,1,0:T(8,128)} %inverse.3) | copy-start | bytes 57604
  11.5 3.8 %copy-start.2 = (s32[32,128]{1,0:T(8,128)S(1)}, s32[32,128]{1,0:T(8,128)}, u32[]{:S(2)}) copy-start(s32[32,128]{1,0:T(8,128)} %land.5) | copy-start | bytes 49156
  11.5 3.8 %copy-start.3 = (s32[32,128]{1,0:T(8,128)S(1)}, s32[32,128]{1,0:T(8,128)}, u32[]{:S(2)}) copy-start(s32[32,128]{1,0:T(8,128)} %soil_class.2) | copy-start | bytes 49156
  11.7 5.0 %collective-permute-start.1 = (f32[40,128]{1,0:T(8,128)S(1)}, f32[40,128]{1,0:T(8,128)S(1)}, u32[]{:S(2)}, u32[]{:S(2)}) collective-permute-start(f32[40,128]{1,0:T(8,128)S(1)} %shard_map.158), channel_id=1, source_target_pairs={{1,0},{2,1},{3,2},{4,3},{5,4},{6,5},{7,6},{8,7},{9,8},{10,9},{11,1... | collective-permute-start | bytes 61448 | tf_op jit(solution)/shard_map/ppermute | solution.py:411
  35.8 20.3 %all-to-all-start.1 = ((f32[32,1,128]{2,1,0:T(1,128)}), f32[32,1,128]{2,1,0:T(1,128)S(1)}, u32[]{:S(2)}, u32[]{:S(2)}) async-start(f32[32,1,128]{2,1,0:T(1,128)} %bitcast.5), calls=%async_computation.1 | async-start | bytes 32768 | tf_op jit(solution)/shard_map/all_to_all | solution.py:416
  43.7 8.1 %collective-permute-start.2 = (f32[24,128]{1,0:T(8,128)S(1)}, f32[24,128]{1,0:T(8,128)S(1)}, u32[]{:S(2)}, u32[]{:S(2)}) collective-permute-start(f32[24,128]{1,0:T(8,128)S(1)} %get-tuple-element.33), channel_id=1, source_target_pairs={{0,16},{16,32},{32,48},{48,64},{64,80},{80,96},{96,112},{112,128},... | collective-permute-start | bytes 36872 | tf_op jit(solution)/shard_map/ppermute | solution.py:406
  51.8 4.3 %collective-permute-start.3 = (f32[32,128]{1,0:T(8,128)S(1)}, f32[32,128]{1,0:T(8,128)S(1)}, u32[]{:S(2)}, u32[]{:S(2)}) collective-permute-start(f32[32,128]{1,0:T(8,128)S(1)} %shard_map.163), channel_id=1, source_target_pairs={{0,1},{1,2},{2,3},{3,4},{4,5},{5,6},{6,7},{7,8},{8,9},{9,10},{10,1... | collective-permute-start | bytes 49160 | tf_op jit(solution)/shard_map/ppermute | solution.py:406
  53.7 2.3 %copy-start.4 = (f32[32,128]{1,0:T(8,128)S(1)}, f32[32,128]{1,0:T(8,128)}, u32[]{:S(2)}) copy-start(f32[32,128]{1,0:T(8,128)} %ponding.1) | copy-start | bytes 49156
